TPU v7x, 256 devices: a whole 4x4x8 slice. The times are simulated.
256 devices in a mesh: ta: 2 (over z_hi), ha: 16 (over x, z_lo), wa: 8 (over y, core).
Axes of the slice: x: 4, y: 4, z: 8 (z_hi: 2, z_lo: 4; z = z_hi * 4 + z_lo), core: 2. Of those that a mesh axis runs over, the one named last changes fastest.
Arguments:
- queries: bfloat16 [4, 64, 128, 1536], P('ta', 'ha', 'wa'), may hold values from -5 to 5
- keys: bfloat16 [4, 64, 128, 1536], P('ta', 'ha', 'wa'), may hold values from -5 to 5
- values: bfloat16 [4, 64, 128, 1536], P('ta', 'ha', 'wa'), may hold values from -6 to 6
- out_grad: bfloat16 [4, 64, 128, 1536], P('ta', 'ha', 'wa'), may hold values from -6 to 6
- head_window: int32 [12, 3], replicated, may hold values from 0 to 1, as said below
Outputs:
- attended: bfloat16 [4, 64, 128, 1536], P('ta', 'ha', 'wa')
- query_grad: bfloat16 [4, 64, 128, 1536], P('ta', 'ha', 'wa')
- key_grad: bfloat16 [4, 64, 128, 1536], P('ta', 'ha', 'wa')
- value_grad: bfloat16 [4, 64, 128, 1536], P('ta', 'ha', 'wa')
Inputs may be any that keep to these rules, and one draw needn't show every extreme that they name: `head_window`: at least one head has radius 1 along all three dimensions, and at least one radius is 0.
All inputs are finite; a program needn't handle non-finite values.
Results may differ from a plain program's by a relative error of at most 0.012.
The roundings to bfloat16 on the way count: a program that leaves them out, or rounds other values in their place, can miss the bound.
Values may be sent and summed in bfloat16 or wider, within the bound.
No kernel may reach another device: no remote copies, remote signals or barrier semaphores. Data moves between devices by JAX's collectives and lax.ppermute only.
A program may use at most 128 MiB of HBM per device.

v0:
```python
from functools import partial
import math

import jax
import jax.numpy as jnp
from jax import lax
from jax.sharding import PartitionSpec as P

TILE = 2


NEG_FILL = -1e30


def padded(cells, sides, width):
    for axis, dim in sides:
        count = lax.axis_size(axis)
        ends = count - 1
        head = lax.slice_in_dim(cells, 0, width, axis=dim)
        tail = lax.slice_in_dim(cells, cells.shape[dim] - width, cells.shape[dim], axis=dim)
        cells = jnp.concatenate(
            [
                lax.ppermute(tail, axis, [(i, (i + 1) % count) for i in range(ends)]),
                cells,
                lax.ppermute(head, axis, [((i + 1) % count, i) for i in range(ends)]),
            ],
            axis=dim,
        )
    return cells


def passed_along(value, axis, by):
    devices = lax.axis_size(axis)
    pairs = [(i, i + by) for i in range(devices) if 0 <= i + by < devices]
    return lax.ppermute(value, axis, pairs)


def axis_allow(radius, pos_a, pos_b, grid_size):
    near = jnp.abs(pos_a[:, None] // TILE - pos_b[None, :] // TILE)
    inside_a = (pos_a >= 0) & (pos_a < grid_size)
    inside_b = (pos_b >= 0) & (pos_b < grid_size)
    return (
        (near[None, :, :] <= radius[:, None, None])
        & inside_a[None, :, None]
        & inside_b[None, None, :]
    )


def window_mask(window, starts_a, sizes_a, starts_b, sizes_b, limits):
    planes = []
    for dim_index in range(3):
        pos_a = starts_a[dim_index] + jnp.arange(sizes_a[dim_index], dtype=jnp.int32)
        pos_b = starts_b[dim_index] + jnp.arange(sizes_b[dim_index], dtype=jnp.int32)
        planes.append(axis_allow(window[:, dim_index], pos_a, pos_b, limits[dim_index]))
    joined = (
        planes[0][:, :, None, None, :, None, None]
        & planes[1][:, None, :, None, None, :, None]
        & planes[2][:, None, None, :, None, None, :]
    )
    count_a = sizes_a[0] * sizes_a[1] * sizes_a[2]
    count_b = sizes_b[0] * sizes_b[1] * sizes_b[2]
    return joined.reshape(window.shape[0], count_a, count_b)


def split_heads(tensor, head_count):
    rows = tensor.shape[0] * tensor.shape[1] * tensor.shape[2]
    return tensor.reshape(rows, head_count, -1).transpose(1, 0, 2)


def merge_heads(tensor, sizes):
    return tensor.transpose(1, 0, 2).reshape(sizes[0], sizes[1], sizes[2], -1)


def add_edges(core_cells, arrived, dim_index, extent):
    lower = (slice(None),) * dim_index + (slice(0, TILE),)
    upper = (slice(None),) * dim_index + (slice(extent - TILE, extent),)
    core_cells = core_cells.at[lower].add(arrived[0])
    return core_cells.at[upper].add(arrived[1])


def query_head(pieces, score_scale, with_keys):
    query, key_rows, value_rows, grad_rows, allowed = pieces
    scores = jnp.dot(query, key_rows.T, preferred_element_type=jnp.float32) * score_scale
    scores = jnp.where(allowed, scores, NEG_FILL)
    row_max = jnp.max(scores, axis=1, keepdims=True)
    log_total = row_max + jnp.log(jnp.sum(jnp.exp(scores - row_max), axis=1, keepdims=True))
    probs = jnp.exp(scores - log_total)
    weights = probs.astype(jnp.bfloat16)
    attended = jnp.dot(weights, value_rows, preferred_element_type=jnp.float32).astype(jnp.bfloat16)
    delta = jnp.sum(grad_rows.astype(jnp.float32) * attended.astype(jnp.float32), axis=1)
    dprobs = jnp.dot(grad_rows, value_rows.T, preferred_element_type=jnp.float32)
    dscores = (probs * (dprobs - delta[:, None])).astype(jnp.bfloat16)
    query_grad = (
        jnp.dot(dscores, key_rows, preferred_element_type=jnp.float32) * score_scale
    ).astype(jnp.bfloat16)
    key_part = jnp.dot(dscores.T, query, preferred_element_type=jnp.float32) * score_scale
    value_part = jnp.dot(weights.T, grad_rows, preferred_element_type=jnp.float32)
    return (attended, query_grad, log_total[:, 0], delta, key_part, value_part)


def local(queries, keys, values, out_grad, head_window):
    box_t, box_h, box_w, features = queries.shape
    head_count = head_window.shape[0]
    score_scale = 1.0 / math.sqrt(features // head_count)
    limits = (box_t * lax.axis_size("ta"), box_h * lax.axis_size("ha"), box_w * lax.axis_size("wa"))
    anchor = (
        lax.axis_index("ta") * box_t,
        lax.axis_index("ha") * box_h,
        lax.axis_index("wa") * box_w,
    )
    outer_start = tuple((start - TILE for start in anchor))
    own_sizes = (box_t, box_h, box_w)
    grown_sizes = (box_t + 2 * TILE, box_h + 2 * TILE, box_w + 2 * TILE)
    allowed = window_mask(head_window, anchor, own_sizes, outer_start, grown_sizes, limits)
    key_value = jnp.concatenate([keys, values], axis=3)
    grown_kv = padded(key_value, (("ta", 0), ("ha", 1), ("wa", 2)), TILE)
    query_rows = split_heads(queries, head_count)
    grad_rows = split_heads(out_grad, head_count)
    key_rows = split_heads(grown_kv[..., :features], head_count)
    value_rows = split_heads(grown_kv[..., features:], head_count)
    pieces = (query_rows, key_rows, value_rows, grad_rows, allowed)
    attended, query_grad, log_total, delta, key_part, value_part = lax.map(
        partial(query_head, score_scale=score_scale, with_keys=True), pieces
    )
    folded = jnp.concatenate(
        [merge_heads(key_part, grown_sizes), merge_heads(value_part, grown_sizes)], axis=3
    )
    arrived = []
    for direction in (1, -1):
        rim_cells = folded[:, :, box_w + TILE :] if direction == 1 else folded[:, :, :TILE]
        arrived.append(passed_along(rim_cells, "wa", direction))
    folded = add_edges(folded[:, :, TILE : TILE + box_w], arrived, 2, box_w)
    arrived = []
    for direction in (1, -1):
        rim_cells = folded[:, box_h + TILE :] if direction == 1 else folded[:, :TILE]
        arrived.append(passed_along(rim_cells, "ha", direction))
    folded = add_edges(folded[:, TILE : TILE + box_h], arrived, 1, box_h)
    arrived = []
    for direction in (1, -1):
        rim_cells = folded[box_t + TILE :] if direction == 1 else folded[:TILE]
        arrived.append(passed_along(rim_cells, "ta", direction))
    folded = add_edges(folded[TILE : TILE + box_t], arrived, 0, box_t)
    key_grad = folded[..., :features].astype(jnp.bfloat16)
    value_grad = folded[..., features:].astype(jnp.bfloat16)
    return (
        merge_heads(attended, own_sizes),
        merge_heads(query_grad, own_sizes),
        key_grad,
        value_grad,
    )


def solution(mesh):
    return jax.shard_map(
        local,
        mesh=mesh,
        in_specs=(
            P("ta", "ha", "wa", None),
            P("ta", "ha", "wa", None),
            P("ta", "ha", "wa", None),
            P("ta", "ha", "wa", None),
            P(),
        ),
        out_specs=(
            P("ta", "ha", "wa", None),
            P("ta", "ha", "wa", None),
            P("ta", "ha", "wa", None),
            P("ta", "ha", "wa", None),
        ),
        check_vma=False,
    )
```

profile of v0, /device:TPU:51, one launch (start us, length us, event | category | flops | bytes accessed | tf_op | source)
XLA Modules:
  0.0 554.7 jit_solution(10119055803327353934)
XLA Ops:
  4.0 8.0 %collective-permute-start = (bf16[2,4,16,3072]{3,2,1,0:T(8,128)(2,1)S(1)}, bf16[2,4,16,3072]{3,2,1,0:T(8,128)(2,1)S(1)}, u32[]{:S(2)}, u32[]{:S(2)}) collective-permute-start(bf16[2,4,16,3072]{3,2,1,0:T(8,128)(2,1)S(1)} %constant_dynamic-update-slice_fusion), channel_id=1, source_target_pairs={{0,128},{1,129},{2,130},{3,131},{4,132},{5,133},{6,134},{7,135},{8... | collective-permute-start | bytes 2359304 | tf_op jit(solution)/shard_map/ppermute | solution.py:23
  13.2 27.9 %collective-permute-done.1 = bf16[2,4,16,3072]{3,2,1,0:T(8,128)(2,1)S(1)} collective-permute-done((bf16[2,4,16,3072]{3,2,1,0:T(8,128)(2,1)S(1)}, bf16[2,4,16,3072]{3,2,1,0:T(8,128)(2,1)S(1)}, u32[]{:S(2)}, u32[]{:S(2)}) %collective-permute-start.1) | collective-permute-done | bytes 786464 | tf_op jit(solution)/shard_map/ppermute | solution.py:25
  41.5 7.2 %collective-permute-start.2 = (bf16[6,2,16,3072]{3,2,1,0:T(8,128)(2,1)S(1)}, bf16[6,2,16,3072]{3,2,1,0:T(8,128)(2,1)S(1)}, u32[]{:S(2)}, u32[]{:S(2)}) collective-permute-start(bf16[6,2,16,3072]{3,2,1,0:T(8,128)(2,1)S(1)} %get-tuple-element.225), channel_id=1, source_target_pairs={{0,8},{8,16},{16,24},{24,32},{32,40},{40,48},{48,56},{56,64},{64,7... | collective-permute-start | bytes 3538952 | tf_op jit(solution)/shard_map/ppermute | solution.py:23
  51.2 23.4 %collective-permute-done.2 = bf16[6,2,16,3072]{3,2,1,0:T(8,128)(2,1)S(1)} collective-permute-done((bf16[6,2,16,3072]{3,2,1,0:T(8,128)(2,1)S(1)}, bf16[6,2,16,3072]{3,2,1,0:T(8,128)(2,1)S(1)}, u32[]{:S(2)}, u32[]{:S(2)}) %collective-permute-start.2) | collective-permute-done | bytes 1179680 | tf_op jit(solution)/shard_map/ppermute | solution.py:23
  74.7 28.0 %collective-permute-done.3 = bf16[6,2,16,3072]{3,2,1,0:T(8,128)(2,1)S(1)} collective-permute-done((bf16[6,2,16,3072]{3,2,1,0:T(8,128)(2,1)S(1)}, bf16[6,2,16,3072]{3,2,1,0:T(8,128)(2,1)S(1)}, u32[]{:S(2)}, u32[]{:S(2)}) %collective-permute-start.3) | collective-permute-done | bytes 1179680 | tf_op jit(solution)/shard_map/ppermute | solution.py:25
  108.3 3.3 collective-permute-start.4
  111.6 6.4 %broadcast_and_fusion = pred[12,2,4,16,6,8,20]{6,5,4,3,2,1,0:T(8,128)(4,1)} fusion(pred[12,16,20]{2,1,0:T(8,128)(4,1)S(1)} %and_and_fusion, pred[12,2,4,6,8]{4,3,2,1,0:T(8,128)(4,1)S(1)} %broadcast_and_fusion.1), kind=kLoop, calls=%fused_computation.43 | loop fusion | flops 1474560 | bytes 1483008 | tf_op jit(solution)/shard_map/and | solution.py:56
  126.1 20.6 %and.296 = pred[12,128,960]{2,1,0:T(32,128)(4,1)} reshape(pred[12,2,4,16,6,8,20]{6,5,4,3,2,1,0:T(8,128)(4,1)} %broadcast_and_fusion) | data formatting | bytes 2949120 | tf_op jit(solution)/shard_map/and | solution.py:56
  146.7 4.3 copy.44
  154.4 5.3 pad_maximum_fusion
  162.2 7.0 %reshape.625 = bf16[960,12,128]{2,1,0:T(8,128)(2,1)} reshape(bf16[6,8,20,1536]{3,2,1,0:T(8,128)(2,1)} %get-tuple-element.219) | data formatting | bytes 5898240 | tf_op jit(solution)/shard_map/reshape | solution.py:67
  169.3 4.5 copy.47
  173.8 4.2 reshape.624
  177.9 2.9 copy.46
  180.9 108.6 %while.24 = (s32[]{:T(128)}, bf16[12,128,128]{1,2,0:T(8,128)(2,1)}, bf16[12,128,128]{2,1,0:T(8,128)(2,1)S(1)}, f32[12,960,128]{2,1,0:T(8,128)}, f32[12,960,128]{...) while((s32[]{:T(128)}, bf16[12,128,128]{1,2,0:T(8,128)(2,1)}, ...), condition=%wide.region_4.5_spmd, body=%wide.region_0.4_spmd.sunk | while | flops 190578432 | bytes 5591161 | solution.py:122
  289.5 9.3 %copy.52 = f32[960,12,128]{2,1,0:T(8,128)} copy(f32[960,12,128]{2,0,1:T(8,128)} %bitcast.97) | data formatting | bytes 11796480 | tf_op jit(solution)/shard_map/transpose | solution.py:71
  298.7 8.9 %reshape.630 = f32[6,8,20,1536]{3,2,1,0:T(8,128)} reshape(f32[960,12,128]{2,1,0:T(8,128)} %copy.52) | data formatting | bytes 11796480 | tf_op jit(solution)/shard_map/reshape | solution.py:71
  307.6 9.3 %copy.51 = f32[960,12,128]{2,1,0:T(8,128)} copy(f32[960,12,128]{2,0,1:T(8,128)} %bitcast.98) | data formatting | bytes 11796480 | tf_op jit(solution)/shard_map/transpose | solution.py:71
  316.8 8.8 %reshape.629 = f32[6,8,20,1536]{3,2,1,0:T(8,128)} reshape(f32[960,12,128]{2,1,0:T(8,128)} %copy.51) | data formatting | bytes 11796480 | tf_op jit(solution)/shard_map/reshape | solution.py:71
  325.7 3.9 constant_dynamic-update-slice_fusion.3
  331.5 3.0 fusion.41
  334.5 2.8 collective-permute-start.6
  339.5 6.6 %slice.256 = f32[6,8,16,3072]{3,2,1,0:T(8,128)S(1)} slice(f32[6,8,20,3072]{3,2,1,0:T(8,128)} %copy-done.1), slice={[0:6], [0:8], [2:18], [0:3072]} | slice | bytes 18874368 | tf_op jit(solution)/shard_map/slice | solution.py:132
  346.1 4.7 collective-permute-done.6
  350.8 3.9 fusion.39
  355.2 2.6 fusion.38
  360.5 3.0 collective-permute-start.9
  364.1 48.6 %collective-permute-done.8 = f32[6,2,16,3072]{3,2,1,0:T(8,128)S(1)} collective-permute-done((f32[6,2,16,3072]{3,2,1,0:T(8,128)S(1)}, f32[6,2,16,3072]{3,2,1,0:T(8,128)S(1)}, u32[]{:S(2)}, u32[]{:S(2)}) %collective-permute-start.8) | collective-permute-done | bytes 2359328 | tf_op jit(solution)/shard_map/ppermute | solution.py:35
  413.1 52.9 %collective-permute-done.9 = f32[6,2,16,3072]{3,2,1,0:T(8,128)S(1)} collective-permute-done((f32[6,2,16,3072]{3,2,1,0:T(8,128)S(1)}, f32[6,2,16,3072]{3,2,1,0:T(8,128)S(1)}, u32[]{:S(2)}, u32[]{:S(2)}) %collective-permute-start.9) | collective-permute-done | bytes 2359328 | tf_op jit(solution)/shard_map/ppermute | solution.py:35
  469.6 8.0 %collective-permute-start.10 = (f32[2,4,16,3072]{3,2,1,0:T(8,128)}, f32[2,4,16,3072]{3,2,1,0:T(8,128)S(1)}, u32[]{:S(2)}, u32[]{:S(2)}) collective-permute-start(f32[2,4,16,3072]{3,2,1,0:T(8,128)} %get-tuple-element.221), channel_id=1, source_target_pairs={{0,128},{1,129},{2,130},{3,131},{4,132},{5,133},{6,134},{7,135},{8... | collective-permute-start | bytes 4718600 | tf_op jit(solution)/shard_map/ppermute | solution.py:35
  481.7 63.8 %collective-permute-done.10 = f32[2,4,16,3072]{3,2,1,0:T(8,128)S(1)} collective-permute-done((f32[2,4,16,3072]{3,2,1,0:T(8,128)}, f32[2,4,16,3072]{3,2,1,0:T(8,128)S(1)}, u32[]{:S(2)}, u32[]{:S(2)}) %collective-permute-start.10) | collective-permute-done | bytes 1572896 | tf_op jit(solution)/shard_map/ppermute | solution.py:35
  545.5 6.0 %collective-permute-done.11 = f32[2,4,16,3072]{3,2,1,0:T(8,128)} collective-permute-done((f32[2,4,16,3072]{3,2,1,0:T(8,128)}, f32[2,4,16,3072]{3,2,1,0:T(8,128)}, u32[]{:S(2)}, u32[]{:S(2)}) %collective-permute-start.11) | collective-permute-done | bytes 1572896 | tf_op jit(solution)/shard_map/ppermute | solution.py:35
  (182 shorter events, 154.3 us)
Async XLA Ops:
  2.7 38.4 %collective-permute-start.1 = (bf16[2,4,16,3072]{3,2,1,0:T(8,128)(2,1)S(1)}, bf16[2,4,16,3072]{3,2,1,0:T(8,128)(2,1)S(1)}, u32[]{:S(2)}, u32[]{:S(2)}) collective-permute-start(bf16[2,4,16,3072]{3,2,1,0:T(8,128)(2,1)S(1)} %constant_dynamic-update-slice_fusion), channel_id=1, source_target_pairs={{128,0},{129,1},{130,2},{131,3},{132,4},{133,5},{134,6},{135,7},{1... | collective-permute-start | bytes 2359304 | tf_op jit(solution)/shard_map/ppermute | solution.py:25
  4.0 37.1 %collective-permute-start = (bf16[2,4,16,3072]{3,2,1,0:T(8,128)(2,1)S(1)}, bf16[2,4,16,3072]{3,2,1,0:T(8,128)(2,1)S(1)}, u32[]{:S(2)}, u32[]{:S(2)}) collective-permute-start(bf16[2,4,16,3072]{3,2,1,0:T(8,128)(2,1)S(1)} %constant_dynamic-update-slice_fusion), channel_id=1, source_target_pairs={{0,128},{1,129},{2,130},{3,131},{4,132},{5,133},{6,134},{7,135},{8... | collective-permute-start | bytes 2359304 | tf_op jit(solution)/shard_map/ppermute | solution.py:23
  41.5 33.1 %collective-permute-start.2 = (bf16[6,2,16,3072]{3,2,1,0:T(8,128)(2,1)S(1)}, bf16[6,2,16,3072]{3,2,1,0:T(8,128)(2,1)S(1)}, u32[]{:S(2)}, u32[]{:S(2)}) collective-permute-start(bf16[6,2,16,3072]{3,2,1,0:T(8,128)(2,1)S(1)} %get-tuple-element.225), channel_id=1, source_target_pairs={{0,8},{8,16},{16,24},{24,32},{32,40},{40,48},{48,56},{56,64},{64,7... | collective-permute-start | bytes 3538952 | tf_op jit(solution)/shard_map/ppermute | solution.py:23
  48.8 53.9 %collective-permute-start.3 = (bf16[6,2,16,3072]{3,2,1,0:T(8,128)(2,1)S(1)}, bf16[6,2,16,3072]{3,2,1,0:T(8,128)(2,1)S(1)}, u32[]{:S(2)}, u32[]{:S(2)}) collective-permute-start(bf16[6,2,16,3072]{3,2,1,0:T(8,128)(2,1)S(1)} %get-tuple-element.226), channel_id=1, source_target_pairs={{8,0},{16,8},{24,16},{32,24},{40,32},{48,40},{56,48},{64,56},{72,6... | collective-permute-start | bytes 3538952 | tf_op jit(solution)/shard_map/ppermute | solution.py:25
  102.7 1.3 copy-start.3
  105.9 45.2 %collective-permute-start.5 = (bf16[6,8,2,3072]{3,1,2,0:T(8,128)(2,1)}, bf16[6,8,2,3072]{3,1,2,0:T(8,128)(2,1)}, u32[]{:S(2)}, u32[]{:S(2)}) collective-permute-start(bf16[6,8,2,3072]{3,1,2,0:T(8,128)(2,1)} %copy.40), channel_id=1, source_target_pairs={{1,0},{2,1},{3,2},{4,3},{5,4},{6,5},{7,6},{9,8},{10,9},{11,10},{12... | collective-permute-start | bytes 1769480 | tf_op jit(solution)/shard_map/ppermute | solution.py:25
  108.3 44.5 %collective-permute-start.4 = (bf16[6,8,2,3072]{3,1,2,0:T(8,128)(2,1)}, bf16[6,8,2,3072]{3,1,2,0:T(8,128)(2,1)}, u32[]{:S(2)}, u32[]{:S(2)}) collective-permute-start(bf16[6,8,2,3072]{3,1,2,0:T(8,128)(2,1)} %copy.39), channel_id=1, source_target_pairs={{0,1},{1,2},{2,3},{3,4},{4,5},{5,6},{6,7},{8,9},{9,10},{10,11},{11... | collective-permute-start | bytes 1769480 | tf_op jit(solution)/shard_map/ppermute | solution.py:23
  146.7 7.7 %copy-start.4 = (bf16[6,2,16,3072]{3,2,1,0:T(8,128)(2,1)S(1)}, bf16[6,2,16,3072]{3,2,1,0:T(8,128)(2,1)}, u32[]{:S(2)}) copy-start(bf16[6,2,16,3072]{3,2,1,0:T(8,128)(2,1)} %copy-done.3) | copy-start | bytes 3538948
  177.9 2.9 copy-start.5
  325.7 5.0 copy-start.2
  331.5 5.8 %copy-start.1 = (f32[6,8,20,3072]{3,2,1,0:T(8,128)}, f32[6,8,20,3072]{3,2,1,0:T(8,128)S(1)}, u32[]{:S(2)}) copy-start(f32[6,8,20,3072]{3,2,1,0:T(8,128)S(1)} %constant_dynamic-update-slice_fusion.2) | copy-start | bytes 35389444
  334.5 16.3 %collective-permute-start.6 = (f32[6,8,2,3072]{3,2,1,0:T(2,128)}, f32[6,8,2,3072]{3,2,1,0:T(2,128)}, u32[]{:S(2)}, u32[]{:S(2)}) collective-permute-start(f32[6,8,2,3072]{3,2,1,0:T(2,128)} %get-tuple-element.216), channel_id=1, source_target_pairs={{0,1},{1,2},{2,3},{3,4},{4,5},{5,6},{6,7},{8,9},{9,10},{10,11},{11... | collective-permute-start | bytes 3538952 | tf_op jit(solution)/shard_map/ppermute | solution.py:35
  337.3 17.8 %collective-permute-start.7 = (f32[6,8,2,3072]{3,2,1,0:T(2,128)}, f32[6,8,2,3072]{3,2,1,0:T(2,128)}, u32[]{:S(2)}, u32[]{:S(2)}) collective-permute-start(f32[6,8,2,3072]{3,2,1,0:T(2,128)} %get-tuple-element.215), channel_id=1, source_target_pairs={{1,0},{2,1},{3,2},{4,3},{5,4},{6,5},{7,6},{9,8},{10,9},{11,10},{12... | collective-permute-start | bytes 3538952 | tf_op jit(solution)/shard_map/ppermute | solution.py:35
  358.3 54.4 %collective-permute-start.8 = (f32[6,2,16,3072]{3,2,1,0:T(8,128)S(1)}, f32[6,2,16,3072]{3,2,1,0:T(8,128)S(1)}, u32[]{:S(2)}, u32[]{:S(2)}) collective-permute-start(f32[6,2,16,3072]{3,2,1,0:T(8,128)S(1)} %get-tuple-element.218), channel_id=1, source_target_pairs={{0,8},{8,16},{16,24},{24,32},{32,40},{40,48},{48,56},{56,64},{64,7... | collective-permute-start | bytes 7077896 | tf_op jit(solution)/shard_map/ppermute | solution.py:35
  360.5 105.4 %collective-permute-start.9 = (f32[6,2,16,3072]{3,2,1,0:T(8,128)S(1)}, f32[6,2,16,3072]{3,2,1,0:T(8,128)S(1)}, u32[]{:S(2)}, u32[]{:S(2)}) collective-permute-start(f32[6,2,16,3072]{3,2,1,0:T(8,128)S(1)} %get-tuple-element.217), channel_id=1, source_target_pairs={{8,0},{16,8},{24,16},{32,24},{40,32},{48,40},{56,48},{64,56},{72,6... | collective-permute-start | bytes 7077896 | tf_op jit(solution)/shard_map/ppermute | solution.py:35
  466.6 3.1 copy-start
  466.6 12.4 %copy-start.6 = (bf16[12,128,128]{1,2,0:T(8,128)(2,1)S(1)}, bf16[12,128,128]{1,2,0:T(8,128)(2,1)}, u32[]{:S(2)}) copy-start(bf16[12,128,128]{1,2,0:T(8,128)(2,1)} %get-tuple-element.147) | copy-start | bytes 1179652
  469.6 75.9 %collective-permute-start.10 = (f32[2,4,16,3072]{3,2,1,0:T(8,128)}, f32[2,4,16,3072]{3,2,1,0:T(8,128)S(1)}, u32[]{:S(2)}, u32[]{:S(2)}) collective-permute-start(f32[2,4,16,3072]{3,2,1,0:T(8,128)} %get-tuple-element.221), channel_id=1, source_target_pairs={{0,128},{1,129},{2,130},{3,131},{4,132},{5,133},{6,134},{7,135},{8... | collective-permute-start | bytes 4718600 | tf_op jit(solution)/shard_map/ppermute | solution.py:35
  477.6 73.9 %collective-permute-start.11 = (f32[2,4,16,3072]{3,2,1,0:T(8,128)}, f32[2,4,16,3072]{3,2,1,0:T(8,128)}, u32[]{:S(2)}, u32[]{:S(2)}) collective-permute-start(f32[2,4,16,3072]{3,2,1,0:T(8,128)} %get-tuple-element.222), channel_id=1, source_target_pairs={{128,0},{129,1},{130,2},{131,3},{132,4},{133,5},{134,6},{135,7},{1... | collective-permute-start | bytes 4718600 | tf_op jit(solution)/shard_map/ppermute | solution.py:35
where the time goes:
time: 561 us; the launch traced here: 555 us
  waiting for transfers between devices  256 us (46%)
  local copies, waits for them, and re-layouts  122 us (22%)
  matrix products  97 us (17%)
  starting transfers between devices  43.8 us (8%)
  other arithmetic  34.9 us (6%)
    ppermute x6, waiting for transfers between devices, passed_along(): return lax.ppermute(value, axis, pairs)  177 us
    ppermute x3, waiting for transfers between devices, padded(): lax.ppermute(head, axis, [((i + 1) % count, i) for i in range(ends)])  55.9 us
    ppermute x3, waiting for transfers between devices, padded(): lax.ppermute(tail, axis, [(i, (i + 1) % count) for i in range(ends)])  23.4 us
    dot_general x12, matrix products, query_head(): jnp.dot(weights, value_rows, preferred_element_type=jnp.float32)  22.5 us
    dot_general x12, matrix products, query_head(): jnp.dot(weights.T, grad_rows, preferred_element_type=jnp.float32)  21.5 us
    dot_general x12, matrix products, query_head(): jnp.dot(dscores.T, query, preferred_element_type=jnp.float32) * score_scale  21 us
    and x1, local copies, waits for them, and re-layouts, window_mask(): planes[0][:, :, None, None, :, None, None]  20.6 us
    reshape x4, local copies, waits for them, and re-layouts, merge_heads(): return tensor.transpose(1, 0, 2).reshape(sizes[0], sizes[1], sizes[2], -1)  19.7 us
  transfers between devices with their start and end apart: 12, of which 9 were waited for; matrix products, arithmetic and copies ran while one was open for 10% of the time, Pallas kernels for 0%

commit v1 on v0

v1 whole, which is shorter than its diff:
```python
from functools import partial
import math

import jax
import jax.numpy as jnp
from jax import lax
from jax.experimental import pallas as pl
from jax.experimental.pallas import tpu as pltpu
from jax.sharding import PartitionSpec as P

NEG = -1e30
BF = jnp.bfloat16
F32 = jnp.float32

GROUPS = 4
LANES = 384
HEAD = 128
GH = LANES // HEAD
TAH = ("ta", "ha")


def place():
    ta, ha = lax.axis_index("ta"), lax.axis_index("ha")
    x, z_lo = ha // 4, ha % 4
    z = ta * 4 + z_lo
    src = ta * 2 + z_lo % 2
    group = z // 2
    half = (z + x) % 2
    return src, group, half, x


def lin(x, z):
    return (z // 4) * 16 + x * 4 + z % 4


def deal_pairs(turn, back):
    pairs = []
    for x in range(4):
        for z in range(8):
            src = (z // 4) * 2 + z % 2
            dest = 2 * (src ^ turn) + ((z % 4) // 2 + x) % 2
            pair = (lin(x, z), lin(x, dest))
            pairs.append(pair[::-1] if back else pair)
    return pairs


def deal(bufs, back):
    return [lax.ppermute(b, TAH, deal_pairs(r, back)) for r, b in enumerate(bufs)]


PARTNER = [(lin(x, z), lin(x, z ^ 1)) for x in range(4) for z in range(8)]


def across_pairs():
    pairs = []
    for x in range(4):
        for z in range(8):
            other = x + 1 if (z + x) % 2 else x - 1
            if 0 <= other < 4:
                pairs.append((lin(x, z), lin(other, z)))
    return pairs


def rows_swap(partner_buf, across_buf):
    return (
        lax.ppermute(partner_buf, TAH, PARTNER),
        lax.ppermute(across_buf, TAH, across_pairs()),
    )


def cols_swap(first, last):
    n = lax.axis_size("wa")
    from_next = lax.ppermute(first, "wa", [(i + 1, i) for i in range(n - 1)])
    from_prev = lax.ppermute(last, "wa", [(i, i + 1) for i in range(n - 1)])
    return from_prev, from_next


def call(body, outs, scratch=(), grid=None, in_specs=None, out_specs=None, flops=0, size=3 << 20, name=None):
    kw = {}
    if grid is not None:
        kw = dict(grid=grid, in_specs=in_specs, out_specs=out_specs)
    return pl.pallas_call(
        body,
        out_shape=outs,
        scratch_shapes=list(scratch),
        compiler_params=pltpu.CompilerParams(vmem_limit_bytes=48 << 20),
        cost_estimate=pl.CostEstimate(flops=flops, bytes_accessed=size, transcendentals=0),
        name=name,
        **kw,
    )


def shaped(*dims, dtype=BF):
    return jax.ShapeDtypeStruct(dims, dtype)


DEALT = (2, 4, 2, 16, LANES)


def pack_body(a_ref, b_ref, *outs):
    src, _, _, _ = place()
    for r, out in enumerate(outs):
        lanes = pl.ds(pl.multiple_of((src ^ r) * LANES, LANES), LANES)
        for i, ref in enumerate((a_ref, b_ref)):
            for t in range(2):
                for h in range(4):
                    out[i, h, t] = ref[t, h, :, lanes]


def pack(a, b, name):
    return call(pack_body, [shaped(*DEALT)] * GROUPS, name=name)(a, b)


def unpack_body(*refs):
    bufs, outs = refs[:GROUPS], refs[GROUPS:]
    src, _, _, _ = place()
    for r, buf in enumerate(bufs):
        lanes = pl.ds(pl.multiple_of((src ^ r) * LANES, LANES), LANES)
        for i, ref in enumerate(outs):
            for t in range(2):
                for h in range(4):
                    ref[t, h, :, lanes] = buf[i, h, t]


def unpack(bufs, name):
    return call(unpack_body, [shaped(2, 4, 16, GROUPS * LANES)] * 2, name=name)(*bufs)


def spot(src, h):
    return pl.multiple_of((src % 2) * 256 + h * 64 + (src // 2) * 32, 32)


def gather_blocks(bufs, i, store):
    _, group, _, _ = place()
    for r, buf in enumerate(bufs):
        src = group ^ r
        for h in range(4):
            store(pl.ds(spot(src, h), 32), buf[i, h].reshape(32, buf.shape[-1]))


def edge_pick(transpose):
    shape = (512, 128) if transpose else (128, 512)
    e = lax.broadcasted_iota(jnp.int32, shape, 1 if transpose else 0)
    token = lax.broadcasted_iota(jnp.int32, shape, 0 if transpose else 1)
    want = (e % 64) // 2 * 16 + e % 2 + 14 * (e // 64)
    return jnp.where(token == want, 1.0, 0.0).astype(BF)


def own_body(*refs):
    bufs, (own, first, last) = refs[:GROUPS], refs[GROUPS:]
    pick = edge_pick(False)
    for i in range(2):
        def store(at, value, i=i):
            own[i, at, :] = value
        gather_blocks(bufs, i, store)
        edges = jnp.dot(pick, own[i], preferred_element_type=F32).astype(BF)
        first[i] = edges[:64]
        last[i] = edges[64:]


def own_kv(bufs):
    outs = [shaped(2, 512, LANES), shaped(2, 64, LANES), shaped(2, 64, LANES)]
    return call(own_body, outs, name="own_kv")(*bufs)


def rows_body(own, left, right, to_partner, to_across):
    _, _, half, _ = place()
    for out, low in ((to_partner, half), (to_across, 1 - half)):
        at = pl.multiple_of((1 - low) * 384, 128)
        side = pl.multiple_of((1 - low) * 48, 16)
        out[:, 0:128] = own[:, pl.ds(at, 128)]
        out[:, 128:144] = left[:, pl.ds(side, 16)]
        out[:, 144:160] = right[:, pl.ds(side, 16)]


def rows_out(own, left, right):
    return call(rows_body, [shaped(2, 160, LANES)] * 2, name="rows_out")(own, left, right)


def attend_body(window, own, left, right, partner, across, *refs):
    qd = refs[:GROUPS]
    back = refs[GROUPS : 2 * GROUPS]
    own_grad, side_grad, to_partner, to_across = refs[2 * GROUPS : 2 * GROUPS + 4]
    kv_mid, kv_left, kv_right, g_mid, g_left, g_right, q_all, o_all = refs[2 * GROUPS + 4 :]
    _, group, half, x = place()
    w_at = lax.axis_index("wa")
    w_last = lax.axis_size("wa") - 1
    scale = 1.0 / math.sqrt(HEAD)
    head = group * GH + pl.program_id(0)
    rad_t, rad_h, rad_w = window[head, 0], window[head, 1], window[head, 2]

    spots = []
    for buf, low in ((partner, half), (across, 1 - half)):
        at = pl.multiple_of((1 - low) * 640, 128)
        side = pl.multiple_of((1 - low) * 80, 16)
        spots.append((buf, at, side))
    for i in range(2):
        kv_mid[i, 128:640] = own[i]
        kv_left[i, 16:80] = left[i]
        kv_right[i, 16:80] = right[i]
        for buf, at, side in spots:
            kv_mid[i, pl.ds(at, 128)] = buf[i, 0:128]
            kv_left[i, pl.ds(side, 16)] = buf[i, 128:144]
            kv_right[i, pl.ds(side, 16)] = buf[i, 144:160]

        def store(at, value, i=i):
            q_all[i, at, :] = value
        gather_blocks(qd, i, store)
    g_mid[...] = jnp.zeros_like(g_mid)
    g_left[...] = jnp.zeros_like(g_left)
    g_right[...] = jnp.zeros_like(g_right)

    qi = lax.broadcasted_iota(jnp.int32, (128, 1), 0)
    q_t, q_w = qi // 32 % 2, qi % 16 // 2
    ki = lax.broadcasted_iota(jnp.int32, (1, 480), 1)
    mid = ki < 384
    ks = jnp.where(ki < 432, ki - 384, ki - 432)
    k_t = jnp.where(mid, ki // 32 % 2, ks // 4 % 2)
    k_w = jnp.where(mid, ki % 16 // 2, jnp.where(ki < 432, -1, 8))
    k_h = jnp.where(mid, ki // 128, ks // 16)
    near = (jnp.abs(q_t - k_t) <= rad_t) & (jnp.abs(q_w - k_w) <= rad_w)
    base = jnp.where(near, 0.0, NEG)
    inside = ((k_w >= 0) | (w_at > 0)) & ((k_w < 8) | (w_at < w_last))
    inside = inside & (jnp.abs(k_h - 1) <= rad_h)
    tile_row = (x * 2 + half) * 4 - 1
    tile_rows = 4 * 8

    for blk in range(4):
        row = tile_row + blk + k_h
        row_bias = jnp.where(inside & (row >= 0) & (row < tile_rows), 0.0, NEG)
        mid_at, side_at, q_at = pl.ds(128 * blk, 384), pl.ds(16 * blk, 48), pl.ds(128 * blk, 128)
        k, v = (
            jnp.concatenate([kv_mid[i, mid_at], kv_left[i, side_at], kv_right[i, side_at]], axis=0)
            for i in range(2)
        )
        q, do = q_all[0, q_at], q_all[1, q_at]
        nt = (((1,), (1,)), ((), ()))
        tn = (((0,), (0,)), ((), ()))
        s = lax.dot_general(q, k, nt, preferred_element_type=F32) * scale + (base + row_bias)
        top = jnp.max(s, axis=1, keepdims=True)
        e = jnp.exp(s - top)
        p = e * (1.0 / jnp.sum(e, axis=1, keepdims=True))
        wts = p.astype(BF)
        o = jnp.dot(wts, v, preferred_element_type=F32).astype(BF)
        delta = jnp.sum(do.astype(F32) * o.astype(F32), axis=1, keepdims=True)
        dp = lax.dot_general(do, v, nt, preferred_element_type=F32)
        ds = (p * (dp - delta)).astype(BF)
        dq = jnp.dot(ds, k, preferred_element_type=F32) * scale
        o_all[0, q_at] = o
        o_all[1, q_at] = dq.astype(BF)
        dk = lax.dot_general(ds, q, tn, preferred_element_type=F32) * scale
        dv = lax.dot_general(wts, do, tn, preferred_element_type=F32)
        for i, d in enumerate((dk, dv)):
            g_mid[i, mid_at] += d[0:384]
            g_left[i, side_at] += d[384:432]
            g_right[i, side_at] += d[432:480]

    for r, out in enumerate(back):
        src = group ^ r
        for i in range(2):
            for h in range(4):
                out[i, h] = o_all[i, pl.ds(spot(src, h), 32), :].reshape(2, 16, HEAD)
    for i in range(2):
        own_grad[i] = g_mid[i, 128:640]
        side_grad[i, 0:64] = g_left[i, 16:80]
        side_grad[i, 64:128] = g_right[i, 16:80]
        for out, (_, at, side) in zip((to_partner, to_across), spots):
            out[i, 0:128] = g_mid[i, pl.ds(at, 128)].astype(BF)
            out[i, 128:144] = g_left[i, pl.ds(side, 16)].astype(BF)
            out[i, 144:160] = g_right[i, pl.ds(side, 16)].astype(BF)


def by_head(*dims):
    lead = len(dims) - 1
    return pl.BlockSpec(dims[:-1] + (HEAD,), lambda n: (0,) * lead + (n,))


def attend(window, own, left, right, partner, across, qd):
    outs = [shaped(*DEALT)] * GROUPS + [
        shaped(2, 512, LANES, dtype=F32),
        shaped(2, 128, LANES, dtype=F32),
        shaped(2, 160, LANES),
        shaped(2, 160, LANES),
    ]
    ins = [own, left, right, partner, across] + list(qd)
    scratch = [
        pltpu.VMEM((2, 768, HEAD), BF),
        pltpu.VMEM((2, 96, HEAD), BF),
        pltpu.VMEM((2, 96, HEAD), BF),
        pltpu.VMEM((2, 768, HEAD), F32),
        pltpu.VMEM((2, 96, HEAD), F32),
        pltpu.VMEM((2, 96, HEAD), F32),
        pltpu.VMEM((2, 512, HEAD), BF),
        pltpu.VMEM((2, 512, HEAD), BF),
    ]
    return call(
        attend_body,
        outs,
        scratch,
        grid=(GH,),
        in_specs=[pl.BlockSpec(memory_space=pltpu.SMEM)] + [by_head(*a.shape) for a in ins],
        out_specs=[by_head(*a.shape) for a in outs],
        flops=1200000000,
        size=8 << 20,
        name="attend",
    )(window, *ins)


def side_body(side_grad, partner, across, to_prev, to_next):
    _, _, half, _ = place()
    for i in range(2):
        for out, lo, first in ((to_prev, 0, 128), (to_next, 64, 144)):
            out[i] = side_grad[i, lo : lo + 64].astype(BF)
            for buf, low in ((partner, half), (across, 1 - half)):
                at = pl.multiple_of((1 - low) * 48, 16)
                total = side_grad[i, pl.ds(lo + at, 16)] + buf[i, first : first + 16].astype(F32)
                out[i, pl.ds(at, 16)] = total.astype(BF)


def side_out(side_grad, partner, across):
    return call(side_body, [shaped(2, 64, LANES)] * 2, name="side_out")(side_grad, partner, across)


def final_body(own_grad, partner, across, from_prev, from_next, *refs):
    outs, total = refs[:GROUPS], refs[GROUPS]
    _, group, half, _ = place()
    spread = edge_pick(True)
    for i in range(2):
        edges = jnp.concatenate([from_prev[i], from_next[i]], axis=0)
        total[...] = own_grad[i] + jnp.dot(spread, edges, preferred_element_type=F32)
        for buf, low in ((partner, half), (across, 1 - half)):
            at = pl.ds(pl.multiple_of((1 - low) * 384, 128), 128)
            total[at, :] += buf[i, 0:128].astype(F32)
        for r, out in enumerate(outs):
            src = group ^ r
            for h in range(4):
                out[i, h] = total[pl.ds(spot(src, h), 32), :].astype(BF).reshape(2, 16, LANES)


def final(own_grad, partner, across, from_prev, from_next):
    return call(
        final_body, [shaped(*DEALT)] * GROUPS, [pltpu.VMEM((512, LANES), F32)], name="final"
    )(own_grad, partner, across, from_prev, from_next)


def local(queries, keys, values, out_grad, head_window):
    kv = deal(pack(keys, values, "pack_kv"), False)
    qd = deal(pack(queries, out_grad, "pack_qd"), False)
    own, first, last = own_kv(kv)
    left, right = cols_swap(first, last)
    partner, across = rows_swap(*rows_out(own, left, right))
    results = attend(head_window, own, left, right, partner, across, qd)
    oq = deal(results[:GROUPS], True)
    own_grad, side_grad, to_partner, to_across = results[GROUPS:]
    partner, across = rows_swap(to_partner, to_across)
    to_prev, to_next = side_out(side_grad, partner, across)
    from_prev, from_next = cols_swap(to_prev, to_next)
    dkv = deal(final(own_grad, partner, across, from_prev, from_next), True)
    attended, query_grad = unpack(oq, "unpack_oq")
    key_grad, value_grad = unpack(dkv, "unpack_dkv")
    return attended, query_grad, key_grad, value_grad


def solution(mesh):
    spec = P("ta", "ha", "wa", None)
    return jax.shard_map(
        local,
        mesh=mesh,
        in_specs=(spec,) * 4 + (P(),),
        out_specs=(spec,) * 4,
        check_vma=False,
    )
```

time: 561 us -> 137 us (0.24)
  the two profiles are of different devices: /device:TPU:51 before, /device:TPU:8 now
where the time goes in v1:
time: 137 us; the launch traced here: 136 us
  starting transfers between devices  65.1 us (48%)
  waiting for transfers between devices  52.2 us (38%)
  Pallas kernels  13.7 us (10%)
  local copies, waits for them, and re-layouts  4.07 us (3%)
    ppermute x16, waiting for transfers between devices, deal(): lax.ppermute(b, TAH, deal_pairs(r, back))  49.7 us
    ppermute x16, starting transfers between devices, deal(): lax.ppermute(b, TAH, deal_pairs(r, back))  44 us
    pallas_call x1, Pallas kernels, attend(): call(attend_body, outs, scratch, grid=(GH,), in_specs=[pl.BlockSpec(memor...  10.5 us
    ppermute x2, starting transfers between devices, rows_swap(): lax.ppermute(partner_buf, TAH, PARTNER)  8.73 us
    ppermute x2, starting transfers between devices, cols_swap(): from_next = lax.ppermute(first, 'wa', [(i + 1, i) for i in range(n - 1)])  7.28 us
    unnamed x11, local copies, waits for them, and re-layouts  4.07 us
    ppermute x2, starting transfers between devices, cols_swap(): from_prev = lax.ppermute(last, 'wa', [(i, i + 1) for i in range(n - 1)])  3.84 us
  transfers between devices with their start and end apart: 24, of which 11 were waited for; matrix products, arithmetic and copies ran while one was open for 0% of the time, Pallas kernels for 2%

profile of v1, /device:TPU:8, one launch (start us, length us, event | category | flops | bytes accessed | tf_op | source)
XLA Modules:
  0.0 136.0 jit_solution(10080767379389949597)
XLA Ops:
  0.6 1.0 copy-done
  1.6 1.0 copy-done.1
  3.4 6.5 %collective-permute-start.1 = (bf16[2,4,2,16,384]{4,3,2,1,0:T(8,128)(2,1)S(1)}, bf16[2,4,2,16,384]{4,3,2,1,0:T(8,128)(2,1)S(1)}, u32[]{:S(2)}, u32[]{:S(2)}) collective-permute-start(bf16[2,4,2,16,384]{4,3,2,1,0:T(8,128)(2,1)S(1)} %get-tuple-element.36), channel_id=1, source_target_pairs={{0,16},{8,0},{16,24},{24,8},{128,144},{136,128},{144,152},{152,136... | collective-permute-start | bytes 589832 | tf_op jit(solution)/shard_map/ppermute | solution.py:48
  9.9 6.4 %collective-permute-start.2 = (bf16[2,4,2,16,384]{4,3,2,1,0:T(8,128)(2,1)S(1)}, bf16[2,4,2,16,384]{4,3,2,1,0:T(8,128)(2,1)S(1)}, u32[]{:S(2)}, u32[]{:S(2)}) collective-permute-start(bf16[2,4,2,16,384]{4,3,2,1,0:T(8,128)(2,1)S(1)} %get-tuple-element.37), channel_id=1, source_target_pairs={{0,128},{8,144},{16,136},{24,152},{128,0},{136,16},{144,8},{152,24... | collective-permute-start | bytes 589832 | tf_op jit(solution)/shard_map/ppermute | solution.py:48
  16.3 1.0 copy-done.2
  17.3 1.0 copy-done.3
  19.0 8.2 %collective-permute-done.2.refs_2_ = bf16[2,4,2,16,384]{4,3,2,1,0:T(8,128)(2,1)S(1)} collective-permute-done((bf16[2,4,2,16,384]{4,3,2,1,0:T(8,128)(2,1)S(1)}, bf16[2,4,2,16,384]{4,3,2,1,0:T(8,128)(2,1)S(1)}, u32[]{:S(2)}, u32[]{:S(2)}) %collective-permute-start.2) | collective-permute-done | bytes 196640 | tf_op jit(solution)/shard_map/ppermute | solution.py:48
  27.3 4.1 %collective-permute-done.3.refs_3_ = bf16[2,4,2,16,384]{4,3,2,1,0:T(8,128)(2,1)S(1)} collective-permute-done((bf16[2,4,2,16,384]{4,3,2,1,0:T(8,128)(2,1)S(1)}, bf16[2,4,2,16,384]{4,3,2,1,0:T(8,128)(2,1)S(1)}, u32[]{:S(2)}, u32[]{:S(2)}) %collective-permute-start.3) | collective-permute-done | bytes 196640 | tf_op jit(solution)/shard_map/ppermute | solution.py:48
  31.8 1.9 %collective-permute-start.4 = (bf16[2,64,384]{2,1,0:T(8,128)(2,1)S(1)}, bf16[2,64,384]{2,1,0:T(8,128)(2,1)S(1)}, u32[]{:S(2)}, u32[]{:S(2)}) collective-permute-start(bf16[2,64,384]{2,1,0:T(8,128)(2,1)S(1)} %get-tuple-element.40), channel_id=1, source_target_pairs={{0,1},{1,2},{2,3},{3,4},{4,5},{5,6},{6,7},{8,9},{9,10},{10,11},{11... | collective-permute-start | bytes 294920 | tf_op jit(solution)/shard_map/ppermute | solution.py:74
  33.7 3.6 %collective-permute-start.5 = (bf16[2,64,384]{2,1,0:T(8,128)(2,1)S(1)}, bf16[2,64,384]{2,1,0:T(8,128)(2,1)S(1)}, u32[]{:S(2)}, u32[]{:S(2)}) collective-permute-start(bf16[2,64,384]{2,1,0:T(8,128)(2,1)S(1)} %get-tuple-element.41), channel_id=1, source_target_pairs={{1,0},{2,1},{3,2},{4,3},{5,4},{6,5},{7,6},{9,8},{10,9},{11,10},{12... | collective-permute-start | bytes 294920 | tf_op jit(solution)/shard_map/ppermute | solution.py:73
  37.7 1.8 %collective-permute-done.5.right = bf16[2,64,384]{2,1,0:T(8,128)(2,1)S(1)} collective-permute-done((bf16[2,64,384]{2,1,0:T(8,128)(2,1)S(1)}, bf16[2,64,384]{2,1,0:T(8,128)(2,1)S(1)}, u32[]{:S(2)}, u32[]{:S(2)}) %collective-permute-start.5) | collective-permute-done | bytes 98336 | tf_op jit(solution)/shard_map/ppermute | solution.py:73
  39.6 4.7 %collective-permute-start.6 = (bf16[2,160,384]{2,1,0:T(8,128)(2,1)S(1)}, bf16[2,160,384]{2,1,0:T(8,128)(2,1)S(1)}, u32[]{:S(2)}, u32[]{:S(2)}) collective-permute-start(bf16[2,160,384]{2,1,0:T(8,128)(2,1)S(1)} %get-tuple-element.42), channel_id=1, source_target_pairs={{0,8},{8,0},{16,24},{24,16},{128,136},{136,128},{144,152},{152,144... | collective-permute-start | bytes 737288 | tf_op jit(solution)/shard_map/ppermute | solution.py:66
  44.9 2.3 %collective-permute-start.9 = (bf16[2,4,2,16,384]{4,3,2,1,0:T(8,128)(2,1)S(1)}, bf16[2,4,2,16,384]{4,3,2,1,0:T(8,128)(2,1)S(1)}, u32[]{:S(2)}, u32[]{:S(2)}) collective-permute-start(bf16[2,4,2,16,384]{4,3,2,1,0:T(8,128)(2,1)S(1)} %get-tuple-element.45), channel_id=1, source_target_pairs={{0,16},{8,0},{16,24},{24,8},{128,144},{136,128},{144,152},{152,136... | collective-permute-start | bytes 589832 | tf_op jit(solution)/shard_map/ppermute | solution.py:48
  47.3 2.0 %collective-permute-start.10 = (bf16[2,4,2,16,384]{4,3,2,1,0:T(8,128)(2,1)S(1)}, bf16[2,4,2,16,384]{4,3,2,1,0:T(8,128)(2,1)S(1)}, u32[]{:S(2)}, u32[]{:S(2)}) collective-permute-start(bf16[2,4,2,16,384]{4,3,2,1,0:T(8,128)(2,1)S(1)} %get-tuple-element.46), channel_id=1, source_target_pairs={{0,128},{8,144},{16,136},{24,152},{128,0},{136,16},{144,8},{152,24... | collective-permute-start | bytes 589832 | tf_op jit(solution)/shard_map/ppermute | solution.py:48
  49.3 4.2 %collective-permute-start.11 = (bf16[2,4,2,16,384]{4,3,2,1,0:T(8,128)(2,1)S(1)}, bf16[2,4,2,16,384]{4,3,2,1,0:T(8,128)(2,1)S(1)}, u32[]{:S(2)}, u32[]{:S(2)}) collective-permute-start(bf16[2,4,2,16,384]{4,3,2,1,0:T(8,128)(2,1)S(1)} %get-tuple-element.47), channel_id=1, source_target_pairs={{0,144},{8,128},{16,152},{24,136},{128,16},{136,0},{144,24},{152,8... | collective-permute-start | bytes 589832 | tf_op jit(solution)/shard_map/ppermute | solution.py:48
  53.6 1.2 collective-permute-done.9.refs_1_
  54.8 5.9 %collective-permute-done.10.refs_2_ = bf16[2,4,2,16,384]{4,3,2,1,0:T(8,128)(2,1)S(1)} collective-permute-done((bf16[2,4,2,16,384]{4,3,2,1,0:T(8,128)(2,1)S(1)}, bf16[2,4,2,16,384]{4,3,2,1,0:T(8,128)(2,1)S(1)}, u32[]{:S(2)}, u32[]{:S(2)}) %collective-permute-start.10) | collective-permute-done | bytes 196640 | tf_op jit(solution)/shard_map/ppermute | solution.py:48
  60.7 10.2 %collective-permute-done.11.refs_3_ = bf16[2,4,2,16,384]{4,3,2,1,0:T(8,128)(2,1)S(1)} collective-permute-done((bf16[2,4,2,16,384]{4,3,2,1,0:T(8,128)(2,1)S(1)}, bf16[2,4,2,16,384]{4,3,2,1,0:T(8,128)(2,1)S(1)}, u32[]{:S(2)}, u32[]{:S(2)}) %collective-permute-start.11) | collective-permute-done | bytes 196640 | tf_op jit(solution)/shard_map/ppermute | solution.py:48
  70.9 10.5 %attend.1 = (bf16[2,4,2,16,384]{4,3,2,1,0:T(8,128)(2,1)S(1)}, bf16[2,4,2,16,384]{4,3,2,1,0:T(8,128)(2,1)S(1)}, bf16[2,4,2,16,384]{4,3,2,1,0:T(8,128)(2,1)S(1)}, ...) custom-call(s32[12,3]{1,0:T(8,128)S(1)} %copy.9.window, ...), custom_call_target="tpu_custom_call" | custom-call | flops 1200000000 | bytes 8388608 | tf_op jit(solution)/shard_map/attend/pallas_call | solution.py:296
  81.4 4.1 %collective-permute-start.16 = (bf16[2,160,384]{2,1,0:T(8,128)(2,1)S(1)}, bf16[2,160,384]{2,1,0:T(8,128)(2,1)S(1)}, u32[]{:S(2)}, u32[]{:S(2)}) collective-permute-start(bf16[2,160,384]{2,1,0:T(8,128)(2,1)S(1)} %get-tuple-element.55), channel_id=1, source_target_pairs={{0,8},{8,0},{16,24},{24,16},{128,136},{136,128},{144,152},{152,144... | collective-permute-start | bytes 737288 | tf_op jit(solution)/shard_map/ppermute | solution.py:66
  86.9 4.4 %collective-permute-start.13 = (bf16[2,4,2,16,384]{4,3,2,1,0:T(8,128)(2,1)S(1)}, bf16[2,4,2,16,384]{4,3,2,1,0:T(8,128)(2,1)S(1)}, u32[]{:S(2)}, u32[]{:S(2)}) collective-permute-start(bf16[2,4,2,16,384]{4,3,2,1,0:T(8,128)(2,1)S(1)} %get-tuple-element.49), channel_id=1, source_target_pairs={{16,0},{0,8},{24,16},{8,24},{144,128},{128,136},{152,144},{136,152... | collective-permute-start | bytes 589832 | tf_op jit(solution)/shard_map/ppermute | solution.py:48
  91.3 4.3 %collective-permute-start.14 = (bf16[2,4,2,16,384]{4,3,2,1,0:T(8,128)(2,1)S(1)}, bf16[2,4,2,16,384]{4,3,2,1,0:T(8,128)(2,1)S(1)}, u32[]{:S(2)}, u32[]{:S(2)}) collective-permute-start(bf16[2,4,2,16,384]{4,3,2,1,0:T(8,128)(2,1)S(1)} %get-tuple-element.50), channel_id=1, source_target_pairs={{128,0},{144,8},{136,16},{152,24},{0,128},{16,136},{8,144},{24,152... | collective-permute-start | bytes 589832 | tf_op jit(solution)/shard_map/ppermute | solution.py:48
  95.6 1.9 %collective-permute-start.18 = (bf16[2,64,384]{2,1,0:T(8,128)(2,1)S(1)}, bf16[2,64,384]{2,1,0:T(8,128)(2,1)S(1)}, u32[]{:S(2)}, u32[]{:S(2)}) collective-permute-start(bf16[2,64,384]{2,1,0:T(8,128)(2,1)S(1)} %get-tuple-element.58), channel_id=1, source_target_pairs={{0,1},{1,2},{2,3},{3,4},{4,5},{5,6},{6,7},{8,9},{9,10},{10,11},{11... | collective-permute-start | bytes 294920 | tf_op jit(solution)/shard_map/ppermute | solution.py:74
  97.6 3.6 %collective-permute-start.19 = (bf16[2,64,384]{2,1,0:T(8,128)(2,1)S(1)}, bf16[2,64,384]{2,1,0:T(8,128)(2,1)S(1)}, u32[]{:S(2)}, u32[]{:S(2)}) collective-permute-start(bf16[2,64,384]{2,1,0:T(8,128)(2,1)S(1)} %get-tuple-element.59), channel_id=1, source_target_pairs={{1,0},{2,1},{3,2},{4,3},{5,4},{6,5},{7,6},{9,8},{10,9},{11,10},{12... | collective-permute-start | bytes 294920 | tf_op jit(solution)/shard_map/ppermute | solution.py:73
  101.6 2.4 %collective-permute-start.15 = (bf16[2,4,2,16,384]{4,3,2,1,0:T(8,128)(2,1)S(1)}, bf16[2,4,2,16,384]{4,3,2,1,0:T(8,128)(2,1)S(1)}, u32[]{:S(2)}, u32[]{:S(2)}) collective-permute-start(bf16[2,4,2,16,384]{4,3,2,1,0:T(8,128)(2,1)S(1)} %get-tuple-element.51), channel_id=1, source_target_pairs={{144,0},{128,8},{152,16},{136,24},{16,128},{0,136},{24,144},{8,152... | collective-permute-start | bytes 589832 | tf_op jit(solution)/shard_map/ppermute | solution.py:48
  105.3 3.6 %collective-permute-start.21 = (bf16[2,4,2,16,384]{4,3,2,1,0:T(8,128)(2,1)S(1)}, bf16[2,4,2,16,384]{4,3,2,1,0:T(8,128)(2,1)S(1)}, u32[]{:S(2)}, u32[]{:S(2)}) collective-permute-start(bf16[2,4,2,16,384]{4,3,2,1,0:T(8,128)(2,1)S(1)} %get-tuple-element.61), channel_id=1, source_target_pairs={{16,0},{0,8},{24,16},{8,24},{144,128},{128,136},{152,144},{136,152... | collective-permute-start | bytes 589832 | tf_op jit(solution)/shard_map/ppermute | solution.py:48
  108.9 4.3 %collective-permute-start.22 = (bf16[2,4,2,16,384]{4,3,2,1,0:T(8,128)(2,1)S(1)}, bf16[2,4,2,16,384]{4,3,2,1,0:T(8,128)(2,1)S(1)}, u32[]{:S(2)}, u32[]{:S(2)}) collective-permute-start(bf16[2,4,2,16,384]{4,3,2,1,0:T(8,128)(2,1)S(1)} %get-tuple-element.62), channel_id=1, source_target_pairs={{128,0},{144,8},{136,16},{152,24},{0,128},{16,136},{8,144},{24,152... | collective-permute-start | bytes 589832 | tf_op jit(solution)/shard_map/ppermute | solution.py:48
  114.0 3.9 %collective-permute-done.15.refs_3_ = bf16[2,4,2,16,384]{4,3,2,1,0:T(8,128)(2,1)S(1)} collective-permute-done((bf16[2,4,2,16,384]{4,3,2,1,0:T(8,128)(2,1)S(1)}, bf16[2,4,2,16,384]{4,3,2,1,0:T(8,128)(2,1)S(1)}, u32[]{:S(2)}, u32[]{:S(2)}) %collective-permute-start.15) | collective-permute-done | bytes 196640 | tf_op jit(solution)/shard_map/ppermute | solution.py:48
  117.9 1.0 unpack_oq.1
  118.8 5.9 %collective-permute-done.21.refs_1_ = bf16[2,4,2,16,384]{4,3,2,1,0:T(8,128)(2,1)S(1)} collective-permute-done((bf16[2,4,2,16,384]{4,3,2,1,0:T(8,128)(2,1)S(1)}, bf16[2,4,2,16,384]{4,3,2,1,0:T(8,128)(2,1)S(1)}, u32[]{:S(2)}, u32[]{:S(2)}) %collective-permute-start.21) | collective-permute-done | bytes 196640 | tf_op jit(solution)/shard_map/ppermute | solution.py:48
  124.7 10.3 %collective-permute-done.22.refs_2_ = bf16[2,4,2,16,384]{4,3,2,1,0:T(8,128)(2,1)S(1)} collective-permute-done((bf16[2,4,2,16,384]{4,3,2,1,0:T(8,128)(2,1)S(1)}, bf16[2,4,2,16,384]{4,3,2,1,0:T(8,128)(2,1)S(1)}, u32[]{:S(2)}, u32[]{:S(2)}) %collective-permute-start.22) | collective-permute-done | bytes 196640 | tf_op jit(solution)/shard_map/ppermute | solution.py:48
  135.0 1.0 unpack_dkv.1
  (36 shorter events, 6.9 us)
Async XLA Ops:
  0.6 1.0 copy-start
  1.6 1.0 copy-start.1
  2.6 50.9 %copy-start.4 = (s32[12,3]{0,1:T(4,128)S(1)}, s32[12,3]{0,1:T(4,128)}, u32[]{:S(2)}) copy-start(s32[12,3]{0,1:T(4,128)} %param.9) | copy-start | bytes 436
  2.7 16.3 %collective-permute-start = (bf16[2,4,2,16,384]{4,3,2,1,0:T(8,128)(2,1)S(1)}, bf16[2,4,2,16,384]{4,3,2,1,0:T(8,128)(2,1)S(1)}, u32[]{:S(2)}, u32[]{:S(2)}) collective-permute-start(bf16[2,4,2,16,384]{4,3,2,1,0:T(8,128)(2,1)S(1)} %get-tuple-element.35), channel_id=1, source_target_pairs={{0,0},{8,16},{16,8},{24,24},{128,128},{136,144},{144,136},{152,152... | collective-permute-start | bytes 589832 | tf_op jit(solution)/shard_map/ppermute | solution.py:48
  3.4 15.7 %collective-permute-start.1 = (bf16[2,4,2,16,384]{4,3,2,1,0:T(8,128)(2,1)S(1)}, bf16[2,4,2,16,384]{4,3,2,1,0:T(8,128)(2,1)S(1)}, u32[]{:S(2)}, u32[]{:S(2)}) collective-permute-start(bf16[2,4,2,16,384]{4,3,2,1,0:T(8,128)(2,1)S(1)} %get-tuple-element.36), channel_id=1, source_target_pairs={{0,16},{8,0},{16,24},{24,8},{128,144},{136,128},{144,152},{152,136... | collective-permute-start | bytes 589832 | tf_op jit(solution)/shard_map/ppermute | solution.py:48
  9.9 17.4 %collective-permute-start.2 = (bf16[2,4,2,16,384]{4,3,2,1,0:T(8,128)(2,1)S(1)}, bf16[2,4,2,16,384]{4,3,2,1,0:T(8,128)(2,1)S(1)}, u32[]{:S(2)}, u32[]{:S(2)}) collective-permute-start(bf16[2,4,2,16,384]{4,3,2,1,0:T(8,128)(2,1)S(1)} %get-tuple-element.37), channel_id=1, source_target_pairs={{0,128},{8,144},{16,136},{24,152},{128,0},{136,16},{144,8},{152,24... | collective-permute-start | bytes 589832 | tf_op jit(solution)/shard_map/ppermute | solution.py:48
  16.3 15.1 %collective-permute-start.3 = (bf16[2,4,2,16,384]{4,3,2,1,0:T(8,128)(2,1)S(1)}, bf16[2,4,2,16,384]{4,3,2,1,0:T(8,128)(2,1)S(1)}, u32[]{:S(2)}, u32[]{:S(2)}) collective-permute-start(bf16[2,4,2,16,384]{4,3,2,1,0:T(8,128)(2,1)S(1)} %get-tuple-element.38), channel_id=1, source_target_pairs={{0,144},{8,128},{16,152},{24,136},{128,16},{136,0},{144,24},{152,8... | collective-permute-start | bytes 589832 | tf_op jit(solution)/shard_map/ppermute | solution.py:48
  16.3 1.0 copy-start.2
  17.3 1.0 copy-start.3
  18.3 30.9 %collective-permute-start.8 = (bf16[2,4,2,16,384]{4,3,2,1,0:T(8,128)(2,1)S(1)}, bf16[2,4,2,16,384]{4,3,2,1,0:T(8,128)(2,1)S(1)}, u32[]{:S(2)}, u32[]{:S(2)}) collective-permute-start(bf16[2,4,2,16,384]{4,3,2,1,0:T(8,128)(2,1)S(1)} %get-tuple-element.44), channel_id=1, source_target_pairs={{0,0},{8,16},{16,8},{24,24},{128,128},{136,144},{144,136},{152,152... | collective-permute-start | bytes 589832 | tf_op jit(solution)/shard_map/ppermute | solution.py:48
  31.8 5.9 %collective-permute-start.4 = (bf16[2,64,384]{2,1,0:T(8,128)(2,1)S(1)}, bf16[2,64,384]{2,1,0:T(8,128)(2,1)S(1)}, u32[]{:S(2)}, u32[]{:S(2)}) collective-permute-start(bf16[2,64,384]{2,1,0:T(8,128)(2,1)S(1)} %get-tuple-element.40), channel_id=1, source_target_pairs={{0,1},{1,2},{2,3},{3,4},{4,5},{5,6},{6,7},{8,9},{9,10},{10,11},{11... | collective-permute-start | bytes 294920 | tf_op jit(solution)/shard_map/ppermute | solution.py:74
  33.7 5.8 %collective-permute-start.5 = (bf16[2,64,384]{2,1,0:T(8,128)(2,1)S(1)}, bf16[2,64,384]{2,1,0:T(8,128)(2,1)S(1)}, u32[]{:S(2)}, u32[]{:S(2)}) collective-permute-start(bf16[2,64,384]{2,1,0:T(8,128)(2,1)S(1)} %get-tuple-element.41), channel_id=1, source_target_pairs={{1,0},{2,1},{3,2},{4,3},{5,4},{6,5},{7,6},{9,8},{10,9},{11,10},{12... | collective-permute-start | bytes 294920 | tf_op jit(solution)/shard_map/ppermute | solution.py:73
  39.6 31.3 %collective-permute-start.6 = (bf16[2,160,384]{2,1,0:T(8,128)(2,1)S(1)}, bf16[2,160,384]{2,1,0:T(8,128)(2,1)S(1)}, u32[]{:S(2)}, u32[]{:S(2)}) collective-permute-start(bf16[2,160,384]{2,1,0:T(8,128)(2,1)S(1)} %get-tuple-element.42), channel_id=1, source_target_pairs={{0,8},{8,0},{16,24},{24,16},{128,136},{136,128},{144,152},{152,144... | collective-permute-start | bytes 737288 | tf_op jit(solution)/shard_map/ppermute | solution.py:66
  44.3 26.7 %collective-permute-start.7 = (bf16[2,160,384]{2,1,0:T(8,128)(2,1)S(1)}, bf16[2,160,384]{2,1,0:T(8,128)(2,1)S(1)}, u32[]{:S(2)}, u32[]{:S(2)}) collective-permute-start(bf16[2,160,384]{2,1,0:T(8,128)(2,1)S(1)} %get-tuple-element.43), channel_id=1, source_target_pairs={{8,40},{24,56},{136,168},{152,184},{32,64},{40,8},{48,80},{56,24},... | collective-permute-start | bytes 737288 | tf_op jit(solution)/shard_map/ppermute | solution.py:67
  44.9 9.9 %collective-permute-start.9 = (bf16[2,4,2,16,384]{4,3,2,1,0:T(8,128)(2,1)S(1)}, bf16[2,4,2,16,384]{4,3,2,1,0:T(8,128)(2,1)S(1)}, u32[]{:S(2)}, u32[]{:S(2)}) collective-permute-start(bf16[2,4,2,16,384]{4,3,2,1,0:T(8,128)(2,1)S(1)} %get-tuple-element.45), channel_id=1, source_target_pairs={{0,16},{8,0},{16,24},{24,8},{128,144},{136,128},{144,152},{152,136... | collective-permute-start | bytes 589832 | tf_op jit(solution)/shard_map/ppermute | solution.py:48
  47.3 13.4 %collective-permute-start.10 = (bf16[2,4,2,16,384]{4,3,2,1,0:T(8,128)(2,1)S(1)}, bf16[2,4,2,16,384]{4,3,2,1,0:T(8,128)(2,1)S(1)}, u32[]{:S(2)}, u32[]{:S(2)}) collective-permute-start(bf16[2,4,2,16,384]{4,3,2,1,0:T(8,128)(2,1)S(1)} %get-tuple-element.46), channel_id=1, source_target_pairs={{0,128},{8,144},{16,136},{24,152},{128,0},{136,16},{144,8},{152,24... | collective-permute-start | bytes 589832 | tf_op jit(solution)/shard_map/ppermute | solution.py:48
  49.3 21.6 %collective-permute-start.11 = (bf16[2,4,2,16,384]{4,3,2,1,0:T(8,128)(2,1)S(1)}, bf16[2,4,2,16,384]{4,3,2,1,0:T(8,128)(2,1)S(1)}, u32[]{:S(2)}, u32[]{:S(2)}) collective-permute-start(bf16[2,4,2,16,384]{4,3,2,1,0:T(8,128)(2,1)S(1)} %get-tuple-element.47), channel_id=1, source_target_pairs={{0,144},{8,128},{16,152},{24,136},{128,16},{136,0},{144,24},{152,8... | collective-permute-start | bytes 589832 | tf_op jit(solution)/shard_map/ppermute | solution.py:48
  81.4 14.2 %collective-permute-start.16 = (bf16[2,160,384]{2,1,0:T(8,128)(2,1)S(1)}, bf16[2,160,384]{2,1,0:T(8,128)(2,1)S(1)}, u32[]{:S(2)}, u32[]{:S(2)}) collective-permute-start(bf16[2,160,384]{2,1,0:T(8,128)(2,1)S(1)} %get-tuple-element.55), channel_id=1, source_target_pairs={{0,8},{8,0},{16,24},{24,16},{128,136},{136,128},{144,152},{152,144... | collective-permute-start | bytes 737288 | tf_op jit(solution)/shard_map/ppermute | solution.py:66
  85.5 10.1 %collective-permute-start.17 = (bf16[2,160,384]{2,1,0:T(8,128)(2,1)S(1)}, bf16[2,160,384]{2,1,0:T(8,128)(2,1)S(1)}, u32[]{:S(2)}, u32[]{:S(2)}) collective-permute-start(bf16[2,160,384]{2,1,0:T(8,128)(2,1)S(1)} %get-tuple-element.56), channel_id=1, source_target_pairs={{8,40},{24,56},{136,168},{152,184},{32,64},{40,8},{48,80},{56,24},... | collective-permute-start | bytes 737288 | tf_op jit(solution)/shard_map/ppermute | solution.py:67
  86.2 19.1 %collective-permute-start.12 = (bf16[2,4,2,16,384]{4,3,2,1,0:T(8,128)(2,1)S(1)}, bf16[2,4,2,16,384]{4,3,2,1,0:T(8,128)(2,1)S(1)}, u32[]{:S(2)}, u32[]{:S(2)}) collective-permute-start(bf16[2,4,2,16,384]{4,3,2,1,0:T(8,128)(2,1)S(1)} %get-tuple-element.48), channel_id=1, source_target_pairs={{0,0},{16,8},{8,16},{24,24},{128,128},{144,136},{136,144},{152,152... | collective-permute-start | bytes 589832 | tf_op jit(solution)/shard_map/ppermute | solution.py:48
  86.9 22.1 %collective-permute-start.13 = (bf16[2,4,2,16,384]{4,3,2,1,0:T(8,128)(2,1)S(1)}, bf16[2,4,2,16,384]{4,3,2,1,0:T(8,128)(2,1)S(1)}, u32[]{:S(2)}, u32[]{:S(2)}) collective-permute-start(bf16[2,4,2,16,384]{4,3,2,1,0:T(8,128)(2,1)S(1)} %get-tuple-element.49), channel_id=1, source_target_pairs={{16,0},{0,8},{24,16},{8,24},{144,128},{128,136},{152,144},{136,152... | collective-permute-start | bytes 589832 | tf_op jit(solution)/shard_map/ppermute | solution.py:48
  91.3 21.9 %collective-permute-start.14 = (bf16[2,4,2,16,384]{4,3,2,1,0:T(8,128)(2,1)S(1)}, bf16[2,4,2,16,384]{4,3,2,1,0:T(8,128)(2,1)S(1)}, u32[]{:S(2)}, u32[]{:S(2)}) collective-permute-start(bf16[2,4,2,16,384]{4,3,2,1,0:T(8,128)(2,1)S(1)} %get-tuple-element.50), channel_id=1, source_target_pairs={{128,0},{144,8},{136,16},{152,24},{0,128},{16,136},{8,144},{24,152... | collective-permute-start | bytes 589832 | tf_op jit(solution)/shard_map/ppermute | solution.py:48
  95.6 5.9 %collective-permute-start.18 = (bf16[2,64,384]{2,1,0:T(8,128)(2,1)S(1)}, bf16[2,64,384]{2,1,0:T(8,128)(2,1)S(1)}, u32[]{:S(2)}, u32[]{:S(2)}) collective-permute-start(bf16[2,64,384]{2,1,0:T(8,128)(2,1)S(1)} %get-tuple-element.58), channel_id=1, source_target_pairs={{0,1},{1,2},{2,3},{3,4},{4,5},{5,6},{6,7},{8,9},{9,10},{10,11},{11... | collective-permute-start | bytes 294920 | tf_op jit(solution)/shard_map/ppermute | solution.py:74
  97.6 6.4 %collective-permute-start.19 = (bf16[2,64,384]{2,1,0:T(8,128)(2,1)S(1)}, bf16[2,64,384]{2,1,0:T(8,128)(2,1)S(1)}, u32[]{:S(2)}, u32[]{:S(2)}) collective-permute-start(bf16[2,64,384]{2,1,0:T(8,128)(2,1)S(1)} %get-tuple-element.59), channel_id=1, source_target_pairs={{1,0},{2,1},{3,2},{4,3},{5,4},{6,5},{7,6},{9,8},{10,9},{11,10},{12... | collective-permute-start | bytes 294920 | tf_op jit(solution)/shard_map/ppermute | solution.py:73
  101.6 16.3 %collective-permute-start.15 = (bf16[2,4,2,16,384]{4,3,2,1,0:T(8,128)(2,1)S(1)}, bf16[2,4,2,16,384]{4,3,2,1,0:T(8,128)(2,1)S(1)}, u32[]{:S(2)}, u32[]{:S(2)}) collective-permute-start(bf16[2,4,2,16,384]{4,3,2,1,0:T(8,128)(2,1)S(1)} %get-tuple-element.51), channel_id=1, source_target_pairs={{144,0},{128,8},{152,16},{136,24},{16,128},{0,136},{24,144},{8,152... | collective-permute-start | bytes 589832 | tf_op jit(solution)/shard_map/ppermute | solution.py:48
  104.6 14.2 %collective-permute-start.20 = (bf16[2,4,2,16,384]{4,3,2,1,0:T(8,128)(2,1)S(1)}, bf16[2,4,2,16,384]{4,3,2,1,0:T(8,128)(2,1)S(1)}, u32[]{:S(2)}, u32[]{:S(2)}) collective-permute-start(bf16[2,4,2,16,384]{4,3,2,1,0:T(8,128)(2,1)S(1)} %get-tuple-element.60), channel_id=1, source_target_pairs={{0,0},{16,8},{8,16},{24,24},{128,128},{144,136},{136,144},{152,152... | collective-permute-start | bytes 589832 | tf_op jit(solution)/shard_map/ppermute | solution.py:48
  105.3 19.4 %collective-permute-start.21 = (bf16[2,4,2,16,384]{4,3,2,1,0:T(8,128)(2,1)S(1)}, bf16[2,4,2,16,384]{4,3,2,1,0:T(8,128)(2,1)S(1)}, u32[]{:S(2)}, u32[]{:S(2)}) collective-permute-start(bf16[2,4,2,16,384]{4,3,2,1,0:T(8,128)(2,1)S(1)} %get-tuple-element.61), channel_id=1, source_target_pairs={{16,0},{0,8},{24,16},{8,24},{144,128},{128,136},{152,144},{136,152... | collective-permute-start | bytes 589832 | tf_op jit(solution)/shard_map/ppermute | solution.py:48
  108.9 26.1 %collective-permute-start.22 = (bf16[2,4,2,16,384]{4,3,2,1,0:T(8,128)(2,1)S(1)}, bf16[2,4,2,16,384]{4,3,2,1,0:T(8,128)(2,1)S(1)}, u32[]{:S(2)}, u32[]{:S(2)}) collective-permute-start(bf16[2,4,2,16,384]{4,3,2,1,0:T(8,128)(2,1)S(1)} %get-tuple-element.62), channel_id=1, source_target_pairs={{128,0},{144,8},{136,16},{152,24},{0,128},{16,136},{8,144},{24,152... | collective-permute-start | bytes 589832 | tf_op jit(solution)/shard_map/ppermute | solution.py:48
  113.2 21.8 %collective-permute-start.23 = (bf16[2,4,2,16,384]{4,3,2,1,0:T(8,128)(2,1)S(1)}, bf16[2,4,2,16,384]{4,3,2,1,0:T(8,128)(2,1)S(1)}, u32[]{:S(2)}, u32[]{:S(2)}) collective-permute-start(bf16[2,4,2,16,384]{4,3,2,1,0:T(8,128)(2,1)S(1)} %get-tuple-element.63), channel_id=1, source_target_pairs={{144,0},{128,8},{152,16},{136,24},{16,128},{0,136},{24,144},{8,152... | collective-permute-start | bytes 589832 | tf_op jit(solution)/shard_map/ppermute | solution.py:48

commit v2 on v1

v2 whole, which is shorter than its diff:
```python
from functools import partial
import math

import jax
import jax.numpy as jnp
from jax import lax
from jax.experimental import pallas as pl
from jax.experimental.pallas import tpu as pltpu
from jax.sharding import PartitionSpec as P

NEG = -1e30
BF = jnp.bfloat16
F32 = jnp.float32

GROUPS = 4
LANES = 384
HEAD = 128
GH = LANES // HEAD
ALL = ("ta", "ha", "wa")


DEAL = (
    (
        ((2, 1, 0, 3), (3, 2, 1, 0), (0, 3, 2, 1), (1, 0, 3, 2)),
        ((2, 1, 0, 3), (3, 0, 1, 2), (0, 3, 2, 1), (1, 2, 3, 0)),
    ),
    (
        ((0, 3, 2, 1), (1, 0, 3, 2), (2, 1, 0, 3), (3, 2, 1, 0)),
        ((0, 3, 2, 1), (3, 2, 1, 0), (2, 1, 0, 3), (1, 0, 3, 2)),
    ),
)


def code(turns):
    bits = sum(turns[r][i] << 2 * (4 * r + i) for r in range(4) for i in range(4))
    return bits - (1 << 32) if bits >= 1 << 31 else bits


def inverse(turns):
    return [[row.index(g) for g in range(4)] for row in turns]


def place():
    ta, ha, wa = (lax.axis_index(n) for n in ALL)
    z, y = ta * 4 + ha % 4, wa // 2
    return z // 2, wa % 2, (z + y) % 2, ha // 4


def looked_up(parity, half, table_of, at):
    which = parity * 2 + half
    bits = jnp.int32(code(table_of(DEAL[0][0])))
    for n in range(1, 4):
        bits = jnp.where(which == n, jnp.int32(code(table_of(DEAL[n // 2][n % 2]))), bits)
    return [lax.shift_right_logical(bits, 2 * (4 * r + at)) & 3 for r in range(GROUPS)]


def groups_out():
    ta, ha, wa = (lax.axis_index(n) for n in ALL)
    return looked_up((wa // 2 + wa) % 2, ha % 4 // 2, lambda t: t, ta * 2 + ha % 2)


def blocks_in():
    ta, ha, wa = (lax.axis_index(n) for n in ALL)
    return looked_up(ha % 2, wa % 2, inverse, (ta * 4 + ha % 4) // 2)


def lin(x, y, z, core):
    return (z // 4) * 128 + (x * 4 + z % 4) * 8 + y * 2 + core


EVERY = [(x, y, z, c) for x in range(4) for y in range(4) for z in range(8) for c in range(2)]


def deal_pairs(turn, back):
    pairs = []
    for x, y, z, core in EVERY:
        parity, half = (core + y) % 2, z % 4 // 2
        group = DEAL[parity][half][turn][(z // 4) * 2 + z % 2]
        pair = (lin(x, y, z, core), lin(x, y, 2 * group + parity, half))
        pairs.append(pair[::-1] if back else pair)
    return pairs


def deal(bufs, back):
    return [lax.ppermute(b, ALL, deal_pairs(r, back)) for r, b in enumerate(bufs)]


def swap(buf, partner_of):
    pairs = []
    for x, y, z, core in EVERY:
        x2, y2, z2, core2 = partner_of(x, y, z, core)
        if 0 <= x2 < 4 and 0 <= y2 < 4:
            pairs.append((lin(x, y, z, core), lin(x2, y2, z2, core2)))
    return lax.ppermute(buf, ALL, pairs)


def rows_swap(inner, outer):
    return (
        swap(inner, lambda x, y, z, c: (x, y, z, 1 - c)),
        swap(outer, lambda x, y, z, c: (x + 2 * c - 1, y, z, 1 - c)),
    )


def cols_swap(inner, outer):
    return (
        swap(inner, lambda x, y, z, c: (x, y, z ^ 1, c)),
        swap(outer, lambda x, y, z, c: (x, y + 2 * ((z + y) % 2) - 1, z, c)),
    )


def ordered(first, later):
    got = lax.optimization_barrier((first[0],) + tuple(later))
    return [got[0]] + list(first[1:]), list(got[1:])


def call(body, outs, scratch=(), flops=0, size=3 << 20, name=None, **specs):
    return pl.pallas_call(
        body,
        out_shape=outs,
        scratch_shapes=list(scratch),
        compiler_params=pltpu.CompilerParams(vmem_limit_bytes=48 << 20),
        cost_estimate=pl.CostEstimate(flops=flops, bytes_accessed=size, transcendentals=0),
        name=name,
        **specs,
    )


def shaped(*dims, dtype=BF):
    return jax.ShapeDtypeStruct(dims, dtype)


DEALT = (2, 2, 4, 16, LANES)
FAR = pl.BlockSpec(memory_space=pltpu.HBM)
NEAR = pl.BlockSpec(memory_space=pltpu.VMEM)


def lanes_of(group):
    return pl.ds(pl.multiple_of(group * LANES, LANES), LANES)


def run_copies(pairs, sems):
    copies = [pltpu.make_async_copy(a, b, sems.at[n]) for n, (a, b) in enumerate(pairs)]
    for c in copies:
        c.start()
    for c in copies:
        c.wait()


def pack_body(*refs):
    ins, outs, sems = refs[:2], refs[2:-1], refs[-1]
    run_copies(
        [
            (ref.at[:, :, :, lanes_of(group)], out.at[i])
            for group, out in zip(groups_out(), outs)
            for i, ref in enumerate(ins)
        ],
        sems,
    )


def pack(a, b, name):
    return call(
        pack_body,
        [shaped(*DEALT)] * GROUPS,
        [pltpu.SemaphoreType.DMA((2 * GROUPS,))],
        in_specs=[FAR] * 2,
        out_specs=[NEAR] * GROUPS,
        name=name,
    )(a, b)


def unpack_body(*refs):
    bufs, outs, sems = refs[:GROUPS], refs[GROUPS:-1], refs[-1]
    run_copies(
        [
            (buf.at[i], ref.at[:, :, :, lanes_of(group)])
            for group, buf in zip(groups_out(), bufs)
            for i, ref in enumerate(outs)
        ],
        sems,
    )


def unpack(bufs, name):
    return call(
        unpack_body,
        [shaped(2, 4, 16, GROUPS * LANES)] * 2,
        [pltpu.SemaphoreType.DMA((2 * GROUPS,))],
        in_specs=[NEAR] * GROUPS,
        out_specs=[FAR] * 2,
        name=name,
    )(*bufs)


def spot(src, t, h):
    return pl.ds(pl.multiple_of((src % 2) * 256 + (src // 2) * 32 + h * 64 + t * 16, 16), 16)


BLOCK = [(t, h) for t in range(2) for h in range(4)]


def gather_blocks(bufs, i, dest):
    for src, buf in zip(blocks_in(), bufs):
        for t, h in BLOCK:
            dest[i, spot(src, t, h), :] = buf[i, t, h]


def edge_pick(transpose):
    shape = (512, 128) if transpose else (128, 512)
    e = lax.broadcasted_iota(jnp.int32, shape, 1 if transpose else 0)
    token = lax.broadcasted_iota(jnp.int32, shape, 0 if transpose else 1)
    want = (e % 64) // 2 * 16 + e % 2 + 14 * (e // 64)
    return jnp.where(token == want, 1.0, 0.0).astype(BF)


def side_slots(block):
    return 1 - block, block


def row_slots(half):
    return 1 - half, half


def at_16(start, size=16):
    return pl.ds(pl.multiple_of(start, 16), size)


def own_body(*refs):
    bufs, (own, *outs), edges = refs[:GROUPS], refs[GROUPS:-1], refs[-1]
    _, _, block, _ = place()
    pick = edge_pick(False)
    for i in range(2):
        gather_blocks(bufs, i, own)
        both = jnp.dot(pick, own[i], preferred_element_type=F32).astype(BF)
        edges[0, i] = both[:64]
        edges[1, i] = both[64:]
    for out, slot in zip(outs, side_slots(block)):
        out[...] = edges[slot]


def own_kv(bufs):
    outs = [shaped(2, 512, LANES), shaped(2, 64, LANES), shaped(2, 64, LANES)]
    return call(own_body, outs, [pltpu.VMEM((2, 2, 64, LANES), BF)], name="own_kv")(*bufs)


def rows_body(own, inner, outer, *outs):
    _, half, block, _ = place()
    for out, below in zip(outs, row_slots(half)):
        out[:, 0:128] = own[:, at_16(below * 384, 128)]
        for side, slot in zip((inner, outer), side_slots(block)):
            out[:, at_16(128 + slot * 16)] = side[:, at_16(below * 48)]


def rows_out(own, inner, outer):
    return call(rows_body, [shaped(2, 160, LANES)] * 2, name="rows_out")(own, inner, outer)


NT = (((1,), (1,)), ((), ()))
TN = (((0,), (0,)), ((), ()))


def attend_body(window, own, col_in, col_out, row_in, row_out, *refs):
    qd = refs[:GROUPS]
    back = refs[GROUPS : 2 * GROUPS]
    own_grad, side_grad, *rows_back = refs[2 * GROUPS : 2 * GROUPS + 4]
    kv_mid, kv_side, g_mid, g_side, q_all, o_all = refs[2 * GROUPS + 4 :]
    group, half, block, x = place()
    w_at = lax.axis_index("wa") // 2 * 2 + block
    w_last = lax.axis_size("wa") - 1
    scale = 1.0 / math.sqrt(HEAD)
    log2e = 1.0 / math.log(2.0)

    rows = list(zip((row_in, row_out), row_slots(half)))
    for i in range(2):
        kv_mid[i, 128:640] = own[i]
        for side, slot in zip((col_in, col_out), side_slots(block)):
            kv_side[slot, i, 16:80] = side[i]
        for buf, below in rows:
            kv_mid[i, at_16(below * 640, 128)] = buf[i, 0:128]
            for slot in range(2):
                kv_side[slot, i, at_16(below * 80)] = buf[i, 128 + 16 * slot : 144 + 16 * slot]
        gather_blocks(qd, i, q_all)

    qi = lax.broadcasted_iota(jnp.int32, (128, 1), 0)
    q_t, q_w = qi // 32 % 2, qi % 16 // 2
    ki = lax.broadcasted_iota(jnp.int32, (1, 480), 1)
    mid = ki < 384
    ks = jnp.where(ki < 432, ki - 384, ki - 432)
    k_t = jnp.where(mid, ki // 32 % 2, ks // 4 % 2)
    k_w = jnp.where(mid, ki % 16 // 2, jnp.where(ki < 432, -1, 8))
    k_h = jnp.where(mid, ki // 128, ks // 16)
    beside = ((k_w >= 0) | (w_at > 0)) & ((k_w < 8) | (w_at < w_last))
    tile_row = (x * 2 + half) * 4 - 1
    tile_rows = 4 * 8

    for n in range(GH):
        f = slice(n * HEAD, (n + 1) * HEAD)
        head = group * GH + n
        rad_t, rad_h, rad_w = window[head, 0], window[head, 1], window[head, 2]
        near = (jnp.abs(q_t - k_t) <= rad_t) & (jnp.abs(q_w - k_w) <= rad_w)
        base = jnp.where(near, 0.0, NEG)
        inside = beside & (jnp.abs(k_h - 1) <= rad_h)
        all_w, all_ds = [], []
        side_g = [[[None] * 6, [None] * 6], [[None] * 6, [None] * 6]]
        for blk in range(4):
            row = tile_row + blk + k_h
            row_bias = jnp.where(inside & (row >= 0) & (row < tile_rows), 0.0, NEG)
            mid_at, side_at, q_at = pl.ds(128 * blk, 384), pl.ds(16 * blk, 48), pl.ds(128 * blk, 128)
            k, v = (
                jnp.concatenate(
                    [kv_mid[i, mid_at, f], kv_side[0, i, side_at, f], kv_side[1, i, side_at, f]], axis=0
                )
                for i in range(2)
            )
            q, do = q_all[0, q_at, f], q_all[1, q_at, f]
            s = lax.dot_general(q, k, NT, preferred_element_type=F32)
            s = s * (scale * log2e) + (base + row_bias)
            top = jnp.max(s, axis=1, keepdims=True)
            e = jnp.exp2(s - top)
            p = e * (1.0 / jnp.sum(e, axis=1, keepdims=True))
            wts = p.astype(BF)
            o = jnp.dot(wts, v, preferred_element_type=F32).astype(BF)
            delta = jnp.sum(do.astype(F32) * o.astype(F32), axis=1, keepdims=True)
            dp = lax.dot_general(do, v, NT, preferred_element_type=F32)
            ds = (p * (dp - delta)).astype(BF)
            dq = jnp.dot(ds, k, preferred_element_type=F32) * scale
            o_all[0, q_at, f] = o
            o_all[1, q_at, f] = dq.astype(BF)
            all_ds.append(ds)
            all_w.append(wts)
            for i, (a, b) in enumerate(((ds, q), (wts, do))):
                part = lax.dot_general(a[:, 384:480], b, TN, preferred_element_type=F32)
                for lr in range(2):
                    for o_ in range(3):
                        piece = part[48 * lr + 16 * o_ : 48 * lr + 16 * o_ + 16]
                        have = side_g[i][lr][blk + o_]
                        side_g[i][lr][blk + o_] = piece if have is None else have + piece
        for i, a in enumerate((all_ds, all_w)):
            mul = scale if i == 0 else 1.0
            for j in range(6):
                blks = [b for b in range(4) if 0 <= j - b <= 2]
                lhs = [a[b][:, 128 * (j - b) : 128 * (j - b) + 128] for b in blks]
                lhs = lhs[0] if len(lhs) == 1 else jnp.concatenate(lhs, axis=0)
                rhs = q_all[i, pl.ds(128 * blks[0], 128 * len(blks)), f]
                g_mid[i, 128 * j : 128 * j + 128, f] = (
                    lax.dot_general(lhs, rhs, TN, preferred_element_type=F32) * mul
                )
                for slot in range(2):
                    g_side[slot, i, 16 * j : 16 * j + 16, f] = side_g[i][slot][j] * mul

    for src, out in zip(blocks_in(), back):
        for i in range(2):
            for t, h in BLOCK:
                out[i, t, h] = o_all[i, spot(src, t, h), :]
    for i in range(2):
        own_grad[i] = g_mid[i, 128:640]
        for slot in range(2):
            side_grad[slot, i] = g_side[slot, i, 16:80]
        for out, (_, below) in zip(rows_back, rows):
            out[i, 0:128] = g_mid[i, at_16(below * 640, 128)].astype(BF)
            for slot in range(2):
                out[i, 128 + 16 * slot : 144 + 16 * slot] = g_side[slot, i, at_16(below * 80)].astype(BF)


def attend(window, own, cols, rows, qd):
    outs = [shaped(*DEALT)] * GROUPS + [
        shaped(2, 512, LANES, dtype=F32),
        shaped(2, 2, 64, LANES, dtype=F32),
        shaped(2, 160, LANES),
        shaped(2, 160, LANES),
    ]
    ins = [own, *cols, *rows, *qd]
    scratch = [
        pltpu.VMEM((2, 768, LANES), BF),
        pltpu.VMEM((2, 2, 96, LANES), BF),
        pltpu.VMEM((2, 768, LANES), F32),
        pltpu.VMEM((2, 2, 96, LANES), F32),
        pltpu.VMEM((2, 512, LANES), BF),
        pltpu.VMEM((2, 512, LANES), BF),
    ]
    return call(
        attend_body,
        outs,
        scratch,
        in_specs=[pl.BlockSpec(memory_space=pltpu.SMEM)] + [NEAR] * len(ins),
        out_specs=[NEAR] * len(outs),
        flops=1200000000,
        size=8 << 20,
        name="attend",
    )(window, *ins)


def side_body(side_grad, row_in, row_out, *outs):
    _, half, block, _ = place()
    for out, slot in zip(outs, side_slots(block)):
        for i in range(2):
            out[i] = side_grad[slot, i].astype(BF)
            for buf, below in zip((row_in, row_out), row_slots(half)):
                at = at_16(below * 48)
                come = buf[i, at_16(128 + slot * 16)].astype(F32)
                out[i, at] = (side_grad[slot, i, at] + come).astype(BF)


def side_out(side_grad, rows):
    return call(side_body, [shaped(2, 64, LANES)] * 2, name="side_out")(side_grad, *rows)


def final_body(own_grad, row_in, row_out, col_in, col_out, *refs):
    outs, (total, edges) = refs[:GROUPS], refs[GROUPS:]
    _, half, block, _ = place()
    spread = edge_pick(True)
    for i in range(2):
        for side, slot in zip((col_in, col_out), side_slots(block)):
            edges[slot, i] = side[i]
        both = jnp.concatenate([edges[0, i], edges[1, i]], axis=0)
        total[i] = own_grad[i] + jnp.dot(spread, both, preferred_element_type=F32)
        for buf, below in zip((row_in, row_out), row_slots(half)):
            total[i, at_16(below * 384, 128), :] += buf[i, 0:128].astype(F32)
        for src, out in zip(blocks_in(), outs):
            for t, h in BLOCK:
                out[i, t, h] = total[i, spot(src, t, h), :].astype(BF)


def final(own_grad, rows, cols):
    scratch = [pltpu.VMEM((2, 512, LANES), F32), pltpu.VMEM((2, 2, 64, LANES), BF)]
    return call(final_body, [shaped(*DEALT)] * GROUPS, scratch, name="final")(own_grad, *rows, *cols)


def local(queries, keys, values, out_grad, head_window):
    sent = list(pack(keys, values, "pack_kv"))
    sent, (queries, out_grad) = ordered(sent, (queries, out_grad))
    kv = deal(sent, False)
    qd = deal(pack(queries, out_grad, "pack_qd"), False)
    kv, qd[:1] = ordered(kv, qd[:1])
    own, *edges = own_kv(kv)
    cols = cols_swap(*edges)
    cols, qd[1:] = ordered(cols, qd[1:])
    rows = rows_swap(*rows_out(own, *cols))
    results = attend(head_window, own, cols, rows, qd)
    oq = deal(results[:GROUPS], True)
    own_grad, side_grad, *rows_back = results[GROUPS:]
    rows = rows_swap(*rows_back)
    cols = cols_swap(*side_out(side_grad, rows))
    dkv = deal(final(own_grad, rows, cols), True)
    attended, query_grad = unpack(oq, "unpack_oq")
    key_grad, value_grad = unpack(dkv, "unpack_dkv")
    return attended, query_grad, key_grad, value_grad


def solution(mesh):
    spec = P("ta", "ha", "wa", None)
    return jax.shard_map(
        local,
        mesh=mesh,
        in_specs=(spec,) * 4 + (P(),),
        out_specs=(spec,) * 4,
        check_vma=False,
    )
```

time: 137 us -> 119 us (0.87)
  the two profiles are of different devices: /device:TPU:8 before, /device:TPU:51 now
where the time goes in v2:
time: 119 us; the launch traced here: 117 us
  starting transfers between devices  72.9 us (61%)
  waiting for transfers between devices  26.1 us (22%)
  Pallas kernels  13.2 us (11%)
  local copies, waits for them, and re-layouts  4.07 us (3%)
    ppermute x16, starting transfers between devices, deal(): lax.ppermute(b, ALL, deal_pairs(r, back))  56 us
    ppermute x8, starting transfers between devices, swap(): return lax.ppermute(buf, ALL, pairs)  16.9 us
    ppermute x16, waiting for transfers between devices, deal(): lax.ppermute(b, ALL, deal_pairs(r, back))  14.3 us
    ppermute x8, waiting for transfers between devices, swap(): return lax.ppermute(buf, ALL, pairs)  11.8 us
    pallas_call x1, Pallas kernels, attend(): call(attend_body, outs, scratch, in_specs=[pl.BlockSpec(memory_space=pltp...  9.71 us
    unnamed x11, local copies, waits for them, and re-layouts  4.07 us
  transfers between devices with their start and end apart: 24, of which 6 were waited for; matrix products, arithmetic and copies ran while one was open for 0% of the time, Pallas kernels for 2%

profile of v2, /device:TPU:51, one launch (start us, length us, event | category | flops | bytes accessed | tf_op | source)
XLA Modules:
  0.0 117.4 jit_solution(12939534165929221572)
XLA Ops:
  0.6 1.0 copy-done
  1.6 1.0 copy-done.1
  2.8 5.8 %collective-permute-start = (bf16[2,2,4,16,384]{4,3,2,1,0:T(8,128)(2,1)S(1)}, bf16[2,2,4,16,384]{4,3,2,1,0:T(8,128)(2,1)S(1)}, u32[]{:S(2)}, u32[]{:S(2)}) collective-permute-start(bf16[2,2,4,16,384]{4,3,2,1,0:T(8,128)(2,1)S(1)} %get-tuple-element.45), channel_id=1, source_target_pairs={{0,128},{1,8},{8,16},{9,152},{16,129},{17,9},{24,17},{25,153},{128... | collective-permute-start | bytes 589832 | tf_op jit(solution)/shard_map/ppermute | solution.py:85
  8.6 1.9 %collective-permute-start.2 = (bf16[2,2,4,16,384]{4,3,2,1,0:T(8,128)(2,1)S(1)}, bf16[2,2,4,16,384]{4,3,2,1,0:T(8,128)(2,1)S(1)}, u32[]{:S(2)}, u32[]{:S(2)}) collective-permute-start(bf16[2,2,4,16,384]{4,3,2,1,0:T(8,128)(2,1)S(1)} %get-tuple-element.50), channel_id=1, source_target_pairs={{0,144},{1,24},{8,128},{9,8},{16,145},{17,153},{24,1},{25,137},{12... | collective-permute-start | bytes 589832 | tf_op jit(solution)/shard_map/ppermute | solution.py:85
  10.5 1.0 copy-done.2
  11.5 1.0 copy-done.3
  12.7 2.7 %collective-permute-start.1 = (bf16[2,2,4,16,384]{4,3,2,1,0:T(8,128)(2,1)S(1)}, bf16[2,2,4,16,384]{4,3,2,1,0:T(8,128)(2,1)S(1)}, u32[]{:S(2)}, u32[]{:S(2)}) collective-permute-start(bf16[2,2,4,16,384]{4,3,2,1,0:T(8,128)(2,1)S(1)} %get-tuple-element.48), channel_id=1, source_target_pairs={{0,128},{1,8},{8,16},{9,152},{16,129},{17,9},{24,17},{25,153},{128... | collective-permute-start | bytes 589832 | tf_op jit(solution)/shard_map/ppermute | solution.py:85
  15.4 2.5 %collective-permute-start.3 = (bf16[2,2,4,16,384]{4,3,2,1,0:T(8,128)(2,1)S(1)}, bf16[2,2,4,16,384]{4,3,2,1,0:T(8,128)(2,1)S(1)}, u32[]{:S(2)}, u32[]{:S(2)}) collective-permute-start(bf16[2,2,4,16,384]{4,3,2,1,0:T(8,128)(2,1)S(1)} %get-tuple-element.51), channel_id=1, source_target_pairs={{0,0},{1,136},{8,144},{9,24},{16,1},{17,137},{24,145},{25,25},{128... | collective-permute-start | bytes 589832 | tf_op jit(solution)/shard_map/ppermute | solution.py:85
  17.9 6.2 %collective-permute-start.4 = (bf16[2,2,4,16,384]{4,3,2,1,0:T(8,128)(2,1)S(1)}, bf16[2,2,4,16,384]{4,3,2,1,0:T(8,128)(2,1)S(1)}, u32[]{:S(2)}, u32[]{:S(2)}) collective-permute-start(bf16[2,2,4,16,384]{4,3,2,1,0:T(8,128)(2,1)S(1)} %get-tuple-element.52), channel_id=1, source_target_pairs={{0,16},{1,152},{8,0},{9,136},{16,17},{17,25},{24,129},{25,9},{128,... | collective-permute-start | bytes 589832 | tf_op jit(solution)/shard_map/ppermute | solution.py:85
  24.1 1.9 %collective-permute-start.6 = (bf16[2,2,4,16,384]{4,3,2,1,0:T(8,128)(2,1)S(1)}, bf16[2,2,4,16,384]{4,3,2,1,0:T(8,128)(2,1)S(1)}, u32[]{:S(2)}, u32[]{:S(2)}) collective-permute-start(bf16[2,2,4,16,384]{4,3,2,1,0:T(8,128)(2,1)S(1)} %get-tuple-element.55), channel_id=1, source_target_pairs={{0,144},{1,24},{8,128},{9,8},{16,145},{17,153},{24,1},{25,137},{12... | collective-permute-start | bytes 589832 | tf_op jit(solution)/shard_map/ppermute | solution.py:85
  26.1 3.4 %collective-permute-start.7 = (bf16[2,2,4,16,384]{4,3,2,1,0:T(8,128)(2,1)S(1)}, bf16[2,2,4,16,384]{4,3,2,1,0:T(8,128)(2,1)S(1)}, u32[]{:S(2)}, u32[]{:S(2)}) collective-permute-start(bf16[2,2,4,16,384]{4,3,2,1,0:T(8,128)(2,1)S(1)} %get-tuple-element.56), channel_id=1, source_target_pairs={{0,0},{1,136},{8,144},{9,24},{16,1},{17,137},{24,145},{25,25},{128... | collective-permute-start | bytes 589832 | tf_op jit(solution)/shard_map/ppermute | solution.py:85
  29.5 5.9 %collective-permute-start.8 = (bf16[2,2,4,16,384]{4,3,2,1,0:T(8,128)(2,1)S(1)}, bf16[2,2,4,16,384]{4,3,2,1,0:T(8,128)(2,1)S(1)}, u32[]{:S(2)}, u32[]{:S(2)}) collective-permute-start(bf16[2,2,4,16,384]{4,3,2,1,0:T(8,128)(2,1)S(1)} %get-tuple-element.57), channel_id=1, source_target_pairs={{0,16},{1,152},{8,0},{9,136},{16,17},{17,25},{24,129},{25,9},{128,... | collective-permute-start | bytes 589832 | tf_op jit(solution)/shard_map/ppermute | solution.py:85
  35.9 2.2 %collective-permute-start.5 = (bf16[2,64,384]{2,1,0:T(8,128)(2,1)S(1)}, bf16[2,64,384]{2,1,0:T(8,128)(2,1)S(1)}, u32[]{:S(2)}, u32[]{:S(2)}) collective-permute-start(bf16[2,64,384]{2,1,0:T(8,128)(2,1)S(1)} %get-tuple-element.54), channel_id=1, source_target_pairs={{0,8},{1,9},{8,0},{9,1},{16,24},{17,25},{24,16},{25,17},{128,136},... | collective-permute-start | bytes 294920 | tf_op jit(solution)/shard_map/ppermute | solution.py:94
  38.0 3.7 %collective-permute-start.9 = (bf16[2,64,384]{2,1,0:T(8,128)(2,1)S(1)}, bf16[2,64,384]{2,1,0:T(8,128)(2,1)S(1)}, u32[]{:S(2)}, u32[]{:S(2)}) collective-permute-start(bf16[2,64,384]{2,1,0:T(8,128)(2,1)S(1)} %get-tuple-element.59), channel_id=1, source_target_pairs={{8,10},{9,11},{24,26},{25,27},{136,138},{137,139},{152,154},{153,1... | collective-permute-start | bytes 294920 | tf_op jit(solution)/shard_map/ppermute | solution.py:94
  41.7 3.3 %collective-permute-done.8.refs_3_ = bf16[2,2,4,16,384]{4,3,2,1,0:T(8,128)(2,1)S(1)} collective-permute-done((bf16[2,2,4,16,384]{4,3,2,1,0:T(8,128)(2,1)S(1)}, bf16[2,2,4,16,384]{4,3,2,1,0:T(8,128)(2,1)S(1)}, u32[]{:S(2)}, u32[]{:S(2)}) %collective-permute-start.8) | collective-permute-done | bytes 196640 | tf_op jit(solution)/shard_map/ppermute | solution.py:85
  45.1 1.1 collective-permute-start.10
  46.2 3.0 %collective-permute-start.11 = (bf16[2,160,384]{2,1,0:T(8,128)(2,1)S(1)}, bf16[2,160,384]{2,1,0:T(8,128)(2,1)S(1)}, u32[]{:S(2)}, u32[]{:S(2)}) collective-permute-start(bf16[2,160,384]{2,1,0:T(8,128)(2,1)S(1)} %get-tuple-element.61), channel_id=1, source_target_pairs={{1,32},{9,40},{17,48},{25,56},{129,160},{137,168},{145,176},{153,1... | collective-permute-start | bytes 737288 | tf_op jit(solution)/shard_map/ppermute | solution.py:94
  49.4 4.4 %collective-permute-done.11.row_out = bf16[2,160,384]{2,1,0:T(8,128)(2,1)S(1)} collective-permute-done((bf16[2,160,384]{2,1,0:T(8,128)(2,1)S(1)}, bf16[2,160,384]{2,1,0:T(8,128)(2,1)S(1)}, u32[]{:S(2)}, u32[]{:S(2)}) %collective-permute-start.11) | collective-permute-done | bytes 245792 | tf_op jit(solution)/shard_map/ppermute | solution.py:94
  53.7 9.7 %attend.1 = (bf16[2,2,4,16,384]{4,3,2,1,0:T(8,128)(2,1)S(1)}, bf16[2,2,4,16,384]{4,3,2,1,0:T(8,128)(2,1)S(1)}, bf16[2,2,4,16,384]{4,3,2,1,0:T(8,128)(2,1)S(1)}, ...) custom-call(s32[12,3]{1,0:T(8,128)S(1)} %copy.9.window, ...), custom_call_target="tpu_custom_call" | custom-call | flops 1200000000 | bytes 8388608 | tf_op jit(solution)/shard_map/attend/pallas_call | solution.py:381
  63.6 3.5 %collective-permute-start.17 = (bf16[2,160,384]{2,1,0:T(8,128)(2,1)S(1)}, bf16[2,160,384]{2,1,0:T(8,128)(2,1)S(1)}, u32[]{:S(2)}, u32[]{:S(2)}) collective-permute-start(bf16[2,160,384]{2,1,0:T(8,128)(2,1)S(1)} %get-tuple-element.74), channel_id=1, source_target_pairs={{1,32},{9,40},{17,48},{25,56},{129,160},{137,168},{145,176},{153,1... | collective-permute-start | bytes 737288 | tf_op jit(solution)/shard_map/ppermute | solution.py:94
  67.0 2.0 %collective-permute-start.12 = (bf16[2,2,4,16,384]{4,3,2,1,0:T(8,128)(2,1)S(1)}, bf16[2,2,4,16,384]{4,3,2,1,0:T(8,128)(2,1)S(1)}, u32[]{:S(2)}, u32[]{:S(2)}) collective-permute-start(bf16[2,2,4,16,384]{4,3,2,1,0:T(8,128)(2,1)S(1)} %get-tuple-element.66), channel_id=1, source_target_pairs={{128,0},{8,1},{16,8},{152,9},{129,16},{9,17},{17,24},{153,25},{0,1... | collective-permute-start | bytes 589832 | tf_op jit(solution)/shard_map/ppermute | solution.py:85
  69.0 7.5 %collective-permute-start.13 = (bf16[2,2,4,16,384]{4,3,2,1,0:T(8,128)(2,1)S(1)}, bf16[2,2,4,16,384]{4,3,2,1,0:T(8,128)(2,1)S(1)}, u32[]{:S(2)}, u32[]{:S(2)}) collective-permute-start(bf16[2,2,4,16,384]{4,3,2,1,0:T(8,128)(2,1)S(1)} %get-tuple-element.67), channel_id=1, source_target_pairs={{144,0},{24,1},{128,8},{8,9},{145,16},{153,17},{1,24},{137,25},{16... | collective-permute-start | bytes 589832 | tf_op jit(solution)/shard_map/ppermute | solution.py:85
  76.5 1.9 %collective-permute-start.14 = (bf16[2,2,4,16,384]{4,3,2,1,0:T(8,128)(2,1)S(1)}, bf16[2,2,4,16,384]{4,3,2,1,0:T(8,128)(2,1)S(1)}, u32[]{:S(2)}, u32[]{:S(2)}) collective-permute-start(bf16[2,2,4,16,384]{4,3,2,1,0:T(8,128)(2,1)S(1)} %get-tuple-element.68), channel_id=1, source_target_pairs={{0,0},{136,1},{144,8},{24,9},{1,16},{137,17},{145,24},{25,25},{128... | collective-permute-start | bytes 589832 | tf_op jit(solution)/shard_map/ppermute | solution.py:85
  78.6 3.2 %collective-permute-start.19 = (bf16[2,64,384]{2,1,0:T(8,128)(2,1)S(1)}, bf16[2,64,384]{2,1,0:T(8,128)(2,1)S(1)}, u32[]{:S(2)}, u32[]{:S(2)}) collective-permute-start(bf16[2,64,384]{2,1,0:T(8,128)(2,1)S(1)} %get-tuple-element.77), channel_id=1, source_target_pairs={{8,10},{9,11},{24,26},{25,27},{136,138},{137,139},{152,154},{153,1... | collective-permute-start | bytes 294920 | tf_op jit(solution)/shard_map/ppermute | solution.py:94
  81.8 7.4 %collective-permute-done.18.col_in = bf16[2,64,384]{2,1,0:T(8,128)(2,1)S(1)} collective-permute-done((bf16[2,64,384]{2,1,0:T(8,128)(2,1)S(1)}, bf16[2,64,384]{2,1,0:T(8,128)(2,1)S(1)}, u32[]{:S(2)}, u32[]{:S(2)}) %collective-permute-start.18) | collective-permute-done | bytes 98336 | tf_op jit(solution)/shard_map/ppermute | solution.py:94
  89.2 1.9 %collective-permute-start.15 = (bf16[2,2,4,16,384]{4,3,2,1,0:T(8,128)(2,1)S(1)}, bf16[2,2,4,16,384]{4,3,2,1,0:T(8,128)(2,1)S(1)}, u32[]{:S(2)}, u32[]{:S(2)}) collective-permute-start(bf16[2,2,4,16,384]{4,3,2,1,0:T(8,128)(2,1)S(1)} %get-tuple-element.69), channel_id=1, source_target_pairs={{16,0},{152,1},{0,8},{136,9},{17,16},{25,17},{129,24},{9,25},{144,... | collective-permute-start | bytes 589832 | tf_op jit(solution)/shard_map/ppermute | solution.py:85
  92.2 4.0 %collective-permute-start.21 = (bf16[2,2,4,16,384]{4,3,2,1,0:T(8,128)(2,1)S(1)}, bf16[2,2,4,16,384]{4,3,2,1,0:T(8,128)(2,1)S(1)}, u32[]{:S(2)}, u32[]{:S(2)}) collective-permute-start(bf16[2,2,4,16,384]{4,3,2,1,0:T(8,128)(2,1)S(1)} %get-tuple-element.79), channel_id=1, source_target_pairs={{144,0},{24,1},{128,8},{8,9},{145,16},{153,17},{1,24},{137,25},{16... | collective-permute-start | bytes 589832 | tf_op jit(solution)/shard_map/ppermute | solution.py:85
  96.2 6.2 %collective-permute-start.22 = (bf16[2,2,4,16,384]{4,3,2,1,0:T(8,128)(2,1)S(1)}, bf16[2,2,4,16,384]{4,3,2,1,0:T(8,128)(2,1)S(1)}, u32[]{:S(2)}, u32[]{:S(2)}) collective-permute-start(bf16[2,2,4,16,384]{4,3,2,1,0:T(8,128)(2,1)S(1)} %get-tuple-element.80), channel_id=1, source_target_pairs={{0,0},{136,1},{144,8},{24,9},{1,16},{137,17},{145,24},{25,25},{128... | collective-permute-start | bytes 589832 | tf_op jit(solution)/shard_map/ppermute | solution.py:85
  102.4 1.9 %collective-permute-start.23 = (bf16[2,2,4,16,384]{4,3,2,1,0:T(8,128)(2,1)S(1)}, bf16[2,2,4,16,384]{4,3,2,1,0:T(8,128)(2,1)S(1)}, u32[]{:S(2)}, u32[]{:S(2)}) collective-permute-start(bf16[2,2,4,16,384]{4,3,2,1,0:T(8,128)(2,1)S(1)} %get-tuple-element.81), channel_id=1, source_target_pairs={{16,0},{152,1},{0,8},{136,9},{17,16},{25,17},{129,24},{9,25},{144,... | collective-permute-start | bytes 589832 | tf_op jit(solution)/shard_map/ppermute | solution.py:85
  105.4 1.1 collective-permute-done.20.refs_0_
  106.4 1.5 %collective-permute-done.22.refs_2_ = bf16[2,2,4,16,384]{4,3,2,1,0:T(8,128)(2,1)S(1)} collective-permute-done((bf16[2,2,4,16,384]{4,3,2,1,0:T(8,128)(2,1)S(1)}, bf16[2,2,4,16,384]{4,3,2,1,0:T(8,128)(2,1)S(1)}, u32[]{:S(2)}, u32[]{:S(2)}) %collective-permute-start.22) | collective-permute-done | bytes 196640 | tf_op jit(solution)/shard_map/ppermute | solution.py:85
  107.9 8.4 %collective-permute-done.23.refs_3_ = bf16[2,2,4,16,384]{4,3,2,1,0:T(8,128)(2,1)S(1)} collective-permute-done((bf16[2,2,4,16,384]{4,3,2,1,0:T(8,128)(2,1)S(1)}, bf16[2,2,4,16,384]{4,3,2,1,0:T(8,128)(2,1)S(1)}, u32[]{:S(2)}, u32[]{:S(2)}) %collective-permute-start.23) | collective-permute-done | bytes 196640 | tf_op jit(solution)/shard_map/ppermute | solution.py:85
  (36 shorter events, 4.2 us)
Async XLA Ops:
  0.6 1.0 copy-start
  1.6 1.0 copy-start.1
  2.6 46.6 %copy-start.4 = (s32[12,3]{0,1:T(4,128)S(1)}, s32[12,3]{0,1:T(4,128)}, u32[]{:S(2)}) copy-start(s32[12,3]{0,1:T(4,128)} %param.9) | copy-start | bytes 436
  2.8 21.3 %collective-permute-start = (bf16[2,2,4,16,384]{4,3,2,1,0:T(8,128)(2,1)S(1)}, bf16[2,2,4,16,384]{4,3,2,1,0:T(8,128)(2,1)S(1)}, u32[]{:S(2)}, u32[]{:S(2)}) collective-permute-start(bf16[2,2,4,16,384]{4,3,2,1,0:T(8,128)(2,1)S(1)} %get-tuple-element.45), channel_id=1, source_target_pairs={{0,128},{1,8},{8,16},{9,152},{16,129},{17,9},{24,17},{25,153},{128... | collective-permute-start | bytes 589832 | tf_op jit(solution)/shard_map/ppermute | solution.py:85
  8.6 17.5 %collective-permute-start.2 = (bf16[2,2,4,16,384]{4,3,2,1,0:T(8,128)(2,1)S(1)}, bf16[2,2,4,16,384]{4,3,2,1,0:T(8,128)(2,1)S(1)}, u32[]{:S(2)}, u32[]{:S(2)}) collective-permute-start(bf16[2,2,4,16,384]{4,3,2,1,0:T(8,128)(2,1)S(1)} %get-tuple-element.50), channel_id=1, source_target_pairs={{0,144},{1,24},{8,128},{9,8},{16,145},{17,153},{24,1},{25,137},{12... | collective-permute-start | bytes 589832 | tf_op jit(solution)/shard_map/ppermute | solution.py:85
  10.5 1.0 copy-start.2
  11.5 1.0 copy-start.3
  12.7 16.8 %collective-permute-start.1 = (bf16[2,2,4,16,384]{4,3,2,1,0:T(8,128)(2,1)S(1)}, bf16[2,2,4,16,384]{4,3,2,1,0:T(8,128)(2,1)S(1)}, u32[]{:S(2)}, u32[]{:S(2)}) collective-permute-start(bf16[2,2,4,16,384]{4,3,2,1,0:T(8,128)(2,1)S(1)} %get-tuple-element.48), channel_id=1, source_target_pairs={{0,128},{1,8},{8,16},{9,152},{16,129},{17,9},{24,17},{25,153},{128... | collective-permute-start | bytes 589832 | tf_op jit(solution)/shard_map/ppermute | solution.py:85
  15.4 20.0 %collective-permute-start.3 = (bf16[2,2,4,16,384]{4,3,2,1,0:T(8,128)(2,1)S(1)}, bf16[2,2,4,16,384]{4,3,2,1,0:T(8,128)(2,1)S(1)}, u32[]{:S(2)}, u32[]{:S(2)}) collective-permute-start(bf16[2,2,4,16,384]{4,3,2,1,0:T(8,128)(2,1)S(1)} %get-tuple-element.51), channel_id=1, source_target_pairs={{0,0},{1,136},{8,144},{9,24},{16,1},{17,137},{24,145},{25,25},{128... | collective-permute-start | bytes 589832 | tf_op jit(solution)/shard_map/ppermute | solution.py:85
  17.9 17.5 %collective-permute-start.4 = (bf16[2,2,4,16,384]{4,3,2,1,0:T(8,128)(2,1)S(1)}, bf16[2,2,4,16,384]{4,3,2,1,0:T(8,128)(2,1)S(1)}, u32[]{:S(2)}, u32[]{:S(2)}) collective-permute-start(bf16[2,2,4,16,384]{4,3,2,1,0:T(8,128)(2,1)S(1)} %get-tuple-element.52), channel_id=1, source_target_pairs={{0,16},{1,152},{8,0},{9,136},{16,17},{17,25},{24,129},{25,9},{128,... | collective-permute-start | bytes 589832 | tf_op jit(solution)/shard_map/ppermute | solution.py:85
  24.1 17.6 %collective-permute-start.6 = (bf16[2,2,4,16,384]{4,3,2,1,0:T(8,128)(2,1)S(1)}, bf16[2,2,4,16,384]{4,3,2,1,0:T(8,128)(2,1)S(1)}, u32[]{:S(2)}, u32[]{:S(2)}) collective-permute-start(bf16[2,2,4,16,384]{4,3,2,1,0:T(8,128)(2,1)S(1)} %get-tuple-element.55), channel_id=1, source_target_pairs={{0,144},{1,24},{8,128},{9,8},{16,145},{17,153},{24,1},{25,137},{12... | collective-permute-start | bytes 589832 | tf_op jit(solution)/shard_map/ppermute | solution.py:85
  26.1 15.7 %collective-permute-start.7 = (bf16[2,2,4,16,384]{4,3,2,1,0:T(8,128)(2,1)S(1)}, bf16[2,2,4,16,384]{4,3,2,1,0:T(8,128)(2,1)S(1)}, u32[]{:S(2)}, u32[]{:S(2)}) collective-permute-start(bf16[2,2,4,16,384]{4,3,2,1,0:T(8,128)(2,1)S(1)} %get-tuple-element.56), channel_id=1, source_target_pairs={{0,0},{1,136},{8,144},{9,24},{16,1},{17,137},{24,145},{25,25},{128... | collective-permute-start | bytes 589832 | tf_op jit(solution)/shard_map/ppermute | solution.py:85
  29.5 15.6 %collective-permute-start.8 = (bf16[2,2,4,16,384]{4,3,2,1,0:T(8,128)(2,1)S(1)}, bf16[2,2,4,16,384]{4,3,2,1,0:T(8,128)(2,1)S(1)}, u32[]{:S(2)}, u32[]{:S(2)}) collective-permute-start(bf16[2,2,4,16,384]{4,3,2,1,0:T(8,128)(2,1)S(1)} %get-tuple-element.57), channel_id=1, source_target_pairs={{0,16},{1,152},{8,0},{9,136},{16,17},{17,25},{24,129},{25,9},{128,... | collective-permute-start | bytes 589832 | tf_op jit(solution)/shard_map/ppermute | solution.py:85
  35.9 9.2 %collective-permute-start.5 = (bf16[2,64,384]{2,1,0:T(8,128)(2,1)S(1)}, bf16[2,64,384]{2,1,0:T(8,128)(2,1)S(1)}, u32[]{:S(2)}, u32[]{:S(2)}) collective-permute-start(bf16[2,64,384]{2,1,0:T(8,128)(2,1)S(1)} %get-tuple-element.54), channel_id=1, source_target_pairs={{0,8},{1,9},{8,0},{9,1},{16,24},{17,25},{24,16},{25,17},{128,136},... | collective-permute-start | bytes 294920 | tf_op jit(solution)/shard_map/ppermute | solution.py:94
  38.0 7.1 %collective-permute-start.9 = (bf16[2,64,384]{2,1,0:T(8,128)(2,1)S(1)}, bf16[2,64,384]{2,1,0:T(8,128)(2,1)S(1)}, u32[]{:S(2)}, u32[]{:S(2)}) collective-permute-start(bf16[2,64,384]{2,1,0:T(8,128)(2,1)S(1)} %get-tuple-element.59), channel_id=1, source_target_pairs={{8,10},{9,11},{24,26},{25,27},{136,138},{137,139},{152,154},{153,1... | collective-permute-start | bytes 294920 | tf_op jit(solution)/shard_map/ppermute | solution.py:94
  45.1 4.2 %collective-permute-start.10 = (bf16[2,160,384]{2,1,0:T(8,128)(2,1)S(1)}, bf16[2,160,384]{2,1,0:T(8,128)(2,1)S(1)}, u32[]{:S(2)}, u32[]{:S(2)}) collective-permute-start(bf16[2,160,384]{2,1,0:T(8,128)(2,1)S(1)} %get-tuple-element.60), channel_id=1, source_target_pairs={{0,1},{1,0},{8,9},{9,8},{16,17},{17,16},{24,25},{25,24},{128,129},... | collective-permute-start | bytes 737288 | tf_op jit(solution)/shard_map/ppermute | solution.py:94
  46.2 7.5 %collective-permute-start.11 = (bf16[2,160,384]{2,1,0:T(8,128)(2,1)S(1)}, bf16[2,160,384]{2,1,0:T(8,128)(2,1)S(1)}, u32[]{:S(2)}, u32[]{:S(2)}) collective-permute-start(bf16[2,160,384]{2,1,0:T(8,128)(2,1)S(1)} %get-tuple-element.61), channel_id=1, source_target_pairs={{1,32},{9,40},{17,48},{25,56},{129,160},{137,168},{145,176},{153,1... | collective-permute-start | bytes 737288 | tf_op jit(solution)/shard_map/ppermute | solution.py:94
  63.4 15.0 %collective-permute-start.16 = (bf16[2,160,384]{2,1,0:T(8,128)(2,1)S(1)}, bf16[2,160,384]{2,1,0:T(8,128)(2,1)S(1)}, u32[]{:S(2)}, u32[]{:S(2)}) collective-permute-start(bf16[2,160,384]{2,1,0:T(8,128)(2,1)S(1)} %get-tuple-element.73), channel_id=1, source_target_pairs={{0,1},{1,0},{8,9},{9,8},{16,17},{17,16},{24,25},{25,24},{128,129},... | collective-permute-start | bytes 737288 | tf_op jit(solution)/shard_map/ppermute | solution.py:94
  63.6 14.9 %collective-permute-start.17 = (bf16[2,160,384]{2,1,0:T(8,128)(2,1)S(1)}, bf16[2,160,384]{2,1,0:T(8,128)(2,1)S(1)}, u32[]{:S(2)}, u32[]{:S(2)}) collective-permute-start(bf16[2,160,384]{2,1,0:T(8,128)(2,1)S(1)} %get-tuple-element.74), channel_id=1, source_target_pairs={{1,32},{9,40},{17,48},{25,56},{129,160},{137,168},{145,176},{153,1... | collective-permute-start | bytes 737288 | tf_op jit(solution)/shard_map/ppermute | solution.py:94
  67.0 25.1 %collective-permute-start.12 = (bf16[2,2,4,16,384]{4,3,2,1,0:T(8,128)(2,1)S(1)}, bf16[2,2,4,16,384]{4,3,2,1,0:T(8,128)(2,1)S(1)}, u32[]{:S(2)}, u32[]{:S(2)}) collective-permute-start(bf16[2,2,4,16,384]{4,3,2,1,0:T(8,128)(2,1)S(1)} %get-tuple-element.66), channel_id=1, source_target_pairs={{128,0},{8,1},{16,8},{152,9},{129,16},{9,17},{17,24},{153,25},{0,1... | collective-permute-start | bytes 589832 | tf_op jit(solution)/shard_map/ppermute | solution.py:85
  69.0 27.2 %collective-permute-start.13 = (bf16[2,2,4,16,384]{4,3,2,1,0:T(8,128)(2,1)S(1)}, bf16[2,2,4,16,384]{4,3,2,1,0:T(8,128)(2,1)S(1)}, u32[]{:S(2)}, u32[]{:S(2)}) collective-permute-start(bf16[2,2,4,16,384]{4,3,2,1,0:T(8,128)(2,1)S(1)} %get-tuple-element.67), channel_id=1, source_target_pairs={{144,0},{24,1},{128,8},{8,9},{145,16},{153,17},{1,24},{137,25},{16... | collective-permute-start | bytes 589832 | tf_op jit(solution)/shard_map/ppermute | solution.py:85
  76.5 26.0 %collective-permute-start.14 = (bf16[2,2,4,16,384]{4,3,2,1,0:T(8,128)(2,1)S(1)}, bf16[2,2,4,16,384]{4,3,2,1,0:T(8,128)(2,1)S(1)}, u32[]{:S(2)}, u32[]{:S(2)}) collective-permute-start(bf16[2,2,4,16,384]{4,3,2,1,0:T(8,128)(2,1)S(1)} %get-tuple-element.68), channel_id=1, source_target_pairs={{0,0},{136,1},{144,8},{24,9},{1,16},{137,17},{145,24},{25,25},{128... | collective-permute-start | bytes 589832 | tf_op jit(solution)/shard_map/ppermute | solution.py:85
  78.5 10.8 %collective-permute-start.18 = (bf16[2,64,384]{2,1,0:T(8,128)(2,1)S(1)}, bf16[2,64,384]{2,1,0:T(8,128)(2,1)S(1)}, u32[]{:S(2)}, u32[]{:S(2)}) collective-permute-start(bf16[2,64,384]{2,1,0:T(8,128)(2,1)S(1)} %get-tuple-element.76), channel_id=1, source_target_pairs={{0,8},{1,9},{8,0},{9,1},{16,24},{17,25},{24,16},{25,17},{128,136},... | collective-permute-start | bytes 294920 | tf_op jit(solution)/shard_map/ppermute | solution.py:94
  78.6 12.6 %collective-permute-start.19 = (bf16[2,64,384]{2,1,0:T(8,128)(2,1)S(1)}, bf16[2,64,384]{2,1,0:T(8,128)(2,1)S(1)}, u32[]{:S(2)}, u32[]{:S(2)}) collective-permute-start(bf16[2,64,384]{2,1,0:T(8,128)(2,1)S(1)} %get-tuple-element.77), channel_id=1, source_target_pairs={{8,10},{9,11},{24,26},{25,27},{136,138},{137,139},{152,154},{153,1... | collective-permute-start | bytes 294920 | tf_op jit(solution)/shard_map/ppermute | solution.py:94
  89.2 15.1 %collective-permute-start.15 = (bf16[2,2,4,16,384]{4,3,2,1,0:T(8,128)(2,1)S(1)}, bf16[2,2,4,16,384]{4,3,2,1,0:T(8,128)(2,1)S(1)}, u32[]{:S(2)}, u32[]{:S(2)}) collective-permute-start(bf16[2,2,4,16,384]{4,3,2,1,0:T(8,128)(2,1)S(1)} %get-tuple-element.69), channel_id=1, source_target_pairs={{16,0},{152,1},{0,8},{136,9},{17,16},{25,17},{129,24},{9,25},{144,... | collective-permute-start | bytes 589832 | tf_op jit(solution)/shard_map/ppermute | solution.py:85
  91.9 14.6 %collective-permute-start.20 = (bf16[2,2,4,16,384]{4,3,2,1,0:T(8,128)(2,1)S(1)}, bf16[2,2,4,16,384]{4,3,2,1,0:T(8,128)(2,1)S(1)}, u32[]{:S(2)}, u32[]{:S(2)}) collective-permute-start(bf16[2,2,4,16,384]{4,3,2,1,0:T(8,128)(2,1)S(1)} %get-tuple-element.78), channel_id=1, source_target_pairs={{128,0},{8,1},{16,8},{152,9},{129,16},{9,17},{17,24},{153,25},{0,1... | collective-permute-start | bytes 589832 | tf_op jit(solution)/shard_map/ppermute | solution.py:85
  92.2 14.3 %collective-permute-start.21 = (bf16[2,2,4,16,384]{4,3,2,1,0:T(8,128)(2,1)S(1)}, bf16[2,2,4,16,384]{4,3,2,1,0:T(8,128)(2,1)S(1)}, u32[]{:S(2)}, u32[]{:S(2)}) collective-permute-start(bf16[2,2,4,16,384]{4,3,2,1,0:T(8,128)(2,1)S(1)} %get-tuple-element.79), channel_id=1, source_target_pairs={{144,0},{24,1},{128,8},{8,9},{145,16},{153,17},{1,24},{137,25},{16... | collective-permute-start | bytes 589832 | tf_op jit(solution)/shard_map/ppermute | solution.py:85
  96.2 11.7 %collective-permute-start.22 = (bf16[2,2,4,16,384]{4,3,2,1,0:T(8,128)(2,1)S(1)}, bf16[2,2,4,16,384]{4,3,2,1,0:T(8,128)(2,1)S(1)}, u32[]{:S(2)}, u32[]{:S(2)}) collective-permute-start(bf16[2,2,4,16,384]{4,3,2,1,0:T(8,128)(2,1)S(1)} %get-tuple-element.80), channel_id=1, source_target_pairs={{0,0},{136,1},{144,8},{24,9},{1,16},{137,17},{145,24},{25,25},{128... | collective-permute-start | bytes 589832 | tf_op jit(solution)/shard_map/ppermute | solution.py:85
  102.4 13.8 %collective-permute-start.23 = (bf16[2,2,4,16,384]{4,3,2,1,0:T(8,128)(2,1)S(1)}, bf16[2,2,4,16,384]{4,3,2,1,0:T(8,128)(2,1)S(1)}, u32[]{:S(2)}, u32[]{:S(2)}) collective-permute-start(bf16[2,2,4,16,384]{4,3,2,1,0:T(8,128)(2,1)S(1)} %get-tuple-element.81), channel_id=1, source_target_pairs={{16,0},{152,1},{0,8},{136,9},{17,16},{25,17},{129,24},{9,25},{144,... | collective-permute-start | bytes 589832 | tf_op jit(solution)/shard_map/ppermute | solution.py:85

commit v3 on v2

--- a/solution.py
+++ b/solution.py
@@ -259,6 +259,15 @@
 TN = (((0,), (0,)), ((), ()))
 
 
+def row_sums(x):
+    high = x.astype(BF)
+    low = (x - high.astype(F32)).astype(BF)
+    ones = jnp.ones((16, HEAD), BF)
+    sums = lax.dot_general(ones, high, NT, preferred_element_type=F32)
+    sums += lax.dot_general(ones, low, NT, preferred_element_type=F32)
+    return sums[0:1]
+
+
 def attend_body(window, own, col_in, col_out, row_in, row_out, *refs):
     qd = refs[:GROUPS]
     back = refs[GROUPS : 2 * GROUPS]
@@ -281,15 +290,15 @@
                 kv_side[slot, i, at_16(below * 80)] = buf[i, 128 + 16 * slot : 144 + 16 * slot]
         gather_blocks(qd, i, q_all)
 
-    qi = lax.broadcasted_iota(jnp.int32, (128, 1), 0)
+    qi = lax.broadcasted_iota(jnp.int32, (1, 128), 1)
     q_t, q_w = qi // 32 % 2, qi % 16 // 2
-    ki = lax.broadcasted_iota(jnp.int32, (1, 480), 1)
-    mid = ki < 384
-    ks = jnp.where(ki < 432, ki - 384, ki - 432)
+    ki = lax.broadcasted_iota(jnp.int32, (160, 1), 0)
+    mid = ki < 128
+    ks = jnp.where(ki < 144, ki - 128, ki - 144)
     k_t = jnp.where(mid, ki // 32 % 2, ks // 4 % 2)
-    k_w = jnp.where(mid, ki % 16 // 2, jnp.where(ki < 432, -1, 8))
-    k_h = jnp.where(mid, ki // 128, ks // 16)
+    k_w = jnp.where(mid, ki % 16 // 2, jnp.where(ki < 144, -1, 8))
     beside = ((k_w >= 0) | (w_at > 0)) & ((k_w < 8) | (w_at < w_last))
+    t_far, w_far = jnp.abs(q_t - k_t), jnp.where(beside, jnp.abs(q_w - k_w), 99)
     tile_row = (x * 2 + half) * 4 - 1
     tile_rows = 4 * 8
 
@@ -297,14 +306,19 @@
         f = slice(n * HEAD, (n + 1) * HEAD)
         head = group * GH + n
         rad_t, rad_h, rad_w = window[head, 0], window[head, 1], window[head, 2]
-        near = (jnp.abs(q_t - k_t) <= rad_t) & (jnp.abs(q_w - k_w) <= rad_w)
-        base = jnp.where(near, 0.0, NEG)
-        inside = beside & (jnp.abs(k_h - 1) <= rad_h)
-        all_w, all_ds = [], []
+        base = jnp.where((t_far <= rad_t) & (w_far <= rad_w), 0.0, NEG)
+        all_w, all_ds, held = [], [], []
         side_g = [[[None] * 6, [None] * 6], [[None] * 6, [None] * 6]]
         for blk in range(4):
-            row = tile_row + blk + k_h
-            row_bias = jnp.where(inside & (row >= 0) & (row < tile_rows), 0.0, NEG)
+            biases = []
+            for j in range(3):
+                row = tile_row + blk + j
+                seen = (row >= 0) & (row < tile_rows) & (abs(j - 1) <= rad_h)
+                biases.append(base + jnp.where(seen, 0.0, NEG))
+            bias = jnp.concatenate(
+                [biases[j][lo:hi] for lo, hi in ((0, 128), (128, 144), (144, 160)) for j in range(3)],
+                axis=0,
+            )
             mid_at, side_at, q_at = pl.ds(128 * blk, 384), pl.ds(16 * blk, 48), pl.ds(128 * blk, 128)
             k, v = (
                 jnp.concatenate(
@@ -313,23 +327,27 @@
                 for i in range(2)
             )
             q, do = q_all[0, q_at, f], q_all[1, q_at, f]
-            s = lax.dot_general(q, k, NT, preferred_element_type=F32)
-            s = s * (scale * log2e) + (base + row_bias)
-            top = jnp.max(s, axis=1, keepdims=True)
-            e = jnp.exp2(s - top)
-            p = e * (1.0 / jnp.sum(e, axis=1, keepdims=True))
+            s = lax.dot_general(k, q, NT, preferred_element_type=F32)
+            dp = lax.dot_general(v, do, NT, preferred_element_type=F32)
+            held.append((k, v, q, do, s, dp, bias))
+        soft = []
+        for blk, (k, v, q, do, s, dp, bias) in enumerate(held):
+            s = s * (scale * log2e) + bias
+            e = jnp.exp2(s - jnp.max(s, axis=0, keepdims=True))
+            p = e * (1.0 / jnp.sum(e, axis=0, keepdims=True))
             wts = p.astype(BF)
-            o = jnp.dot(wts, v, preferred_element_type=F32).astype(BF)
-            delta = jnp.sum(do.astype(F32) * o.astype(F32), axis=1, keepdims=True)
-            dp = lax.dot_general(do, v, NT, preferred_element_type=F32)
+            o = lax.dot_general(wts, v, TN, preferred_element_type=F32).astype(BF)
+            o_all[0, pl.ds(128 * blk, 128), f] = o
+            soft.append((p, wts, row_sums(do.astype(F32) * o.astype(F32))))
+        for blk, (k, v, q, do, s, dp, bias) in enumerate(held):
+            p, wts, delta = soft[blk]
             ds = (p * (dp - delta)).astype(BF)
-            dq = jnp.dot(ds, k, preferred_element_type=F32) * scale
-            o_all[0, q_at, f] = o
-            o_all[1, q_at, f] = dq.astype(BF)
+            dq = lax.dot_general(ds, k, TN, preferred_element_type=F32) * scale
+            o_all[1, pl.ds(128 * blk, 128), f] = dq.astype(BF)
             all_ds.append(ds)
             all_w.append(wts)
             for i, (a, b) in enumerate(((ds, q), (wts, do))):
-                part = lax.dot_general(a[:, 384:480], b, TN, preferred_element_type=F32)
+                part = jnp.dot(a[384:480], b, preferred_element_type=F32)
                 for lr in range(2):
                     for o_ in range(3):
                         piece = part[48 * lr + 16 * o_ : 48 * lr + 16 * o_ + 16]
@@ -339,11 +357,11 @@
             mul = scale if i == 0 else 1.0
             for j in range(6):
                 blks = [b for b in range(4) if 0 <= j - b <= 2]
-                lhs = [a[b][:, 128 * (j - b) : 128 * (j - b) + 128] for b in blks]
-                lhs = lhs[0] if len(lhs) == 1 else jnp.concatenate(lhs, axis=0)
+                lhs = [a[b][128 * (j - b) : 128 * (j - b) + 128] for b in blks]
+                lhs = lhs[0] if len(lhs) == 1 else jnp.concatenate(lhs, axis=1)
                 rhs = q_all[i, pl.ds(128 * blks[0], 128 * len(blks)), f]
                 g_mid[i, 128 * j : 128 * j + 128, f] = (
-                    lax.dot_general(lhs, rhs, TN, preferred_element_type=F32) * mul
+                    jnp.dot(lhs, rhs, preferred_element_type=F32) * mul
                 )
                 for slot in range(2):
                     g_side[slot, i, 16 * j : 16 * j + 16, f] = side_g[i][slot][j] * mul
@@ -427,10 +445,14 @@
 
 
 def local(queries, keys, values, out_grad, head_window):
+    queries, keys, values, out_grad = (
+        pltpu.with_memory_space_constraint(v, pltpu.HBM) for v in (queries, keys, values, out_grad)
+    )
     sent = list(pack(keys, values, "pack_kv"))
     sent, (queries, out_grad) = ordered(sent, (queries, out_grad))
     kv = deal(sent, False)
-    qd = deal(pack(queries, out_grad, "pack_qd"), False)
+    ask = list(pack(queries, out_grad, "pack_qd"))
+    qd = deal(ask, False)
     kv, qd[:1] = ordered(kv, qd[:1])
     own, *edges = own_kv(kv)
     cols = cols_swap(*edges)

time: 119 us -> 113 us (0.950)
  local copies, waits for them, and re-layouts: 4.07 us -> 0.1 us
  Pallas kernels: 13.2 us -> 11.2 us
    pallas_call x1, Pallas kernels: 9.71 us -> 5.35 us  [attend(): call(attend_body, outs, scratch, in_specs=[pl.BlockSpec(memory_space=pltp...]
    unnamed x11 -> x3, local copies, waits for them, and re-layouts: 4.07 us -> 0.1 us
    pallas_call x2, Pallas kernels: 0.35 us -> 2.65 us  [pack(): call(pack_body, [shaped(*DEALT)] * GROUPS, [pltpu.SemaphoreType.DMA((2 *...]
    ppermute x8, starting transfers between devices: 16.9 us -> 18.4 us  [swap(): return lax.ppermute(buf, ALL, pairs)]
  transfers between devices with their start and end apart: 24 -> 24, of which waited for: 6 -> 5; matrix products, arithmetic and copies ran while one was open for 0% -> 0% of each run, Pallas kernels for 2% -> 3%
where the time goes in v3:
time: 113 us; the launch traced here: 112 us
  starting transfers between devices  73.3 us (65%)
  waiting for transfers between devices  26 us (23%)
  Pallas kernels  11.2 us (10%)
    ppermute x16, starting transfers between devices, deal(): lax.ppermute(b, ALL, deal_pairs(r, back))  55 us
    ppermute x8, starting transfers between devices, swap(): return lax.ppermute(buf, ALL, pairs)  18.4 us
    ppermute x16, waiting for transfers between devices, deal(): lax.ppermute(b, ALL, deal_pairs(r, back))  14.3 us
    ppermute x8, waiting for transfers between devices, swap(): return lax.ppermute(buf, ALL, pairs)  11.7 us
    pallas_call x1, Pallas kernels, attend(): call(attend_body, outs, scratch, in_specs=[pl.BlockSpec(memory_space=pltp...  5.35 us
    pallas_call x2, Pallas kernels, pack(): call(pack_body, [shaped(*DEALT)] * GROUPS, [pltpu.SemaphoreType.DMA((2 *...  2.65 us
  transfers between devices with their start and end apart: 24, of which 5 were waited for; matrix products, arithmetic and copies ran while one was open for 0% of the time, Pallas kernels for 3%

profile of v3, /device:TPU:51, one launch (start us, length us, event | category | flops | bytes accessed | tf_op | source)
XLA Modules:
  0.0 111.5 jit_solution(17051100069811165881)
XLA Ops:
  0.6 1.3 %pack_kv.1 = (bf16[2,2,4,16,384]{4,3,2,1,0:T(8,128)(2,1)S(1)}, bf16[2,2,4,16,384]{4,3,2,1,0:T(8,128)(2,1)S(1)}, bf16[2,2,4,16,384]{4,3,2,1,0:T(8,128)(2,1)S(1)}, bf16[2,2,4,16,384]{4,3,2,1,0:T(8,128)(2,1)S(1)}) custom-call(bf16[2,4,16,1536]{3,2,1,0:T(8,128)(2,1)} %refs_0_.1, bf16[2,4,16,1536]{3,2,1,0:T(8,128)(2,1)} %refs_1_.1), custom_call_target="tpu_custom_call" | custom-call | bytes 3145728 | tf_op jit(solution)/shard_map/pack_kv/pallas_call | solution.py:162
  2.0 5.8 %collective-permute-start = (bf16[2,2,4,16,384]{4,3,2,1,0:T(8,128)(2,1)S(1)}, bf16[2,2,4,16,384]{4,3,2,1,0:T(8,128)(2,1)S(1)}, u32[]{:S(2)}, u32[]{:S(2)}) collective-permute-start(bf16[2,2,4,16,384]{4,3,2,1,0:T(8,128)(2,1)S(1)} %get-tuple-element.45), channel_id=1, source_target_pairs={{0,128},{1,8},{8,16},{9,152},{16,129},{17,9},{24,17},{25,153},{128... | collective-permute-start | bytes 589832 | tf_op jit(solution)/shard_map/ppermute | solution.py:85
  7.7 1.9 %collective-permute-start.2 = (bf16[2,2,4,16,384]{4,3,2,1,0:T(8,128)(2,1)S(1)}, bf16[2,2,4,16,384]{4,3,2,1,0:T(8,128)(2,1)S(1)}, u32[]{:S(2)}, u32[]{:S(2)}) collective-permute-start(bf16[2,2,4,16,384]{4,3,2,1,0:T(8,128)(2,1)S(1)} %get-tuple-element.50), channel_id=1, source_target_pairs={{0,144},{1,24},{8,128},{9,8},{16,145},{17,153},{24,1},{25,137},{12... | collective-permute-start | bytes 589832 | tf_op jit(solution)/shard_map/ppermute | solution.py:85
  9.7 1.3 %pack_qd.1 = (bf16[2,2,4,16,384]{4,3,2,1,0:T(8,128)(2,1)S(1)}, bf16[2,2,4,16,384]{4,3,2,1,0:T(8,128)(2,1)S(1)}, bf16[2,2,4,16,384]{4,3,2,1,0:T(8,128)(2,1)S(1)}, bf16[2,2,4,16,384]{4,3,2,1,0:T(8,128)(2,1)S(1)}) custom-call(bf16[2,4,16,1536]{3,2,1,0:T(8,128)(2,1)} %refs_0_.2, bf16[2,4,16,1536]{3,2,1,0:T(8,128)(2,1)} %refs_1_.2), custom_call_target="tpu_custom_call" | custom-call | bytes 3145728 | tf_op jit(solution)/shard_map/pack_qd/pallas_call | solution.py:162
  11.0 2.7 %collective-permute-start.1 = (bf16[2,2,4,16,384]{4,3,2,1,0:T(8,128)(2,1)S(1)}, bf16[2,2,4,16,384]{4,3,2,1,0:T(8,128)(2,1)S(1)}, u32[]{:S(2)}, u32[]{:S(2)}) collective-permute-start(bf16[2,2,4,16,384]{4,3,2,1,0:T(8,128)(2,1)S(1)} %get-tuple-element.48), channel_id=1, source_target_pairs={{0,128},{1,8},{8,16},{9,152},{16,129},{17,9},{24,17},{25,153},{128... | collective-permute-start | bytes 589832 | tf_op jit(solution)/shard_map/ppermute | solution.py:85
  13.7 2.5 %collective-permute-start.3 = (bf16[2,2,4,16,384]{4,3,2,1,0:T(8,128)(2,1)S(1)}, bf16[2,2,4,16,384]{4,3,2,1,0:T(8,128)(2,1)S(1)}, u32[]{:S(2)}, u32[]{:S(2)}) collective-permute-start(bf16[2,2,4,16,384]{4,3,2,1,0:T(8,128)(2,1)S(1)} %get-tuple-element.51), channel_id=1, source_target_pairs={{0,0},{1,136},{8,144},{9,24},{16,1},{17,137},{24,145},{25,25},{128... | collective-permute-start | bytes 589832 | tf_op jit(solution)/shard_map/ppermute | solution.py:85
  16.2 6.2 %collective-permute-start.4 = (bf16[2,2,4,16,384]{4,3,2,1,0:T(8,128)(2,1)S(1)}, bf16[2,2,4,16,384]{4,3,2,1,0:T(8,128)(2,1)S(1)}, u32[]{:S(2)}, u32[]{:S(2)}) collective-permute-start(bf16[2,2,4,16,384]{4,3,2,1,0:T(8,128)(2,1)S(1)} %get-tuple-element.52), channel_id=1, source_target_pairs={{0,16},{1,152},{8,0},{9,136},{16,17},{17,25},{24,129},{25,9},{128,... | collective-permute-start | bytes 589832 | tf_op jit(solution)/shard_map/ppermute | solution.py:85
  22.5 1.9 %collective-permute-start.6 = (bf16[2,2,4,16,384]{4,3,2,1,0:T(8,128)(2,1)S(1)}, bf16[2,2,4,16,384]{4,3,2,1,0:T(8,128)(2,1)S(1)}, u32[]{:S(2)}, u32[]{:S(2)}) collective-permute-start(bf16[2,2,4,16,384]{4,3,2,1,0:T(8,128)(2,1)S(1)} %get-tuple-element.55), channel_id=1, source_target_pairs={{0,144},{1,24},{8,128},{9,8},{16,145},{17,153},{24,1},{25,137},{12... | collective-permute-start | bytes 589832 | tf_op jit(solution)/shard_map/ppermute | solution.py:85
  24.4 3.4 %collective-permute-start.7 = (bf16[2,2,4,16,384]{4,3,2,1,0:T(8,128)(2,1)S(1)}, bf16[2,2,4,16,384]{4,3,2,1,0:T(8,128)(2,1)S(1)}, u32[]{:S(2)}, u32[]{:S(2)}) collective-permute-start(bf16[2,2,4,16,384]{4,3,2,1,0:T(8,128)(2,1)S(1)} %get-tuple-element.56), channel_id=1, source_target_pairs={{0,0},{1,136},{8,144},{9,24},{16,1},{17,137},{24,145},{25,25},{128... | collective-permute-start | bytes 589832 | tf_op jit(solution)/shard_map/ppermute | solution.py:85
  27.8 5.9 %collective-permute-start.8 = (bf16[2,2,4,16,384]{4,3,2,1,0:T(8,128)(2,1)S(1)}, bf16[2,2,4,16,384]{4,3,2,1,0:T(8,128)(2,1)S(1)}, u32[]{:S(2)}, u32[]{:S(2)}) collective-permute-start(bf16[2,2,4,16,384]{4,3,2,1,0:T(8,128)(2,1)S(1)} %get-tuple-element.57), channel_id=1, source_target_pairs={{0,16},{1,152},{8,0},{9,136},{16,17},{17,25},{24,129},{25,9},{128,... | collective-permute-start | bytes 589832 | tf_op jit(solution)/shard_map/ppermute | solution.py:85
  34.2 3.1 %collective-permute-start.5 = (bf16[2,64,384]{2,1,0:T(8,128)(2,1)S(1)}, bf16[2,64,384]{2,1,0:T(8,128)(2,1)S(1)}, u32[]{:S(2)}, u32[]{:S(2)}) collective-permute-start(bf16[2,64,384]{2,1,0:T(8,128)(2,1)S(1)} %get-tuple-element.54), channel_id=1, source_target_pairs={{0,8},{1,9},{8,0},{9,1},{16,24},{17,25},{24,16},{25,17},{128,136},... | collective-permute-start | bytes 294920 | tf_op jit(solution)/shard_map/ppermute | solution.py:94
  37.3 2.4 %collective-permute-start.9 = (bf16[2,64,384]{2,1,0:T(8,128)(2,1)S(1)}, bf16[2,64,384]{2,1,0:T(8,128)(2,1)S(1)}, u32[]{:S(2)}, u32[]{:S(2)}) collective-permute-start(bf16[2,64,384]{2,1,0:T(8,128)(2,1)S(1)} %get-tuple-element.59), channel_id=1, source_target_pairs={{8,10},{9,11},{24,26},{25,27},{136,138},{137,139},{152,154},{153,1... | collective-permute-start | bytes 294920 | tf_op jit(solution)/shard_map/ppermute | solution.py:94
  39.7 4.0 %collective-permute-done.8.refs_3_ = bf16[2,2,4,16,384]{4,3,2,1,0:T(8,128)(2,1)S(1)} collective-permute-done((bf16[2,2,4,16,384]{4,3,2,1,0:T(8,128)(2,1)S(1)}, bf16[2,2,4,16,384]{4,3,2,1,0:T(8,128)(2,1)S(1)}, u32[]{:S(2)}, u32[]{:S(2)}) %collective-permute-start.8) | collective-permute-done | bytes 196640 | tf_op jit(solution)/shard_map/ppermute | solution.py:85
  43.7 0.9 collective-permute-start.10
  44.6 3.0 %collective-permute-start.11 = (bf16[2,160,384]{2,1,0:T(8,128)(2,1)S(1)}, bf16[2,160,384]{2,1,0:T(8,128)(2,1)S(1)}, u32[]{:S(2)}, u32[]{:S(2)}) collective-permute-start(bf16[2,160,384]{2,1,0:T(8,128)(2,1)S(1)} %get-tuple-element.61), channel_id=1, source_target_pairs={{1,32},{9,40},{17,48},{25,56},{129,160},{137,168},{145,176},{153,1... | collective-permute-start | bytes 737288 | tf_op jit(solution)/shard_map/ppermute | solution.py:94
  47.7 4.4 %collective-permute-done.11.row_out = bf16[2,160,384]{2,1,0:T(8,128)(2,1)S(1)} collective-permute-done((bf16[2,160,384]{2,1,0:T(8,128)(2,1)S(1)}, bf16[2,160,384]{2,1,0:T(8,128)(2,1)S(1)}, u32[]{:S(2)}, u32[]{:S(2)}) %collective-permute-start.11) | collective-permute-done | bytes 245792 | tf_op jit(solution)/shard_map/ppermute | solution.py:94
  52.1 5.4 %attend.1 = (bf16[2,2,4,16,384]{4,3,2,1,0:T(8,128)(2,1)S(1)}, bf16[2,2,4,16,384]{4,3,2,1,0:T(8,128)(2,1)S(1)}, bf16[2,2,4,16,384]{4,3,2,1,0:T(8,128)(2,1)S(1)}, ...) custom-call(s32[12,3]{1,0:T(8,128)S(1)} %copy.9.window, ...), custom_call_target="tpu_custom_call" | custom-call | flops 1200000000 | bytes 8388608 | tf_op jit(solution)/shard_map/attend/pallas_call | solution.py:399
  57.6 3.5 %collective-permute-start.17 = (bf16[2,160,384]{2,1,0:T(8,128)(2,1)S(1)}, bf16[2,160,384]{2,1,0:T(8,128)(2,1)S(1)}, u32[]{:S(2)}, u32[]{:S(2)}) collective-permute-start(bf16[2,160,384]{2,1,0:T(8,128)(2,1)S(1)} %get-tuple-element.74), channel_id=1, source_target_pairs={{1,32},{9,40},{17,48},{25,56},{129,160},{137,168},{145,176},{153,1... | collective-permute-start | bytes 737288 | tf_op jit(solution)/shard_map/ppermute | solution.py:94
  61.1 1.0 collective-permute-start.12
  62.1 6.4 %collective-permute-start.13 = (bf16[2,2,4,16,384]{4,3,2,1,0:T(8,128)(2,1)S(1)}, bf16[2,2,4,16,384]{4,3,2,1,0:T(8,128)(2,1)S(1)}, u32[]{:S(2)}, u32[]{:S(2)}) collective-permute-start(bf16[2,2,4,16,384]{4,3,2,1,0:T(8,128)(2,1)S(1)} %get-tuple-element.67), channel_id=1, source_target_pairs={{144,0},{24,1},{128,8},{8,9},{145,16},{153,17},{1,24},{137,25},{16... | collective-permute-start | bytes 589832 | tf_op jit(solution)/shard_map/ppermute | solution.py:85
  68.4 1.9 %collective-permute-start.14 = (bf16[2,2,4,16,384]{4,3,2,1,0:T(8,128)(2,1)S(1)}, bf16[2,2,4,16,384]{4,3,2,1,0:T(8,128)(2,1)S(1)}, u32[]{:S(2)}, u32[]{:S(2)}) collective-permute-start(bf16[2,2,4,16,384]{4,3,2,1,0:T(8,128)(2,1)S(1)} %get-tuple-element.68), channel_id=1, source_target_pairs={{0,0},{136,1},{144,8},{24,9},{1,16},{137,17},{145,24},{25,25},{128... | collective-permute-start | bytes 589832 | tf_op jit(solution)/shard_map/ppermute | solution.py:85
  70.4 2.1 %collective-permute-start.18 = (bf16[2,64,384]{2,1,0:T(8,128)(2,1)S(1)}, bf16[2,64,384]{2,1,0:T(8,128)(2,1)S(1)}, u32[]{:S(2)}, u32[]{:S(2)}) collective-permute-start(bf16[2,64,384]{2,1,0:T(8,128)(2,1)S(1)} %get-tuple-element.76), channel_id=1, source_target_pairs={{0,8},{1,9},{8,0},{9,1},{16,24},{17,25},{24,16},{25,17},{128,136},... | collective-permute-start | bytes 294920 | tf_op jit(solution)/shard_map/ppermute | solution.py:94
  72.5 3.3 %collective-permute-start.19 = (bf16[2,64,384]{2,1,0:T(8,128)(2,1)S(1)}, bf16[2,64,384]{2,1,0:T(8,128)(2,1)S(1)}, u32[]{:S(2)}, u32[]{:S(2)}) collective-permute-start(bf16[2,64,384]{2,1,0:T(8,128)(2,1)S(1)} %get-tuple-element.77), channel_id=1, source_target_pairs={{8,10},{9,11},{24,26},{25,27},{136,138},{137,139},{152,154},{153,1... | collective-permute-start | bytes 294920 | tf_op jit(solution)/shard_map/ppermute | solution.py:94
  75.9 7.3 %collective-permute-done.18.col_in = bf16[2,64,384]{2,1,0:T(8,128)(2,1)S(1)} collective-permute-done((bf16[2,64,384]{2,1,0:T(8,128)(2,1)S(1)}, bf16[2,64,384]{2,1,0:T(8,128)(2,1)S(1)}, u32[]{:S(2)}, u32[]{:S(2)}) %collective-permute-start.18) | collective-permute-done | bytes 98336 | tf_op jit(solution)/shard_map/ppermute | solution.py:94
  83.1 1.9 %collective-permute-start.15 = (bf16[2,2,4,16,384]{4,3,2,1,0:T(8,128)(2,1)S(1)}, bf16[2,2,4,16,384]{4,3,2,1,0:T(8,128)(2,1)S(1)}, u32[]{:S(2)}, u32[]{:S(2)}) collective-permute-start(bf16[2,2,4,16,384]{4,3,2,1,0:T(8,128)(2,1)S(1)} %get-tuple-element.69), channel_id=1, source_target_pairs={{16,0},{152,1},{0,8},{136,9},{17,16},{25,17},{129,24},{9,25},{144,... | collective-permute-start | bytes 589832 | tf_op jit(solution)/shard_map/ppermute | solution.py:85
  86.4 4.0 %collective-permute-start.21 = (bf16[2,2,4,16,384]{4,3,2,1,0:T(8,128)(2,1)S(1)}, bf16[2,2,4,16,384]{4,3,2,1,0:T(8,128)(2,1)S(1)}, u32[]{:S(2)}, u32[]{:S(2)}) collective-permute-start(bf16[2,2,4,16,384]{4,3,2,1,0:T(8,128)(2,1)S(1)} %get-tuple-element.79), channel_id=1, source_target_pairs={{144,0},{24,1},{128,8},{8,9},{145,16},{153,17},{1,24},{137,25},{16... | collective-permute-start | bytes 589832 | tf_op jit(solution)/shard_map/ppermute | solution.py:85
  90.4 6.9 %collective-permute-start.22 = (bf16[2,2,4,16,384]{4,3,2,1,0:T(8,128)(2,1)S(1)}, bf16[2,2,4,16,384]{4,3,2,1,0:T(8,128)(2,1)S(1)}, u32[]{:S(2)}, u32[]{:S(2)}) collective-permute-start(bf16[2,2,4,16,384]{4,3,2,1,0:T(8,128)(2,1)S(1)} %get-tuple-element.80), channel_id=1, source_target_pairs={{0,0},{136,1},{144,8},{24,9},{1,16},{137,17},{145,24},{25,25},{128... | collective-permute-start | bytes 589832 | tf_op jit(solution)/shard_map/ppermute | solution.py:85
  97.3 1.9 %collective-permute-start.23 = (bf16[2,2,4,16,384]{4,3,2,1,0:T(8,128)(2,1)S(1)}, bf16[2,2,4,16,384]{4,3,2,1,0:T(8,128)(2,1)S(1)}, u32[]{:S(2)}, u32[]{:S(2)}) collective-permute-start(bf16[2,2,4,16,384]{4,3,2,1,0:T(8,128)(2,1)S(1)} %get-tuple-element.81), channel_id=1, source_target_pairs={{16,0},{152,1},{0,8},{136,9},{17,16},{25,17},{129,24},{9,25},{144,... | collective-permute-start | bytes 589832 | tf_op jit(solution)/shard_map/ppermute | solution.py:85
  99.3 1.0 unpack_oq.1
  100.3 0.9 collective-permute-done.22.refs_2_
  101.1 9.4 %collective-permute-done.23.refs_3_ = bf16[2,2,4,16,384]{4,3,2,1,0:T(8,128)(2,1)S(1)} collective-permute-done((bf16[2,2,4,16,384]{4,3,2,1,0:T(8,128)(2,1)S(1)}, bf16[2,2,4,16,384]{4,3,2,1,0:T(8,128)(2,1)S(1)}, u32[]{:S(2)}, u32[]{:S(2)}) %collective-permute-start.23) | collective-permute-done | bytes 196640 | tf_op jit(solution)/shard_map/ppermute | solution.py:85
  110.6 0.9 unpack_dkv.1
  (28 shorter events, 2.2 us)
Async XLA Ops:
  0.6 47.0 %copy-start = (s32[12,3]{0,1:T(4,128)S(1)}, s32[12,3]{0,1:T(4,128)}, u32[]{:S(2)}) copy-start(s32[12,3]{0,1:T(4,128)} %param.9) | copy-start | bytes 436
  2.0 20.5 %collective-permute-start = (bf16[2,2,4,16,384]{4,3,2,1,0:T(8,128)(2,1)S(1)}, bf16[2,2,4,16,384]{4,3,2,1,0:T(8,128)(2,1)S(1)}, u32[]{:S(2)}, u32[]{:S(2)}) collective-permute-start(bf16[2,2,4,16,384]{4,3,2,1,0:T(8,128)(2,1)S(1)} %get-tuple-element.45), channel_id=1, source_target_pairs={{0,128},{1,8},{8,16},{9,152},{16,129},{17,9},{24,17},{25,153},{128... | collective-permute-start | bytes 589832 | tf_op jit(solution)/shard_map/ppermute | solution.py:85
  7.7 16.6 %collective-permute-start.2 = (bf16[2,2,4,16,384]{4,3,2,1,0:T(8,128)(2,1)S(1)}, bf16[2,2,4,16,384]{4,3,2,1,0:T(8,128)(2,1)S(1)}, u32[]{:S(2)}, u32[]{:S(2)}) collective-permute-start(bf16[2,2,4,16,384]{4,3,2,1,0:T(8,128)(2,1)S(1)} %get-tuple-element.50), channel_id=1, source_target_pairs={{0,144},{1,24},{8,128},{9,8},{16,145},{17,153},{24,1},{25,137},{12... | collective-permute-start | bytes 589832 | tf_op jit(solution)/shard_map/ppermute | solution.py:85
  11.0 16.8 %collective-permute-start.1 = (bf16[2,2,4,16,384]{4,3,2,1,0:T(8,128)(2,1)S(1)}, bf16[2,2,4,16,384]{4,3,2,1,0:T(8,128)(2,1)S(1)}, u32[]{:S(2)}, u32[]{:S(2)}) collective-permute-start(bf16[2,2,4,16,384]{4,3,2,1,0:T(8,128)(2,1)S(1)} %get-tuple-element.48), channel_id=1, source_target_pairs={{0,128},{1,8},{8,16},{9,152},{16,129},{17,9},{24,17},{25,153},{128... | collective-permute-start | bytes 589832 | tf_op jit(solution)/shard_map/ppermute | solution.py:85
  13.7 20.0 %collective-permute-start.3 = (bf16[2,2,4,16,384]{4,3,2,1,0:T(8,128)(2,1)S(1)}, bf16[2,2,4,16,384]{4,3,2,1,0:T(8,128)(2,1)S(1)}, u32[]{:S(2)}, u32[]{:S(2)}) collective-permute-start(bf16[2,2,4,16,384]{4,3,2,1,0:T(8,128)(2,1)S(1)} %get-tuple-element.51), channel_id=1, source_target_pairs={{0,0},{1,136},{8,144},{9,24},{16,1},{17,137},{24,145},{25,25},{128... | collective-permute-start | bytes 589832 | tf_op jit(solution)/shard_map/ppermute | solution.py:85
  16.2 17.5 %collective-permute-start.4 = (bf16[2,2,4,16,384]{4,3,2,1,0:T(8,128)(2,1)S(1)}, bf16[2,2,4,16,384]{4,3,2,1,0:T(8,128)(2,1)S(1)}, u32[]{:S(2)}, u32[]{:S(2)}) collective-permute-start(bf16[2,2,4,16,384]{4,3,2,1,0:T(8,128)(2,1)S(1)} %get-tuple-element.52), channel_id=1, source_target_pairs={{0,16},{1,152},{8,0},{9,136},{16,17},{17,25},{24,129},{25,9},{128,... | collective-permute-start | bytes 589832 | tf_op jit(solution)/shard_map/ppermute | solution.py:85
  22.5 17.2 %collective-permute-start.6 = (bf16[2,2,4,16,384]{4,3,2,1,0:T(8,128)(2,1)S(1)}, bf16[2,2,4,16,384]{4,3,2,1,0:T(8,128)(2,1)S(1)}, u32[]{:S(2)}, u32[]{:S(2)}) collective-permute-start(bf16[2,2,4,16,384]{4,3,2,1,0:T(8,128)(2,1)S(1)} %get-tuple-element.55), channel_id=1, source_target_pairs={{0,144},{1,24},{8,128},{9,8},{16,145},{17,153},{24,1},{25,137},{12... | collective-permute-start | bytes 589832 | tf_op jit(solution)/shard_map/ppermute | solution.py:85
  24.4 15.3 %collective-permute-start.7 = (bf16[2,2,4,16,384]{4,3,2,1,0:T(8,128)(2,1)S(1)}, bf16[2,2,4,16,384]{4,3,2,1,0:T(8,128)(2,1)S(1)}, u32[]{:S(2)}, u32[]{:S(2)}) collective-permute-start(bf16[2,2,4,16,384]{4,3,2,1,0:T(8,128)(2,1)S(1)} %get-tuple-element.56), channel_id=1, source_target_pairs={{0,0},{1,136},{8,144},{9,24},{16,1},{17,137},{24,145},{25,25},{128... | collective-permute-start | bytes 589832 | tf_op jit(solution)/shard_map/ppermute | solution.py:85
  27.8 15.9 %collective-permute-start.8 = (bf16[2,2,4,16,384]{4,3,2,1,0:T(8,128)(2,1)S(1)}, bf16[2,2,4,16,384]{4,3,2,1,0:T(8,128)(2,1)S(1)}, u32[]{:S(2)}, u32[]{:S(2)}) collective-permute-start(bf16[2,2,4,16,384]{4,3,2,1,0:T(8,128)(2,1)S(1)} %get-tuple-element.57), channel_id=1, source_target_pairs={{0,16},{1,152},{8,0},{9,136},{16,17},{17,25},{24,129},{25,9},{128,... | collective-permute-start | bytes 589832 | tf_op jit(solution)/shard_map/ppermute | solution.py:85
  34.2 9.5 %collective-permute-start.5 = (bf16[2,64,384]{2,1,0:T(8,128)(2,1)S(1)}, bf16[2,64,384]{2,1,0:T(8,128)(2,1)S(1)}, u32[]{:S(2)}, u32[]{:S(2)}) collective-permute-start(bf16[2,64,384]{2,1,0:T(8,128)(2,1)S(1)} %get-tuple-element.54), channel_id=1, source_target_pairs={{0,8},{1,9},{8,0},{9,1},{16,24},{17,25},{24,16},{25,17},{128,136},... | collective-permute-start | bytes 294920 | tf_op jit(solution)/shard_map/ppermute | solution.py:94
  37.3 6.4 %collective-permute-start.9 = (bf16[2,64,384]{2,1,0:T(8,128)(2,1)S(1)}, bf16[2,64,384]{2,1,0:T(8,128)(2,1)S(1)}, u32[]{:S(2)}, u32[]{:S(2)}) collective-permute-start(bf16[2,64,384]{2,1,0:T(8,128)(2,1)S(1)} %get-tuple-element.59), channel_id=1, source_target_pairs={{8,10},{9,11},{24,26},{25,27},{136,138},{137,139},{152,154},{153,1... | collective-permute-start | bytes 294920 | tf_op jit(solution)/shard_map/ppermute | solution.py:94
  43.7 4.0 %collective-permute-start.10 = (bf16[2,160,384]{2,1,0:T(8,128)(2,1)S(1)}, bf16[2,160,384]{2,1,0:T(8,128)(2,1)S(1)}, u32[]{:S(2)}, u32[]{:S(2)}) collective-permute-start(bf16[2,160,384]{2,1,0:T(8,128)(2,1)S(1)} %get-tuple-element.60), channel_id=1, source_target_pairs={{0,1},{1,0},{8,9},{9,8},{16,17},{17,16},{24,25},{25,24},{128,129},... | collective-permute-start | bytes 737288 | tf_op jit(solution)/shard_map/ppermute | solution.py:94
  44.6 7.5 %collective-permute-start.11 = (bf16[2,160,384]{2,1,0:T(8,128)(2,1)S(1)}, bf16[2,160,384]{2,1,0:T(8,128)(2,1)S(1)}, u32[]{:S(2)}, u32[]{:S(2)}) collective-permute-start(bf16[2,160,384]{2,1,0:T(8,128)(2,1)S(1)} %get-tuple-element.61), channel_id=1, source_target_pairs={{1,32},{9,40},{17,48},{25,56},{129,160},{137,168},{145,176},{153,1... | collective-permute-start | bytes 737288 | tf_op jit(solution)/shard_map/ppermute | solution.py:94
  57.5 12.9 %collective-permute-start.16 = (bf16[2,160,384]{2,1,0:T(8,128)(2,1)S(1)}, bf16[2,160,384]{2,1,0:T(8,128)(2,1)S(1)}, u32[]{:S(2)}, u32[]{:S(2)}) collective-permute-start(bf16[2,160,384]{2,1,0:T(8,128)(2,1)S(1)} %get-tuple-element.73), channel_id=1, source_target_pairs={{0,1},{1,0},{8,9},{9,8},{16,17},{17,16},{24,25},{25,24},{128,129},... | collective-permute-start | bytes 737288 | tf_op jit(solution)/shard_map/ppermute | solution.py:94
  57.6 12.8 %collective-permute-start.17 = (bf16[2,160,384]{2,1,0:T(8,128)(2,1)S(1)}, bf16[2,160,384]{2,1,0:T(8,128)(2,1)S(1)}, u32[]{:S(2)}, u32[]{:S(2)}) collective-permute-start(bf16[2,160,384]{2,1,0:T(8,128)(2,1)S(1)} %get-tuple-element.74), channel_id=1, source_target_pairs={{1,32},{9,40},{17,48},{25,56},{129,160},{137,168},{145,176},{153,1... | collective-permute-start | bytes 737288 | tf_op jit(solution)/shard_map/ppermute | solution.py:94
  61.1 25.3 %collective-permute-start.12 = (bf16[2,2,4,16,384]{4,3,2,1,0:T(8,128)(2,1)S(1)}, bf16[2,2,4,16,384]{4,3,2,1,0:T(8,128)(2,1)S(1)}, u32[]{:S(2)}, u32[]{:S(2)}) collective-permute-start(bf16[2,2,4,16,384]{4,3,2,1,0:T(8,128)(2,1)S(1)} %get-tuple-element.66), channel_id=1, source_target_pairs={{128,0},{8,1},{16,8},{152,9},{129,16},{9,17},{17,24},{153,25},{0,1... | collective-permute-start | bytes 589832 | tf_op jit(solution)/shard_map/ppermute | solution.py:85
  62.1 28.3 %collective-permute-start.13 = (bf16[2,2,4,16,384]{4,3,2,1,0:T(8,128)(2,1)S(1)}, bf16[2,2,4,16,384]{4,3,2,1,0:T(8,128)(2,1)S(1)}, u32[]{:S(2)}, u32[]{:S(2)}) collective-permute-start(bf16[2,2,4,16,384]{4,3,2,1,0:T(8,128)(2,1)S(1)} %get-tuple-element.67), channel_id=1, source_target_pairs={{144,0},{24,1},{128,8},{8,9},{145,16},{153,17},{1,24},{137,25},{16... | collective-permute-start | bytes 589832 | tf_op jit(solution)/shard_map/ppermute | solution.py:85
  68.4 28.9 %collective-permute-start.14 = (bf16[2,2,4,16,384]{4,3,2,1,0:T(8,128)(2,1)S(1)}, bf16[2,2,4,16,384]{4,3,2,1,0:T(8,128)(2,1)S(1)}, u32[]{:S(2)}, u32[]{:S(2)}) collective-permute-start(bf16[2,2,4,16,384]{4,3,2,1,0:T(8,128)(2,1)S(1)} %get-tuple-element.68), channel_id=1, source_target_pairs={{0,0},{136,1},{144,8},{24,9},{1,16},{137,17},{145,24},{25,25},{128... | collective-permute-start | bytes 589832 | tf_op jit(solution)/shard_map/ppermute | solution.py:85
  70.4 12.7 %collective-permute-start.18 = (bf16[2,64,384]{2,1,0:T(8,128)(2,1)S(1)}, bf16[2,64,384]{2,1,0:T(8,128)(2,1)S(1)}, u32[]{:S(2)}, u32[]{:S(2)}) collective-permute-start(bf16[2,64,384]{2,1,0:T(8,128)(2,1)S(1)} %get-tuple-element.76), channel_id=1, source_target_pairs={{0,8},{1,9},{8,0},{9,1},{16,24},{17,25},{24,16},{25,17},{128,136},... | collective-permute-start | bytes 294920 | tf_op jit(solution)/shard_map/ppermute | solution.py:94
  72.5 12.5 %collective-permute-start.19 = (bf16[2,64,384]{2,1,0:T(8,128)(2,1)S(1)}, bf16[2,64,384]{2,1,0:T(8,128)(2,1)S(1)}, u32[]{:S(2)}, u32[]{:S(2)}) collective-permute-start(bf16[2,64,384]{2,1,0:T(8,128)(2,1)S(1)} %get-tuple-element.77), channel_id=1, source_target_pairs={{8,10},{9,11},{24,26},{25,27},{136,138},{137,139},{152,154},{153,1... | collective-permute-start | bytes 294920 | tf_op jit(solution)/shard_map/ppermute | solution.py:94
  83.1 16.1 %collective-permute-start.15 = (bf16[2,2,4,16,384]{4,3,2,1,0:T(8,128)(2,1)S(1)}, bf16[2,2,4,16,384]{4,3,2,1,0:T(8,128)(2,1)S(1)}, u32[]{:S(2)}, u32[]{:S(2)}) collective-permute-start(bf16[2,2,4,16,384]{4,3,2,1,0:T(8,128)(2,1)S(1)} %get-tuple-element.69), channel_id=1, source_target_pairs={{16,0},{152,1},{0,8},{136,9},{17,16},{25,17},{129,24},{9,25},{144,... | collective-permute-start | bytes 589832 | tf_op jit(solution)/shard_map/ppermute | solution.py:85
  85.8 14.5 %collective-permute-start.20 = (bf16[2,2,4,16,384]{4,3,2,1,0:T(8,128)(2,1)S(1)}, bf16[2,2,4,16,384]{4,3,2,1,0:T(8,128)(2,1)S(1)}, u32[]{:S(2)}, u32[]{:S(2)}) collective-permute-start(bf16[2,2,4,16,384]{4,3,2,1,0:T(8,128)(2,1)S(1)} %get-tuple-element.78), channel_id=1, source_target_pairs={{128,0},{8,1},{16,8},{152,9},{129,16},{9,17},{17,24},{153,25},{0,1... | collective-permute-start | bytes 589832 | tf_op jit(solution)/shard_map/ppermute | solution.py:85
  86.4 13.9 %collective-permute-start.21 = (bf16[2,2,4,16,384]{4,3,2,1,0:T(8,128)(2,1)S(1)}, bf16[2,2,4,16,384]{4,3,2,1,0:T(8,128)(2,1)S(1)}, u32[]{:S(2)}, u32[]{:S(2)}) collective-permute-start(bf16[2,2,4,16,384]{4,3,2,1,0:T(8,128)(2,1)S(1)} %get-tuple-element.79), channel_id=1, source_target_pairs={{144,0},{24,1},{128,8},{8,9},{145,16},{153,17},{1,24},{137,25},{16... | collective-permute-start | bytes 589832 | tf_op jit(solution)/shard_map/ppermute | solution.py:85
  90.4 10.7 %collective-permute-start.22 = (bf16[2,2,4,16,384]{4,3,2,1,0:T(8,128)(2,1)S(1)}, bf16[2,2,4,16,384]{4,3,2,1,0:T(8,128)(2,1)S(1)}, u32[]{:S(2)}, u32[]{:S(2)}) collective-permute-start(bf16[2,2,4,16,384]{4,3,2,1,0:T(8,128)(2,1)S(1)} %get-tuple-element.80), channel_id=1, source_target_pairs={{0,0},{136,1},{144,8},{24,9},{1,16},{137,17},{145,24},{25,25},{128... | collective-permute-start | bytes 589832 | tf_op jit(solution)/shard_map/ppermute | solution.py:85
  97.3 13.2 %collective-permute-start.23 = (bf16[2,2,4,16,384]{4,3,2,1,0:T(8,128)(2,1)S(1)}, bf16[2,2,4,16,384]{4,3,2,1,0:T(8,128)(2,1)S(1)}, u32[]{:S(2)}, u32[]{:S(2)}) collective-permute-start(bf16[2,2,4,16,384]{4,3,2,1,0:T(8,128)(2,1)S(1)} %get-tuple-element.81), channel_id=1, source_target_pairs={{16,0},{152,1},{0,8},{136,9},{17,16},{25,17},{129,24},{9,25},{144,... | collective-permute-start | bytes 589832 | tf_op jit(solution)/shard_map/ppermute | solution.py:85

commit v4 on v3

--- a/solution.py
+++ b/solution.py
@@ -205,11 +205,12 @@
             dest[i, spot(src, t, h), :] = buf[i, t, h]
 
 
-def edge_pick(transpose):
-    shape = (512, 128) if transpose else (128, 512)
+def edge_pick(transpose, rows=8):
+    few, many = 16 * rows, 64 * rows
+    shape = (many, few) if transpose else (few, many)
     e = lax.broadcasted_iota(jnp.int32, shape, 1 if transpose else 0)
     token = lax.broadcasted_iota(jnp.int32, shape, 0 if transpose else 1)
-    want = (e % 64) // 2 * 16 + e % 2 + 14 * (e // 64)
+    want = e % (8 * rows) // 2 * 16 + e % 2 + 14 * (e // (8 * rows))
     return jnp.where(token == want, 1.0, 0.0).astype(BF)
 
 
@@ -271,7 +272,7 @@
 def attend_body(window, own, col_in, col_out, row_in, row_out, *refs):
     qd = refs[:GROUPS]
     back = refs[GROUPS : 2 * GROUPS]
-    own_grad, side_grad, *rows_back = refs[2 * GROUPS : 2 * GROUPS + 4]
+    own_grad, rows_grad, *cols_back = refs[2 * GROUPS : 2 * GROUPS + 4]
     kv_mid, kv_side, g_mid, g_side, q_all, o_all = refs[2 * GROUPS + 4 :]
     group, half, block, x = place()
     w_at = lax.axis_index("wa") // 2 * 2 + block
@@ -372,20 +373,18 @@
                 out[i, t, h] = o_all[i, spot(src, t, h), :]
     for i in range(2):
         own_grad[i] = g_mid[i, 128:640]
-        for slot in range(2):
-            side_grad[slot, i] = g_side[slot, i, 16:80]
-        for out, (_, below) in zip(rows_back, rows):
-            out[i, 0:128] = g_mid[i, at_16(below * 640, 128)].astype(BF)
-            for slot in range(2):
-                out[i, 128 + 16 * slot : 144 + 16 * slot] = g_side[slot, i, at_16(below * 80)].astype(BF)
+        for n, (_, below) in enumerate(rows):
+            rows_grad[n, i] = g_mid[i, at_16(below * 640, 128)]
+        for out, slot in zip(cols_back, side_slots(block)):
+            out[i] = g_side[slot, i].astype(BF)
 
 
 def attend(window, own, cols, rows, qd):
     outs = [shaped(*DEALT)] * GROUPS + [
         shaped(2, 512, LANES, dtype=F32),
-        shaped(2, 2, 64, LANES, dtype=F32),
-        shaped(2, 160, LANES),
-        shaped(2, 160, LANES),
+        shaped(2, 2, 128, LANES, dtype=F32),
+        shaped(2, 96, LANES),
+        shaped(2, 96, LANES),
     ]
     ins = [own, *cols, *rows, *qd]
     scratch = [
@@ -408,32 +407,35 @@
     )(window, *ins)
 
 
-def side_body(side_grad, row_in, row_out, *outs):
+def rows_back_body(rows_grad, col_in, col_out, *refs):
+    outs, edges = refs[:2], refs[2]
     _, half, block, _ = place()
-    for out, slot in zip(outs, side_slots(block)):
+    spread = edge_pick(True, 2)
+    for side, slot in zip((col_in, col_out), side_slots(block)):
+        edges[slot] = side[...]
+    for n, (out, below) in enumerate(zip(outs, row_slots(half))):
         for i in range(2):
-            out[i] = side_grad[slot, i].astype(BF)
-            for buf, below in zip((row_in, row_out), row_slots(half)):
-                at = at_16(below * 48)
-                come = buf[i, at_16(128 + slot * 16)].astype(F32)
-                out[i, at] = (side_grad[slot, i, at] + come).astype(BF)
-
-
-def side_out(side_grad, rows):
-    return call(side_body, [shaped(2, 64, LANES)] * 2, name="side_out")(side_grad, *rows)
+            both = jnp.concatenate([edges[slot, i, at_16(below * 80)] for slot in range(2)], axis=0)
+            total = rows_grad[n, i] + jnp.dot(spread, both, preferred_element_type=F32)
+            out[i] = total.astype(BF)
+
+
+def rows_back(rows_grad, cols):
+    scratch = [pltpu.VMEM((2, 2, 96, LANES), BF)]
+    return call(rows_back_body, [shaped(2, 128, LANES)] * 2, scratch, name="rows_back")(rows_grad, *cols)
 
 
 def final_body(own_grad, row_in, row_out, col_in, col_out, *refs):
     outs, (total, edges) = refs[:GROUPS], refs[GROUPS:]
     _, half, block, _ = place()
     spread = edge_pick(True)
+    for side, slot in zip((col_in, col_out), side_slots(block)):
+        edges[slot] = side[:, 16:80]
     for i in range(2):
-        for side, slot in zip((col_in, col_out), side_slots(block)):
-            edges[slot, i] = side[i]
         both = jnp.concatenate([edges[0, i], edges[1, i]], axis=0)
         total[i] = own_grad[i] + jnp.dot(spread, both, preferred_element_type=F32)
         for buf, below in zip((row_in, row_out), row_slots(half)):
-            total[i, at_16(below * 384, 128), :] += buf[i, 0:128].astype(F32)
+            total[i, at_16(below * 384, 128), :] += buf[i].astype(F32)
         for src, out in zip(blocks_in(), outs):
             for t, h in BLOCK:
                 out[i, t, h] = total[i, spot(src, t, h), :].astype(BF)
@@ -460,9 +462,10 @@
     rows = rows_swap(*rows_out(own, *cols))
     results = attend(head_window, own, cols, rows, qd)
     oq = deal(results[:GROUPS], True)
-    own_grad, side_grad, *rows_back = results[GROUPS:]
-    rows = rows_swap(*rows_back)
-    cols = cols_swap(*side_out(side_grad, rows))
+    own_grad, rows_grad, *cols_back = results[GROUPS:]
+    cols = cols_swap(*cols_back)
+    rows = rows_swap(*rows_back(rows_grad, cols))
+    rows, oq[0:2] = ordered(rows, oq[0:2])
     dkv = deal(final(own_grad, rows, cols), True)
     attended, query_grad = unpack(oq, "unpack_oq")
     key_grad, value_grad = unpack(dkv, "unpack_dkv")

time: 113 us -> 109 us (0.965); the launches traced: 112 us -> 109 us
  waiting for transfers between devices: 26 us -> 20.3 us
  starting transfers between devices: 73.3 us -> 76.1 us
    ppermute x8, waiting for transfers between devices: 11.7 us -> 4.39 us  [swap(): return lax.ppermute(buf, ALL, pairs)]
    ppermute x16, starting transfers between devices: 55 us -> 57.9 us  [deal(): lax.ppermute(b, ALL, deal_pairs(r, back))]
    ppermute x16, waiting for transfers between devices: 14.3 us -> 15.9 us  [deal(): lax.ppermute(b, ALL, deal_pairs(r, back))]
  transfers between devices with their start and end apart: 24 -> 24, of which waited for: 5 -> 4; matrix products, arithmetic and copies ran while one was open for 0% -> 0% of each run, Pallas kernels for 3% -> 3%
where the time goes in v4:
time: 109 us
  starting transfers between devices  76.1 us (70%)
  waiting for transfers between devices  20.3 us (19%)
  Pallas kernels  11.4 us (10%)
    ppermute x16, starting transfers between devices, deal(): lax.ppermute(b, ALL, deal_pairs(r, back))  57.9 us
    ppermute x8, starting transfers between devices, swap(): return lax.ppermute(buf, ALL, pairs)  18.2 us
    ppermute x16, waiting for transfers between devices, deal(): lax.ppermute(b, ALL, deal_pairs(r, back))  15.9 us
    pallas_call x1, Pallas kernels, attend(): call(attend_body, outs, scratch, in_specs=[pl.BlockSpec(memory_space=pltp...  5.4 us
    ppermute x8, waiting for transfers between devices, swap(): return lax.ppermute(buf, ALL, pairs)  4.39 us
    pallas_call x2, Pallas kernels, pack(): call(pack_body, [shaped(*DEALT)] * GROUPS, [pltpu.SemaphoreType.DMA((2 *...  2.65 us
  transfers between devices with their start and end apart: 24, of which 4 were waited for; matrix products, arithmetic and copies ran while one was open for 0% of the time, Pallas kernels for 3%

profile of v4, /device:TPU:51, one launch (start us, length us, event | category | flops | bytes accessed | tf_op | source)
XLA Modules:
  0.0 108.9 jit_solution(15029587368188561347)
XLA Ops:
  0.6 1.3 %pack_kv.1 = (bf16[2,2,4,16,384]{4,3,2,1,0:T(8,128)(2,1)S(1)}, bf16[2,2,4,16,384]{4,3,2,1,0:T(8,128)(2,1)S(1)}, bf16[2,2,4,16,384]{4,3,2,1,0:T(8,128)(2,1)S(1)}, bf16[2,2,4,16,384]{4,3,2,1,0:T(8,128)(2,1)S(1)}) custom-call(bf16[2,4,16,1536]{3,2,1,0:T(8,128)(2,1)} %refs_0_.1, bf16[2,4,16,1536]{3,2,1,0:T(8,128)(2,1)} %refs_1_.1), custom_call_target="tpu_custom_call" | custom-call | bytes 3145728 | tf_op jit(solution)/shard_map/pack_kv/pallas_call | solution.py:162
  2.0 5.8 %collective-permute-start = (bf16[2,2,4,16,384]{4,3,2,1,0:T(8,128)(2,1)S(1)}, bf16[2,2,4,16,384]{4,3,2,1,0:T(8,128)(2,1)S(1)}, u32[]{:S(2)}, u32[]{:S(2)}) collective-permute-start(bf16[2,2,4,16,384]{4,3,2,1,0:T(8,128)(2,1)S(1)} %get-tuple-element.48), channel_id=1, source_target_pairs={{0,128},{1,8},{8,16},{9,152},{16,129},{17,9},{24,17},{25,153},{128... | collective-permute-start | bytes 589832 | tf_op jit(solution)/shard_map/ppermute | solution.py:85
  7.7 1.9 %collective-permute-start.2 = (bf16[2,2,4,16,384]{4,3,2,1,0:T(8,128)(2,1)S(1)}, bf16[2,2,4,16,384]{4,3,2,1,0:T(8,128)(2,1)S(1)}, u32[]{:S(2)}, u32[]{:S(2)}) collective-permute-start(bf16[2,2,4,16,384]{4,3,2,1,0:T(8,128)(2,1)S(1)} %get-tuple-element.53), channel_id=1, source_target_pairs={{0,144},{1,24},{8,128},{9,8},{16,145},{17,153},{24,1},{25,137},{12... | collective-permute-start | bytes 589832 | tf_op jit(solution)/shard_map/ppermute | solution.py:85
  9.7 1.3 %pack_qd.1 = (bf16[2,2,4,16,384]{4,3,2,1,0:T(8,128)(2,1)S(1)}, bf16[2,2,4,16,384]{4,3,2,1,0:T(8,128)(2,1)S(1)}, bf16[2,2,4,16,384]{4,3,2,1,0:T(8,128)(2,1)S(1)}, bf16[2,2,4,16,384]{4,3,2,1,0:T(8,128)(2,1)S(1)}) custom-call(bf16[2,4,16,1536]{3,2,1,0:T(8,128)(2,1)} %refs_0_.2, bf16[2,4,16,1536]{3,2,1,0:T(8,128)(2,1)} %refs_1_.2), custom_call_target="tpu_custom_call" | custom-call | bytes 3145728 | tf_op jit(solution)/shard_map/pack_qd/pallas_call | solution.py:162
  11.0 2.7 %collective-permute-start.1 = (bf16[2,2,4,16,384]{4,3,2,1,0:T(8,128)(2,1)S(1)}, bf16[2,2,4,16,384]{4,3,2,1,0:T(8,128)(2,1)S(1)}, u32[]{:S(2)}, u32[]{:S(2)}) collective-permute-start(bf16[2,2,4,16,384]{4,3,2,1,0:T(8,128)(2,1)S(1)} %get-tuple-element.51), channel_id=1, source_target_pairs={{0,128},{1,8},{8,16},{9,152},{16,129},{17,9},{24,17},{25,153},{128... | collective-permute-start | bytes 589832 | tf_op jit(solution)/shard_map/ppermute | solution.py:85
  13.7 2.5 %collective-permute-start.3 = (bf16[2,2,4,16,384]{4,3,2,1,0:T(8,128)(2,1)S(1)}, bf16[2,2,4,16,384]{4,3,2,1,0:T(8,128)(2,1)S(1)}, u32[]{:S(2)}, u32[]{:S(2)}) collective-permute-start(bf16[2,2,4,16,384]{4,3,2,1,0:T(8,128)(2,1)S(1)} %get-tuple-element.54), channel_id=1, source_target_pairs={{0,0},{1,136},{8,144},{9,24},{16,1},{17,137},{24,145},{25,25},{128... | collective-permute-start | bytes 589832 | tf_op jit(solution)/shard_map/ppermute | solution.py:85
  16.2 6.2 %collective-permute-start.4 = (bf16[2,2,4,16,384]{4,3,2,1,0:T(8,128)(2,1)S(1)}, bf16[2,2,4,16,384]{4,3,2,1,0:T(8,128)(2,1)S(1)}, u32[]{:S(2)}, u32[]{:S(2)}) collective-permute-start(bf16[2,2,4,16,384]{4,3,2,1,0:T(8,128)(2,1)S(1)} %get-tuple-element.55), channel_id=1, source_target_pairs={{0,16},{1,152},{8,0},{9,136},{16,17},{17,25},{24,129},{25,9},{128,... | collective-permute-start | bytes 589832 | tf_op jit(solution)/shard_map/ppermute | solution.py:85
  22.5 1.9 %collective-permute-start.6 = (bf16[2,2,4,16,384]{4,3,2,1,0:T(8,128)(2,1)S(1)}, bf16[2,2,4,16,384]{4,3,2,1,0:T(8,128)(2,1)S(1)}, u32[]{:S(2)}, u32[]{:S(2)}) collective-permute-start(bf16[2,2,4,16,384]{4,3,2,1,0:T(8,128)(2,1)S(1)} %get-tuple-element.58), channel_id=1, source_target_pairs={{0,144},{1,24},{8,128},{9,8},{16,145},{17,153},{24,1},{25,137},{12... | collective-permute-start | bytes 589832 | tf_op jit(solution)/shard_map/ppermute | solution.py:85
  24.4 3.4 %collective-permute-start.7 = (bf16[2,2,4,16,384]{4,3,2,1,0:T(8,128)(2,1)S(1)}, bf16[2,2,4,16,384]{4,3,2,1,0:T(8,128)(2,1)S(1)}, u32[]{:S(2)}, u32[]{:S(2)}) collective-permute-start(bf16[2,2,4,16,384]{4,3,2,1,0:T(8,128)(2,1)S(1)} %get-tuple-element.59), channel_id=1, source_target_pairs={{0,0},{1,136},{8,144},{9,24},{16,1},{17,137},{24,145},{25,25},{128... | collective-permute-start | bytes 589832 | tf_op jit(solution)/shard_map/ppermute | solution.py:85
  27.8 5.9 %collective-permute-start.8 = (bf16[2,2,4,16,384]{4,3,2,1,0:T(8,128)(2,1)S(1)}, bf16[2,2,4,16,384]{4,3,2,1,0:T(8,128)(2,1)S(1)}, u32[]{:S(2)}, u32[]{:S(2)}) collective-permute-start(bf16[2,2,4,16,384]{4,3,2,1,0:T(8,128)(2,1)S(1)} %get-tuple-element.60), channel_id=1, source_target_pairs={{0,16},{1,152},{8,0},{9,136},{16,17},{17,25},{24,129},{25,9},{128,... | collective-permute-start | bytes 589832 | tf_op jit(solution)/shard_map/ppermute | solution.py:85
  33.7 0.4 own_kv.1
  34.2 3.1 %collective-permute-start.5 = (bf16[2,64,384]{2,1,0:T(8,128)(2,1)S(1)}, bf16[2,64,384]{2,1,0:T(8,128)(2,1)S(1)}, u32[]{:S(2)}, u32[]{:S(2)}) collective-permute-start(bf16[2,64,384]{2,1,0:T(8,128)(2,1)S(1)} %get-tuple-element.57), channel_id=1, source_target_pairs={{0,8},{1,9},{8,0},{9,1},{16,24},{17,25},{24,16},{25,17},{128,136},... | collective-permute-start | bytes 294920 | tf_op jit(solution)/shard_map/ppermute | solution.py:94
  37.3 2.4 %collective-permute-start.9 = (bf16[2,64,384]{2,1,0:T(8,128)(2,1)S(1)}, bf16[2,64,384]{2,1,0:T(8,128)(2,1)S(1)}, u32[]{:S(2)}, u32[]{:S(2)}) collective-permute-start(bf16[2,64,384]{2,1,0:T(8,128)(2,1)S(1)} %get-tuple-element.62), channel_id=1, source_target_pairs={{8,10},{9,11},{24,26},{25,27},{136,138},{137,139},{152,154},{153,1... | collective-permute-start | bytes 294920 | tf_op jit(solution)/shard_map/ppermute | solution.py:94
  39.7 4.0 %collective-permute-done.8.refs_3_ = bf16[2,2,4,16,384]{4,3,2,1,0:T(8,128)(2,1)S(1)} collective-permute-done((bf16[2,2,4,16,384]{4,3,2,1,0:T(8,128)(2,1)S(1)}, bf16[2,2,4,16,384]{4,3,2,1,0:T(8,128)(2,1)S(1)}, u32[]{:S(2)}, u32[]{:S(2)}) %collective-permute-start.8) | collective-permute-done | bytes 196640 | tf_op jit(solution)/shard_map/ppermute | solution.py:85
  43.7 0.9 collective-permute-start.10
  44.6 3.0 %collective-permute-start.11 = (bf16[2,160,384]{2,1,0:T(8,128)(2,1)S(1)}, bf16[2,160,384]{2,1,0:T(8,128)(2,1)S(1)}, u32[]{:S(2)}, u32[]{:S(2)}) collective-permute-start(bf16[2,160,384]{2,1,0:T(8,128)(2,1)S(1)} %get-tuple-element.64), channel_id=1, source_target_pairs={{1,32},{9,40},{17,48},{25,56},{129,160},{137,168},{145,176},{153,1... | collective-permute-start | bytes 737288 | tf_op jit(solution)/shard_map/ppermute | solution.py:94
  47.7 4.4 %collective-permute-done.11.row_out = bf16[2,160,384]{2,1,0:T(8,128)(2,1)S(1)} collective-permute-done((bf16[2,160,384]{2,1,0:T(8,128)(2,1)S(1)}, bf16[2,160,384]{2,1,0:T(8,128)(2,1)S(1)}, u32[]{:S(2)}, u32[]{:S(2)}) %collective-permute-start.11) | collective-permute-done | bytes 245792 | tf_op jit(solution)/shard_map/ppermute | solution.py:94
  52.1 5.4 %attend.1 = (bf16[2,2,4,16,384]{4,3,2,1,0:T(8,128)(2,1)S(1)}, bf16[2,2,4,16,384]{4,3,2,1,0:T(8,128)(2,1)S(1)}, bf16[2,2,4,16,384]{4,3,2,1,0:T(8,128)(2,1)S(1)}, ...) custom-call(s32[12,3]{1,0:T(8,128)S(1)} %copy.9.window, ...), custom_call_target="tpu_custom_call" | custom-call | flops 1200000000 | bytes 8388608 | tf_op jit(solution)/shard_map/attend/pallas_call | solution.py:398
  57.5 2.3 %collective-permute-start.12 = (bf16[2,96,384]{2,1,0:T(8,128)(2,1)S(1)}, bf16[2,96,384]{2,1,0:T(8,128)(2,1)S(1)}, u32[]{:S(2)}, u32[]{:S(2)}) collective-permute-start(bf16[2,96,384]{2,1,0:T(8,128)(2,1)S(1)} %get-tuple-element.70), channel_id=1, source_target_pairs={{0,8},{1,9},{8,0},{9,1},{16,24},{17,25},{24,16},{25,17},{128,136},... | collective-permute-start | bytes 442376 | tf_op jit(solution)/shard_map/ppermute | solution.py:94
  59.8 2.9 %collective-permute-start.13 = (bf16[2,96,384]{2,1,0:T(8,128)(2,1)S(1)}, bf16[2,96,384]{2,1,0:T(8,128)(2,1)S(1)}, u32[]{:S(2)}, u32[]{:S(2)}) collective-permute-start(bf16[2,96,384]{2,1,0:T(8,128)(2,1)S(1)} %get-tuple-element.71), channel_id=1, source_target_pairs={{8,10},{9,11},{24,26},{25,27},{136,138},{137,139},{152,154},{153,1... | collective-permute-start | bytes 442376 | tf_op jit(solution)/shard_map/ppermute | solution.py:94
  62.9 5.8 %collective-permute-start.16 = (bf16[2,2,4,16,384]{4,3,2,1,0:T(8,128)(2,1)S(1)}, bf16[2,2,4,16,384]{4,3,2,1,0:T(8,128)(2,1)S(1)}, u32[]{:S(2)}, u32[]{:S(2)}) collective-permute-start(bf16[2,2,4,16,384]{4,3,2,1,0:T(8,128)(2,1)S(1)} %get-tuple-element.74), channel_id=1, source_target_pairs={{144,0},{24,1},{128,8},{8,9},{145,16},{153,17},{1,24},{137,25},{16... | collective-permute-start | bytes 589832 | tf_op jit(solution)/shard_map/ppermute | solution.py:85
  69.1 3.5 %collective-permute-start.19 = (bf16[2,128,384]{2,1,0:T(8,128)(2,1)S(1)}, bf16[2,128,384]{2,1,0:T(8,128)(2,1)S(1)}, u32[]{:S(2)}, u32[]{:S(2)}) collective-permute-start(bf16[2,128,384]{2,1,0:T(8,128)(2,1)S(1)} %get-tuple-element.83), channel_id=1, source_target_pairs={{1,32},{9,40},{17,48},{25,56},{129,160},{137,168},{145,176},{153,1... | collective-permute-start | bytes 589832 | tf_op jit(solution)/shard_map/ppermute | solution.py:94
  72.6 5.4 %collective-permute-start.17 = (bf16[2,2,4,16,384]{4,3,2,1,0:T(8,128)(2,1)S(1)}, bf16[2,2,4,16,384]{4,3,2,1,0:T(8,128)(2,1)S(1)}, u32[]{:S(2)}, u32[]{:S(2)}) collective-permute-start(bf16[2,2,4,16,384]{4,3,2,1,0:T(8,128)(2,1)S(1)} %get-tuple-element.77), channel_id=1, source_target_pairs={{0,0},{136,1},{144,8},{24,9},{1,16},{137,17},{145,24},{25,25},{128... | collective-permute-start | bytes 589832 | tf_op jit(solution)/shard_map/ppermute | solution.py:85
  78.1 1.9 %collective-permute-start.18 = (bf16[2,2,4,16,384]{4,3,2,1,0:T(8,128)(2,1)S(1)}, bf16[2,2,4,16,384]{4,3,2,1,0:T(8,128)(2,1)S(1)}, u32[]{:S(2)}, u32[]{:S(2)}) collective-permute-start(bf16[2,2,4,16,384]{4,3,2,1,0:T(8,128)(2,1)S(1)} %get-tuple-element.78), channel_id=1, source_target_pairs={{16,0},{152,1},{0,8},{136,9},{17,16},{25,17},{129,24},{9,25},{144,... | collective-permute-start | bytes 589832 | tf_op jit(solution)/shard_map/ppermute | solution.py:85
  80.0 0.7 final.1
  80.8 4.4 %collective-permute-start.21 = (bf16[2,2,4,16,384]{4,3,2,1,0:T(8,128)(2,1)S(1)}, bf16[2,2,4,16,384]{4,3,2,1,0:T(8,128)(2,1)S(1)}, u32[]{:S(2)}, u32[]{:S(2)}) collective-permute-start(bf16[2,2,4,16,384]{4,3,2,1,0:T(8,128)(2,1)S(1)} %get-tuple-element.85), channel_id=1, source_target_pairs={{144,0},{24,1},{128,8},{8,9},{145,16},{153,17},{1,24},{137,25},{16... | collective-permute-start | bytes 589832 | tf_op jit(solution)/shard_map/ppermute | solution.py:85
  85.2 7.8 %collective-permute-start.22 = (bf16[2,2,4,16,384]{4,3,2,1,0:T(8,128)(2,1)S(1)}, bf16[2,2,4,16,384]{4,3,2,1,0:T(8,128)(2,1)S(1)}, u32[]{:S(2)}, u32[]{:S(2)}) collective-permute-start(bf16[2,2,4,16,384]{4,3,2,1,0:T(8,128)(2,1)S(1)} %get-tuple-element.86), channel_id=1, source_target_pairs={{0,0},{136,1},{144,8},{24,9},{1,16},{137,17},{145,24},{25,25},{128... | collective-permute-start | bytes 589832 | tf_op jit(solution)/shard_map/ppermute | solution.py:85
  93.1 1.9 %collective-permute-start.23 = (bf16[2,2,4,16,384]{4,3,2,1,0:T(8,128)(2,1)S(1)}, bf16[2,2,4,16,384]{4,3,2,1,0:T(8,128)(2,1)S(1)}, u32[]{:S(2)}, u32[]{:S(2)}) collective-permute-start(bf16[2,2,4,16,384]{4,3,2,1,0:T(8,128)(2,1)S(1)} %get-tuple-element.87), channel_id=1, source_target_pairs={{16,0},{152,1},{0,8},{136,9},{17,16},{25,17},{129,24},{9,25},{144,... | collective-permute-start | bytes 589832 | tf_op jit(solution)/shard_map/ppermute | solution.py:85
  95.0 1.0 unpack_oq.1
  96.0 9.0 %collective-permute-done.22.refs_2_ = bf16[2,2,4,16,384]{4,3,2,1,0:T(8,128)(2,1)S(1)} collective-permute-done((bf16[2,2,4,16,384]{4,3,2,1,0:T(8,128)(2,1)S(1)}, bf16[2,2,4,16,384]{4,3,2,1,0:T(8,128)(2,1)S(1)}, u32[]{:S(2)}, u32[]{:S(2)}) %collective-permute-start.22) | collective-permute-done | bytes 196640 | tf_op jit(solution)/shard_map/ppermute | solution.py:85
  105.0 2.9 %collective-permute-done.23.refs_3_ = bf16[2,2,4,16,384]{4,3,2,1,0:T(8,128)(2,1)S(1)} collective-permute-done((bf16[2,2,4,16,384]{4,3,2,1,0:T(8,128)(2,1)S(1)}, bf16[2,2,4,16,384]{4,3,2,1,0:T(8,128)(2,1)S(1)}, u32[]{:S(2)}, u32[]{:S(2)}) %collective-permute-start.23) | collective-permute-done | bytes 196640 | tf_op jit(solution)/shard_map/ppermute | solution.py:85
  107.9 0.9 unpack_dkv.1
  (28 shorter events, 0.8 us)
Async XLA Ops:
  0.6 47.0 %copy-start = (s32[12,3]{0,1:T(4,128)S(1)}, s32[12,3]{0,1:T(4,128)}, u32[]{:S(2)}) copy-start(s32[12,3]{0,1:T(4,128)} %param.9) | copy-start | bytes 436
  2.0 20.5 %collective-permute-start = (bf16[2,2,4,16,384]{4,3,2,1,0:T(8,128)(2,1)S(1)}, bf16[2,2,4,16,384]{4,3,2,1,0:T(8,128)(2,1)S(1)}, u32[]{:S(2)}, u32[]{:S(2)}) collective-permute-start(bf16[2,2,4,16,384]{4,3,2,1,0:T(8,128)(2,1)S(1)} %get-tuple-element.48), channel_id=1, source_target_pairs={{0,128},{1,8},{8,16},{9,152},{16,129},{17,9},{24,17},{25,153},{128... | collective-permute-start | bytes 589832 | tf_op jit(solution)/shard_map/ppermute | solution.py:85
  7.7 16.6 %collective-permute-start.2 = (bf16[2,2,4,16,384]{4,3,2,1,0:T(8,128)(2,1)S(1)}, bf16[2,2,4,16,384]{4,3,2,1,0:T(8,128)(2,1)S(1)}, u32[]{:S(2)}, u32[]{:S(2)}) collective-permute-start(bf16[2,2,4,16,384]{4,3,2,1,0:T(8,128)(2,1)S(1)} %get-tuple-element.53), channel_id=1, source_target_pairs={{0,144},{1,24},{8,128},{9,8},{16,145},{17,153},{24,1},{25,137},{12... | collective-permute-start | bytes 589832 | tf_op jit(solution)/shard_map/ppermute | solution.py:85
  11.0 16.8 %collective-permute-start.1 = (bf16[2,2,4,16,384]{4,3,2,1,0:T(8,128)(2,1)S(1)}, bf16[2,2,4,16,384]{4,3,2,1,0:T(8,128)(2,1)S(1)}, u32[]{:S(2)}, u32[]{:S(2)}) collective-permute-start(bf16[2,2,4,16,384]{4,3,2,1,0:T(8,128)(2,1)S(1)} %get-tuple-element.51), channel_id=1, source_target_pairs={{0,128},{1,8},{8,16},{9,152},{16,129},{17,9},{24,17},{25,153},{128... | collective-permute-start | bytes 589832 | tf_op jit(solution)/shard_map/ppermute | solution.py:85
  13.7 20.0 %collective-permute-start.3 = (bf16[2,2,4,16,384]{4,3,2,1,0:T(8,128)(2,1)S(1)}, bf16[2,2,4,16,384]{4,3,2,1,0:T(8,128)(2,1)S(1)}, u32[]{:S(2)}, u32[]{:S(2)}) collective-permute-start(bf16[2,2,4,16,384]{4,3,2,1,0:T(8,128)(2,1)S(1)} %get-tuple-element.54), channel_id=1, source_target_pairs={{0,0},{1,136},{8,144},{9,24},{16,1},{17,137},{24,145},{25,25},{128... | collective-permute-start | bytes 589832 | tf_op jit(solution)/shard_map/ppermute | solution.py:85
  16.2 17.5 %collective-permute-start.4 = (bf16[2,2,4,16,384]{4,3,2,1,0:T(8,128)(2,1)S(1)}, bf16[2,2,4,16,384]{4,3,2,1,0:T(8,128)(2,1)S(1)}, u32[]{:S(2)}, u32[]{:S(2)}) collective-permute-start(bf16[2,2,4,16,384]{4,3,2,1,0:T(8,128)(2,1)S(1)} %get-tuple-element.55), channel_id=1, source_target_pairs={{0,16},{1,152},{8,0},{9,136},{16,17},{17,25},{24,129},{25,9},{128,... | collective-permute-start | bytes 589832 | tf_op jit(solution)/shard_map/ppermute | solution.py:85
  22.5 17.2 %collective-permute-start.6 = (bf16[2,2,4,16,384]{4,3,2,1,0:T(8,128)(2,1)S(1)}, bf16[2,2,4,16,384]{4,3,2,1,0:T(8,128)(2,1)S(1)}, u32[]{:S(2)}, u32[]{:S(2)}) collective-permute-start(bf16[2,2,4,16,384]{4,3,2,1,0:T(8,128)(2,1)S(1)} %get-tuple-element.58), channel_id=1, source_target_pairs={{0,144},{1,24},{8,128},{9,8},{16,145},{17,153},{24,1},{25,137},{12... | collective-permute-start | bytes 589832 | tf_op jit(solution)/shard_map/ppermute | solution.py:85
  24.4 15.3 %collective-permute-start.7 = (bf16[2,2,4,16,384]{4,3,2,1,0:T(8,128)(2,1)S(1)}, bf16[2,2,4,16,384]{4,3,2,1,0:T(8,128)(2,1)S(1)}, u32[]{:S(2)}, u32[]{:S(2)}) collective-permute-start(bf16[2,2,4,16,384]{4,3,2,1,0:T(8,128)(2,1)S(1)} %get-tuple-element.59), channel_id=1, source_target_pairs={{0,0},{1,136},{8,144},{9,24},{16,1},{17,137},{24,145},{25,25},{128... | collective-permute-start | bytes 589832 | tf_op jit(solution)/shard_map/ppermute | solution.py:85
  27.8 15.9 %collective-permute-start.8 = (bf16[2,2,4,16,384]{4,3,2,1,0:T(8,128)(2,1)S(1)}, bf16[2,2,4,16,384]{4,3,2,1,0:T(8,128)(2,1)S(1)}, u32[]{:S(2)}, u32[]{:S(2)}) collective-permute-start(bf16[2,2,4,16,384]{4,3,2,1,0:T(8,128)(2,1)S(1)} %get-tuple-element.60), channel_id=1, source_target_pairs={{0,16},{1,152},{8,0},{9,136},{16,17},{17,25},{24,129},{25,9},{128,... | collective-permute-start | bytes 589832 | tf_op jit(solution)/shard_map/ppermute | solution.py:85
  34.2 9.5 %collective-permute-start.5 = (bf16[2,64,384]{2,1,0:T(8,128)(2,1)S(1)}, bf16[2,64,384]{2,1,0:T(8,128)(2,1)S(1)}, u32[]{:S(2)}, u32[]{:S(2)}) collective-permute-start(bf16[2,64,384]{2,1,0:T(8,128)(2,1)S(1)} %get-tuple-element.57), channel_id=1, source_target_pairs={{0,8},{1,9},{8,0},{9,1},{16,24},{17,25},{24,16},{25,17},{128,136},... | collective-permute-start | bytes 294920 | tf_op jit(solution)/shard_map/ppermute | solution.py:94
  37.3 6.4 %collective-permute-start.9 = (bf16[2,64,384]{2,1,0:T(8,128)(2,1)S(1)}, bf16[2,64,384]{2,1,0:T(8,128)(2,1)S(1)}, u32[]{:S(2)}, u32[]{:S(2)}) collective-permute-start(bf16[2,64,384]{2,1,0:T(8,128)(2,1)S(1)} %get-tuple-element.62), channel_id=1, source_target_pairs={{8,10},{9,11},{24,26},{25,27},{136,138},{137,139},{152,154},{153,1... | collective-permute-start | bytes 294920 | tf_op jit(solution)/shard_map/ppermute | solution.py:94
  43.7 4.0 %collective-permute-start.10 = (bf16[2,160,384]{2,1,0:T(8,128)(2,1)S(1)}, bf16[2,160,384]{2,1,0:T(8,128)(2,1)S(1)}, u32[]{:S(2)}, u32[]{:S(2)}) collective-permute-start(bf16[2,160,384]{2,1,0:T(8,128)(2,1)S(1)} %get-tuple-element.63), channel_id=1, source_target_pairs={{0,1},{1,0},{8,9},{9,8},{16,17},{17,16},{24,25},{25,24},{128,129},... | collective-permute-start | bytes 737288 | tf_op jit(solution)/shard_map/ppermute | solution.py:94
  44.6 7.5 %collective-permute-start.11 = (bf16[2,160,384]{2,1,0:T(8,128)(2,1)S(1)}, bf16[2,160,384]{2,1,0:T(8,128)(2,1)S(1)}, u32[]{:S(2)}, u32[]{:S(2)}) collective-permute-start(bf16[2,160,384]{2,1,0:T(8,128)(2,1)S(1)} %get-tuple-element.64), channel_id=1, source_target_pairs={{1,32},{9,40},{17,48},{25,56},{129,160},{137,168},{145,176},{153,1... | collective-permute-start | bytes 737288 | tf_op jit(solution)/shard_map/ppermute | solution.py:94
  57.5 11.2 %collective-permute-start.12 = (bf16[2,96,384]{2,1,0:T(8,128)(2,1)S(1)}, bf16[2,96,384]{2,1,0:T(8,128)(2,1)S(1)}, u32[]{:S(2)}, u32[]{:S(2)}) collective-permute-start(bf16[2,96,384]{2,1,0:T(8,128)(2,1)S(1)} %get-tuple-element.70), channel_id=1, source_target_pairs={{0,8},{1,9},{8,0},{9,1},{16,24},{17,25},{24,16},{25,17},{128,136},... | collective-permute-start | bytes 442376 | tf_op jit(solution)/shard_map/ppermute | solution.py:94
  59.8 8.9 %collective-permute-start.13 = (bf16[2,96,384]{2,1,0:T(8,128)(2,1)S(1)}, bf16[2,96,384]{2,1,0:T(8,128)(2,1)S(1)}, u32[]{:S(2)}, u32[]{:S(2)}) collective-permute-start(bf16[2,96,384]{2,1,0:T(8,128)(2,1)S(1)} %get-tuple-element.71), channel_id=1, source_target_pairs={{8,10},{9,11},{24,26},{25,27},{136,138},{137,139},{152,154},{153,1... | collective-permute-start | bytes 442376 | tf_op jit(solution)/shard_map/ppermute | solution.py:94
  62.8 15.3 %collective-permute-start.15 = (bf16[2,2,4,16,384]{4,3,2,1,0:T(8,128)(2,1)S(1)}, bf16[2,2,4,16,384]{4,3,2,1,0:T(8,128)(2,1)S(1)}, u32[]{:S(2)}, u32[]{:S(2)}) collective-permute-start(bf16[2,2,4,16,384]{4,3,2,1,0:T(8,128)(2,1)S(1)} %get-tuple-element.73), channel_id=1, source_target_pairs={{128,0},{8,1},{16,8},{152,9},{129,16},{9,17},{17,24},{153,25},{0,1... | collective-permute-start | bytes 589832 | tf_op jit(solution)/shard_map/ppermute | solution.py:85
  62.9 17.1 %collective-permute-start.16 = (bf16[2,2,4,16,384]{4,3,2,1,0:T(8,128)(2,1)S(1)}, bf16[2,2,4,16,384]{4,3,2,1,0:T(8,128)(2,1)S(1)}, u32[]{:S(2)}, u32[]{:S(2)}) collective-permute-start(bf16[2,2,4,16,384]{4,3,2,1,0:T(8,128)(2,1)S(1)} %get-tuple-element.74), channel_id=1, source_target_pairs={{144,0},{24,1},{128,8},{8,9},{145,16},{153,17},{1,24},{137,25},{16... | collective-permute-start | bytes 589832 | tf_op jit(solution)/shard_map/ppermute | solution.py:85
  69.0 11.0 %collective-permute-start.14 = (bf16[2,128,384]{2,1,0:T(8,128)(2,1)S(1)}, bf16[2,128,384]{2,1,0:T(8,128)(2,1)S(1)}, u32[]{:S(2)}, u32[]{:S(2)}) collective-permute-start(bf16[2,128,384]{2,1,0:T(8,128)(2,1)S(1)} %get-tuple-element.72), channel_id=1, source_target_pairs={{0,1},{1,0},{8,9},{9,8},{16,17},{17,16},{24,25},{25,24},{128,129},... | collective-permute-start | bytes 589832 | tf_op jit(solution)/shard_map/ppermute | solution.py:94
  69.1 10.9 %collective-permute-start.19 = (bf16[2,128,384]{2,1,0:T(8,128)(2,1)S(1)}, bf16[2,128,384]{2,1,0:T(8,128)(2,1)S(1)}, u32[]{:S(2)}, u32[]{:S(2)}) collective-permute-start(bf16[2,128,384]{2,1,0:T(8,128)(2,1)S(1)} %get-tuple-element.83), channel_id=1, source_target_pairs={{1,32},{9,40},{17,48},{25,56},{129,160},{137,168},{145,176},{153,1... | collective-permute-start | bytes 589832 | tf_op jit(solution)/shard_map/ppermute | solution.py:94
  72.6 20.5 %collective-permute-start.17 = (bf16[2,2,4,16,384]{4,3,2,1,0:T(8,128)(2,1)S(1)}, bf16[2,2,4,16,384]{4,3,2,1,0:T(8,128)(2,1)S(1)}, u32[]{:S(2)}, u32[]{:S(2)}) collective-permute-start(bf16[2,2,4,16,384]{4,3,2,1,0:T(8,128)(2,1)S(1)} %get-tuple-element.77), channel_id=1, source_target_pairs={{0,0},{136,1},{144,8},{24,9},{1,16},{137,17},{145,24},{25,25},{128... | collective-permute-start | bytes 589832 | tf_op jit(solution)/shard_map/ppermute | solution.py:85
  78.1 16.9 %collective-permute-start.18 = (bf16[2,2,4,16,384]{4,3,2,1,0:T(8,128)(2,1)S(1)}, bf16[2,2,4,16,384]{4,3,2,1,0:T(8,128)(2,1)S(1)}, u32[]{:S(2)}, u32[]{:S(2)}) collective-permute-start(bf16[2,2,4,16,384]{4,3,2,1,0:T(8,128)(2,1)S(1)} %get-tuple-element.78), channel_id=1, source_target_pairs={{16,0},{152,1},{0,8},{136,9},{17,16},{25,17},{129,24},{9,25},{144,... | collective-permute-start | bytes 589832 | tf_op jit(solution)/shard_map/ppermute | solution.py:85
  80.7 15.3 %collective-permute-start.20 = (bf16[2,2,4,16,384]{4,3,2,1,0:T(8,128)(2,1)S(1)}, bf16[2,2,4,16,384]{4,3,2,1,0:T(8,128)(2,1)S(1)}, u32[]{:S(2)}, u32[]{:S(2)}) collective-permute-start(bf16[2,2,4,16,384]{4,3,2,1,0:T(8,128)(2,1)S(1)} %get-tuple-element.84), channel_id=1, source_target_pairs={{128,0},{8,1},{16,8},{152,9},{129,16},{9,17},{17,24},{153,25},{0,1... | collective-permute-start | bytes 589832 | tf_op jit(solution)/shard_map/ppermute | solution.py:85
  80.8 15.2 %collective-permute-start.21 = (bf16[2,2,4,16,384]{4,3,2,1,0:T(8,128)(2,1)S(1)}, bf16[2,2,4,16,384]{4,3,2,1,0:T(8,128)(2,1)S(1)}, u32[]{:S(2)}, u32[]{:S(2)}) collective-permute-start(bf16[2,2,4,16,384]{4,3,2,1,0:T(8,128)(2,1)S(1)} %get-tuple-element.85), channel_id=1, source_target_pairs={{144,0},{24,1},{128,8},{8,9},{145,16},{153,17},{1,24},{137,25},{16... | collective-permute-start | bytes 589832 | tf_op jit(solution)/shard_map/ppermute | solution.py:85
  85.2 19.8 %collective-permute-start.22 = (bf16[2,2,4,16,384]{4,3,2,1,0:T(8,128)(2,1)S(1)}, bf16[2,2,4,16,384]{4,3,2,1,0:T(8,128)(2,1)S(1)}, u32[]{:S(2)}, u32[]{:S(2)}) collective-permute-start(bf16[2,2,4,16,384]{4,3,2,1,0:T(8,128)(2,1)S(1)} %get-tuple-element.86), channel_id=1, source_target_pairs={{0,0},{136,1},{144,8},{24,9},{1,16},{137,17},{145,24},{25,25},{128... | collective-permute-start | bytes 589832 | tf_op jit(solution)/shard_map/ppermute | solution.py:85
  93.1 14.8 %collective-permute-start.23 = (bf16[2,2,4,16,384]{4,3,2,1,0:T(8,128)(2,1)S(1)}, bf16[2,2,4,16,384]{4,3,2,1,0:T(8,128)(2,1)S(1)}, u32[]{:S(2)}, u32[]{:S(2)}) collective-permute-start(bf16[2,2,4,16,384]{4,3,2,1,0:T(8,128)(2,1)S(1)} %get-tuple-element.87), channel_id=1, source_target_pairs={{16,0},{152,1},{0,8},{136,9},{17,16},{25,17},{129,24},{9,25},{144,... | collective-permute-start | bytes 589832 | tf_op jit(solution)/shard_map/ppermute | solution.py:85

commit v5 on v4

--- a/solution.py
+++ b/solution.py
@@ -169,27 +169,29 @@
     )(a, b)
 
 
-def unpack_body(*refs):
-    bufs, outs, sems = refs[:GROUPS], refs[GROUPS:-1], refs[-1]
+def unpack_body(*refs, turns, held):
+    bufs, outs, sems = refs[: len(turns)], refs[len(turns) + held : -1], refs[-1]
+    groups = groups_out()
     run_copies(
         [
-            (buf.at[i], ref.at[:, :, :, lanes_of(group)])
-            for group, buf in zip(groups_out(), bufs)
+            (buf.at[i], ref.at[:, :, :, lanes_of(groups[turn])])
+            for turn, buf in zip(turns, bufs)
             for i, ref in enumerate(outs)
         ],
         sems,
     )
 
 
-def unpack(bufs, name):
+def unpack(bufs, name, turns=tuple(range(GROUPS)), into=()):
     return call(
-        unpack_body,
+        partial(unpack_body, turns=turns, held=len(into)),
         [shaped(2, 4, 16, GROUPS * LANES)] * 2,
-        [pltpu.SemaphoreType.DMA((2 * GROUPS,))],
-        in_specs=[NEAR] * GROUPS,
+        [pltpu.SemaphoreType.DMA((2 * len(turns),))],
+        in_specs=[NEAR] * len(turns) + [FAR] * len(into),
         out_specs=[FAR] * 2,
+        input_output_aliases={len(turns) + i: i for i in range(len(into))},
         name=name,
-    )(*bufs)
+    )(*(bufs[t] for t in turns), *into)
 
 
 def spot(src, t, h):
@@ -468,7 +470,8 @@
     rows, oq[0:2] = ordered(rows, oq[0:2])
     dkv = deal(final(own_grad, rows, cols), True)
     attended, query_grad = unpack(oq, "unpack_oq")
-    key_grad, value_grad = unpack(dkv, "unpack_dkv")
+    early = unpack(dkv, "unpack_dkv_early", (0, 1, 2))
+    key_grad, value_grad = unpack(dkv, "unpack_dkv_last", (3,), early)
     return attended, query_grad, key_grad, value_grad
 
 

time: 109 us -> 110 us (level); the launches traced: 109 us -> 109 us
    pallas_call x2 -> x3, Pallas kernels: 1.91 us -> 2.51 us  [unpack(): call(partial(unpack_body, turns=turns, held=len(into)), [shaped(2, 4, 16,...]
  transfers between devices with their start and end apart: 24 -> 24, of which waited for: 4 -> 4; matrix products, arithmetic and copies ran while one was open for 0% -> 0% of each run, Pallas kernels for 3% -> 4%
where the time goes in v5:
time: 110 us; the launch traced here: 109 us
  starting transfers between devices  76.1 us (69%)
  waiting for transfers between devices  19.4 us (18%)
  Pallas kernels  12 us (11%)
    ppermute x16, starting transfers between devices, deal(): lax.ppermute(b, ALL, deal_pairs(r, back))  57.9 us
    ppermute x8, starting transfers between devices, swap(): return lax.ppermute(buf, ALL, pairs)  18.2 us
    ppermute x16, waiting for transfers between devices, deal(): lax.ppermute(b, ALL, deal_pairs(r, back))  15 us
    pallas_call x1, Pallas kernels, attend(): call(attend_body, outs, scratch, in_specs=[pl.BlockSpec(memory_space=pltp...  5.4 us
    ppermute x8, waiting for transfers between devices, swap(): return lax.ppermute(buf, ALL, pairs)  4.39 us
    pallas_call x2, Pallas kernels, pack(): call(pack_body, [shaped(*DEALT)] * GROUPS, [pltpu.SemaphoreType.DMA((2 *...  2.65 us
    pallas_call x3, Pallas kernels, unpack(): call(partial(unpack_body, turns=turns, held=len(into)), [shaped(2, 4, 16,...  2.51 us
  transfers between devices with their start and end apart: 24, of which 4 were waited for; matrix products, arithmetic and copies ran while one was open for 0% of the time, Pallas kernels for 4%

profile of v5, /device:TPU:51, one launch (start us, length us, event | category | flops | bytes accessed | tf_op | source)
XLA Modules:
  0.0 108.6 jit_solution(796312581944046350)
XLA Ops:
  0.6 1.3 %pack_kv.1 = (bf16[2,2,4,16,384]{4,3,2,1,0:T(8,128)(2,1)S(1)}, bf16[2,2,4,16,384]{4,3,2,1,0:T(8,128)(2,1)S(1)}, bf16[2,2,4,16,384]{4,3,2,1,0:T(8,128)(2,1)S(1)}, bf16[2,2,4,16,384]{4,3,2,1,0:T(8,128)(2,1)S(1)}) custom-call(bf16[2,4,16,1536]{3,2,1,0:T(8,128)(2,1)} %refs_0_.1, bf16[2,4,16,1536]{3,2,1,0:T(8,128)(2,1)} %refs_1_.1), custom_call_target="tpu_custom_call" | custom-call | bytes 3145728 | tf_op jit(solution)/shard_map/pack_kv/pallas_call | solution.py:162
  2.0 5.8 %collective-permute-start = (bf16[2,2,4,16,384]{4,3,2,1,0:T(8,128)(2,1)S(1)}, bf16[2,2,4,16,384]{4,3,2,1,0:T(8,128)(2,1)S(1)}, u32[]{:S(2)}, u32[]{:S(2)}) collective-permute-start(bf16[2,2,4,16,384]{4,3,2,1,0:T(8,128)(2,1)S(1)} %get-tuple-element.50), channel_id=1, source_target_pairs={{0,128},{1,8},{8,16},{9,152},{16,129},{17,9},{24,17},{25,153},{128... | collective-permute-start | bytes 589832 | tf_op jit(solution)/shard_map/ppermute | solution.py:85
  7.7 1.9 %collective-permute-start.2 = (bf16[2,2,4,16,384]{4,3,2,1,0:T(8,128)(2,1)S(1)}, bf16[2,2,4,16,384]{4,3,2,1,0:T(8,128)(2,1)S(1)}, u32[]{:S(2)}, u32[]{:S(2)}) collective-permute-start(bf16[2,2,4,16,384]{4,3,2,1,0:T(8,128)(2,1)S(1)} %get-tuple-element.55), channel_id=1, source_target_pairs={{0,144},{1,24},{8,128},{9,8},{16,145},{17,153},{24,1},{25,137},{12... | collective-permute-start | bytes 589832 | tf_op jit(solution)/shard_map/ppermute | solution.py:85
  9.7 1.3 %pack_qd.1 = (bf16[2,2,4,16,384]{4,3,2,1,0:T(8,128)(2,1)S(1)}, bf16[2,2,4,16,384]{4,3,2,1,0:T(8,128)(2,1)S(1)}, bf16[2,2,4,16,384]{4,3,2,1,0:T(8,128)(2,1)S(1)}, bf16[2,2,4,16,384]{4,3,2,1,0:T(8,128)(2,1)S(1)}) custom-call(bf16[2,4,16,1536]{3,2,1,0:T(8,128)(2,1)} %refs_0_.2, bf16[2,4,16,1536]{3,2,1,0:T(8,128)(2,1)} %refs_1_.2), custom_call_target="tpu_custom_call" | custom-call | bytes 3145728 | tf_op jit(solution)/shard_map/pack_qd/pallas_call | solution.py:162
  11.0 2.7 %collective-permute-start.1 = (bf16[2,2,4,16,384]{4,3,2,1,0:T(8,128)(2,1)S(1)}, bf16[2,2,4,16,384]{4,3,2,1,0:T(8,128)(2,1)S(1)}, u32[]{:S(2)}, u32[]{:S(2)}) collective-permute-start(bf16[2,2,4,16,384]{4,3,2,1,0:T(8,128)(2,1)S(1)} %get-tuple-element.53), channel_id=1, source_target_pairs={{0,128},{1,8},{8,16},{9,152},{16,129},{17,9},{24,17},{25,153},{128... | collective-permute-start | bytes 589832 | tf_op jit(solution)/shard_map/ppermute | solution.py:85
  13.7 2.5 %collective-permute-start.3 = (bf16[2,2,4,16,384]{4,3,2,1,0:T(8,128)(2,1)S(1)}, bf16[2,2,4,16,384]{4,3,2,1,0:T(8,128)(2,1)S(1)}, u32[]{:S(2)}, u32[]{:S(2)}) collective-permute-start(bf16[2,2,4,16,384]{4,3,2,1,0:T(8,128)(2,1)S(1)} %get-tuple-element.56), channel_id=1, source_target_pairs={{0,0},{1,136},{8,144},{9,24},{16,1},{17,137},{24,145},{25,25},{128... | collective-permute-start | bytes 589832 | tf_op jit(solution)/shard_map/ppermute | solution.py:85
  16.2 6.2 %collective-permute-start.4 = (bf16[2,2,4,16,384]{4,3,2,1,0:T(8,128)(2,1)S(1)}, bf16[2,2,4,16,384]{4,3,2,1,0:T(8,128)(2,1)S(1)}, u32[]{:S(2)}, u32[]{:S(2)}) collective-permute-start(bf16[2,2,4,16,384]{4,3,2,1,0:T(8,128)(2,1)S(1)} %get-tuple-element.57), channel_id=1, source_target_pairs={{0,16},{1,152},{8,0},{9,136},{16,17},{17,25},{24,129},{25,9},{128,... | collective-permute-start | bytes 589832 | tf_op jit(solution)/shard_map/ppermute | solution.py:85
  22.5 1.9 %collective-permute-start.6 = (bf16[2,2,4,16,384]{4,3,2,1,0:T(8,128)(2,1)S(1)}, bf16[2,2,4,16,384]{4,3,2,1,0:T(8,128)(2,1)S(1)}, u32[]{:S(2)}, u32[]{:S(2)}) collective-permute-start(bf16[2,2,4,16,384]{4,3,2,1,0:T(8,128)(2,1)S(1)} %get-tuple-element.60), channel_id=1, source_target_pairs={{0,144},{1,24},{8,128},{9,8},{16,145},{17,153},{24,1},{25,137},{12... | collective-permute-start | bytes 589832 | tf_op jit(solution)/shard_map/ppermute | solution.py:85
  24.4 3.4 %collective-permute-start.7 = (bf16[2,2,4,16,384]{4,3,2,1,0:T(8,128)(2,1)S(1)}, bf16[2,2,4,16,384]{4,3,2,1,0:T(8,128)(2,1)S(1)}, u32[]{:S(2)}, u32[]{:S(2)}) collective-permute-start(bf16[2,2,4,16,384]{4,3,2,1,0:T(8,128)(2,1)S(1)} %get-tuple-element.61), channel_id=1, source_target_pairs={{0,0},{1,136},{8,144},{9,24},{16,1},{17,137},{24,145},{25,25},{128... | collective-permute-start | bytes 589832 | tf_op jit(solution)/shard_map/ppermute | solution.py:85
  27.8 5.9 %collective-permute-start.8 = (bf16[2,2,4,16,384]{4,3,2,1,0:T(8,128)(2,1)S(1)}, bf16[2,2,4,16,384]{4,3,2,1,0:T(8,128)(2,1)S(1)}, u32[]{:S(2)}, u32[]{:S(2)}) collective-permute-start(bf16[2,2,4,16,384]{4,3,2,1,0:T(8,128)(2,1)S(1)} %get-tuple-element.62), channel_id=1, source_target_pairs={{0,16},{1,152},{8,0},{9,136},{16,17},{17,25},{24,129},{25,9},{128,... | collective-permute-start | bytes 589832 | tf_op jit(solution)/shard_map/ppermute | solution.py:85
  34.2 3.1 %collective-permute-start.5 = (bf16[2,64,384]{2,1,0:T(8,128)(2,1)S(1)}, bf16[2,64,384]{2,1,0:T(8,128)(2,1)S(1)}, u32[]{:S(2)}, u32[]{:S(2)}) collective-permute-start(bf16[2,64,384]{2,1,0:T(8,128)(2,1)S(1)} %get-tuple-element.59), channel_id=1, source_target_pairs={{0,8},{1,9},{8,0},{9,1},{16,24},{17,25},{24,16},{25,17},{128,136},... | collective-permute-start | bytes 294920 | tf_op jit(solution)/shard_map/ppermute | solution.py:94
  37.3 2.4 %collective-permute-start.9 = (bf16[2,64,384]{2,1,0:T(8,128)(2,1)S(1)}, bf16[2,64,384]{2,1,0:T(8,128)(2,1)S(1)}, u32[]{:S(2)}, u32[]{:S(2)}) collective-permute-start(bf16[2,64,384]{2,1,0:T(8,128)(2,1)S(1)} %get-tuple-element.64), channel_id=1, source_target_pairs={{8,10},{9,11},{24,26},{25,27},{136,138},{137,139},{152,154},{153,1... | collective-permute-start | bytes 294920 | tf_op jit(solution)/shard_map/ppermute | solution.py:94
  39.7 4.0 %collective-permute-done.8.refs_3_ = bf16[2,2,4,16,384]{4,3,2,1,0:T(8,128)(2,1)S(1)} collective-permute-done((bf16[2,2,4,16,384]{4,3,2,1,0:T(8,128)(2,1)S(1)}, bf16[2,2,4,16,384]{4,3,2,1,0:T(8,128)(2,1)S(1)}, u32[]{:S(2)}, u32[]{:S(2)}) %collective-permute-start.8) | collective-permute-done | bytes 196640 | tf_op jit(solution)/shard_map/ppermute | solution.py:85
  43.7 0.9 collective-permute-start.10
  44.6 3.0 %collective-permute-start.11 = (bf16[2,160,384]{2,1,0:T(8,128)(2,1)S(1)}, bf16[2,160,384]{2,1,0:T(8,128)(2,1)S(1)}, u32[]{:S(2)}, u32[]{:S(2)}) collective-permute-start(bf16[2,160,384]{2,1,0:T(8,128)(2,1)S(1)} %get-tuple-element.66), channel_id=1, source_target_pairs={{1,32},{9,40},{17,48},{25,56},{129,160},{137,168},{145,176},{153,1... | collective-permute-start | bytes 737288 | tf_op jit(solution)/shard_map/ppermute | solution.py:94
  47.7 4.4 %collective-permute-done.11.row_out = bf16[2,160,384]{2,1,0:T(8,128)(2,1)S(1)} collective-permute-done((bf16[2,160,384]{2,1,0:T(8,128)(2,1)S(1)}, bf16[2,160,384]{2,1,0:T(8,128)(2,1)S(1)}, u32[]{:S(2)}, u32[]{:S(2)}) %collective-permute-start.11) | collective-permute-done | bytes 245792 | tf_op jit(solution)/shard_map/ppermute | solution.py:94
  52.1 5.4 %attend.1 = (bf16[2,2,4,16,384]{4,3,2,1,0:T(8,128)(2,1)S(1)}, bf16[2,2,4,16,384]{4,3,2,1,0:T(8,128)(2,1)S(1)}, bf16[2,2,4,16,384]{4,3,2,1,0:T(8,128)(2,1)S(1)}, ...) custom-call(s32[12,3]{1,0:T(8,128)S(1)} %copy.11.window, ...), custom_call_target="tpu_custom_call" | custom-call | flops 1200000000 | bytes 8388608 | tf_op jit(solution)/shard_map/attend/pallas_call | solution.py:400
  57.5 2.3 %collective-permute-start.12 = (bf16[2,96,384]{2,1,0:T(8,128)(2,1)S(1)}, bf16[2,96,384]{2,1,0:T(8,128)(2,1)S(1)}, u32[]{:S(2)}, u32[]{:S(2)}) collective-permute-start(bf16[2,96,384]{2,1,0:T(8,128)(2,1)S(1)} %get-tuple-element.72), channel_id=1, source_target_pairs={{0,8},{1,9},{8,0},{9,1},{16,24},{17,25},{24,16},{25,17},{128,136},... | collective-permute-start | bytes 442376 | tf_op jit(solution)/shard_map/ppermute | solution.py:94
  59.8 2.9 %collective-permute-start.13 = (bf16[2,96,384]{2,1,0:T(8,128)(2,1)S(1)}, bf16[2,96,384]{2,1,0:T(8,128)(2,1)S(1)}, u32[]{:S(2)}, u32[]{:S(2)}) collective-permute-start(bf16[2,96,384]{2,1,0:T(8,128)(2,1)S(1)} %get-tuple-element.73), channel_id=1, source_target_pairs={{8,10},{9,11},{24,26},{25,27},{136,138},{137,139},{152,154},{153,1... | collective-permute-start | bytes 442376 | tf_op jit(solution)/shard_map/ppermute | solution.py:94
  62.9 5.8 %collective-permute-start.16 = (bf16[2,2,4,16,384]{4,3,2,1,0:T(8,128)(2,1)S(1)}, bf16[2,2,4,16,384]{4,3,2,1,0:T(8,128)(2,1)S(1)}, u32[]{:S(2)}, u32[]{:S(2)}) collective-permute-start(bf16[2,2,4,16,384]{4,3,2,1,0:T(8,128)(2,1)S(1)} %get-tuple-element.76), channel_id=1, source_target_pairs={{144,0},{24,1},{128,8},{8,9},{145,16},{153,17},{1,24},{137,25},{16... | collective-permute-start | bytes 589832 | tf_op jit(solution)/shard_map/ppermute | solution.py:85
  69.1 3.5 %collective-permute-start.19 = (bf16[2,128,384]{2,1,0:T(8,128)(2,1)S(1)}, bf16[2,128,384]{2,1,0:T(8,128)(2,1)S(1)}, u32[]{:S(2)}, u32[]{:S(2)}) collective-permute-start(bf16[2,128,384]{2,1,0:T(8,128)(2,1)S(1)} %get-tuple-element.85), channel_id=1, source_target_pairs={{1,32},{9,40},{17,48},{25,56},{129,160},{137,168},{145,176},{153,1... | collective-permute-start | bytes 589832 | tf_op jit(solution)/shard_map/ppermute | solution.py:94
  72.6 5.4 %collective-permute-start.17 = (bf16[2,2,4,16,384]{4,3,2,1,0:T(8,128)(2,1)S(1)}, bf16[2,2,4,16,384]{4,3,2,1,0:T(8,128)(2,1)S(1)}, u32[]{:S(2)}, u32[]{:S(2)}) collective-permute-start(bf16[2,2,4,16,384]{4,3,2,1,0:T(8,128)(2,1)S(1)} %get-tuple-element.79), channel_id=1, source_target_pairs={{0,0},{136,1},{144,8},{24,9},{1,16},{137,17},{145,24},{25,25},{128... | collective-permute-start | bytes 589832 | tf_op jit(solution)/shard_map/ppermute | solution.py:85
  78.1 1.9 %collective-permute-start.18 = (bf16[2,2,4,16,384]{4,3,2,1,0:T(8,128)(2,1)S(1)}, bf16[2,2,4,16,384]{4,3,2,1,0:T(8,128)(2,1)S(1)}, u32[]{:S(2)}, u32[]{:S(2)}) collective-permute-start(bf16[2,2,4,16,384]{4,3,2,1,0:T(8,128)(2,1)S(1)} %get-tuple-element.80), channel_id=1, source_target_pairs={{16,0},{152,1},{0,8},{136,9},{17,16},{25,17},{129,24},{9,25},{144,... | collective-permute-start | bytes 589832 | tf_op jit(solution)/shard_map/ppermute | solution.py:85
  80.0 0.7 final.1
  80.8 4.4 %collective-permute-start.22 = (bf16[2,2,4,16,384]{4,3,2,1,0:T(8,128)(2,1)S(1)}, bf16[2,2,4,16,384]{4,3,2,1,0:T(8,128)(2,1)S(1)}, u32[]{:S(2)}, u32[]{:S(2)}) collective-permute-start(bf16[2,2,4,16,384]{4,3,2,1,0:T(8,128)(2,1)S(1)} %get-tuple-element.88), channel_id=1, source_target_pairs={{144,0},{24,1},{128,8},{8,9},{145,16},{153,17},{1,24},{137,25},{16... | collective-permute-start | bytes 589832 | tf_op jit(solution)/shard_map/ppermute | solution.py:85
  85.2 7.8 %collective-permute-start.23 = (bf16[2,2,4,16,384]{4,3,2,1,0:T(8,128)(2,1)S(1)}, bf16[2,2,4,16,384]{4,3,2,1,0:T(8,128)(2,1)S(1)}, u32[]{:S(2)}, u32[]{:S(2)}) collective-permute-start(bf16[2,2,4,16,384]{4,3,2,1,0:T(8,128)(2,1)S(1)} %get-tuple-element.89), channel_id=1, source_target_pairs={{0,0},{136,1},{144,8},{24,9},{1,16},{137,17},{145,24},{25,25},{128... | collective-permute-start | bytes 589832 | tf_op jit(solution)/shard_map/ppermute | solution.py:85
  93.1 1.9 %collective-permute-start.20 = (bf16[2,2,4,16,384]{4,3,2,1,0:T(8,128)(2,1)S(1)}, bf16[2,2,4,16,384]{4,3,2,1,0:T(8,128)(2,1)S(1)}, u32[]{:S(2)}, u32[]{:S(2)}) collective-permute-start(bf16[2,2,4,16,384]{4,3,2,1,0:T(8,128)(2,1)S(1)} %get-tuple-element.86), channel_id=1, source_target_pairs={{16,0},{152,1},{0,8},{136,9},{17,16},{25,17},{129,24},{9,25},{144,... | collective-permute-start | bytes 589832 | tf_op jit(solution)/shard_map/ppermute | solution.py:85
  95.0 1.0 unpack_oq.1
  96.0 9.0 %collective-permute-done.23.refs_2_ = bf16[2,2,4,16,384]{4,3,2,1,0:T(8,128)(2,1)S(1)} collective-permute-done((bf16[2,2,4,16,384]{4,3,2,1,0:T(8,128)(2,1)S(1)}, bf16[2,2,4,16,384]{4,3,2,1,0:T(8,128)(2,1)S(1)}, u32[]{:S(2)}, u32[]{:S(2)}) %collective-permute-start.23) | collective-permute-done | bytes 196640 | tf_op jit(solution)/shard_map/ppermute | solution.py:85
  105.0 0.9 unpack_dkv_early.1
  105.9 2.0 %collective-permute-done.20.refs_0_ = bf16[2,2,4,16,384]{4,3,2,1,0:T(8,128)(2,1)S(1)} collective-permute-done((bf16[2,2,4,16,384]{4,3,2,1,0:T(8,128)(2,1)S(1)}, bf16[2,2,4,16,384]{4,3,2,1,0:T(8,128)(2,1)S(1)}, u32[]{:S(2)}, u32[]{:S(2)}) %collective-permute-start.20) | collective-permute-done | bytes 196640 | tf_op jit(solution)/shard_map/ppermute | solution.py:85
  107.9 0.7 unpack_dkv_last.1
  (29 shorter events, 1.2 us)
Async XLA Ops:
  0.6 47.0 %copy-start = (s32[12,3]{0,1:T(4,128)S(1)}, s32[12,3]{0,1:T(4,128)}, u32[]{:S(2)}) copy-start(s32[12,3]{0,1:T(4,128)} %param.9) | copy-start | bytes 436
  2.0 20.5 %collective-permute-start = (bf16[2,2,4,16,384]{4,3,2,1,0:T(8,128)(2,1)S(1)}, bf16[2,2,4,16,384]{4,3,2,1,0:T(8,128)(2,1)S(1)}, u32[]{:S(2)}, u32[]{:S(2)}) collective-permute-start(bf16[2,2,4,16,384]{4,3,2,1,0:T(8,128)(2,1)S(1)} %get-tuple-element.50), channel_id=1, source_target_pairs={{0,128},{1,8},{8,16},{9,152},{16,129},{17,9},{24,17},{25,153},{128... | collective-permute-start | bytes 589832 | tf_op jit(solution)/shard_map/ppermute | solution.py:85
  7.7 16.6 %collective-permute-start.2 = (bf16[2,2,4,16,384]{4,3,2,1,0:T(8,128)(2,1)S(1)}, bf16[2,2,4,16,384]{4,3,2,1,0:T(8,128)(2,1)S(1)}, u32[]{:S(2)}, u32[]{:S(2)}) collective-permute-start(bf16[2,2,4,16,384]{4,3,2,1,0:T(8,128)(2,1)S(1)} %get-tuple-element.55), channel_id=1, source_target_pairs={{0,144},{1,24},{8,128},{9,8},{16,145},{17,153},{24,1},{25,137},{12... | collective-permute-start | bytes 589832 | tf_op jit(solution)/shard_map/ppermute | solution.py:85
  11.0 16.8 %collective-permute-start.1 = (bf16[2,2,4,16,384]{4,3,2,1,0:T(8,128)(2,1)S(1)}, bf16[2,2,4,16,384]{4,3,2,1,0:T(8,128)(2,1)S(1)}, u32[]{:S(2)}, u32[]{:S(2)}) collective-permute-start(bf16[2,2,4,16,384]{4,3,2,1,0:T(8,128)(2,1)S(1)} %get-tuple-element.53), channel_id=1, source_target_pairs={{0,128},{1,8},{8,16},{9,152},{16,129},{17,9},{24,17},{25,153},{128... | collective-permute-start | bytes 589832 | tf_op jit(solution)/shard_map/ppermute | solution.py:85
  13.7 20.0 %collective-permute-start.3 = (bf16[2,2,4,16,384]{4,3,2,1,0:T(8,128)(2,1)S(1)}, bf16[2,2,4,16,384]{4,3,2,1,0:T(8,128)(2,1)S(1)}, u32[]{:S(2)}, u32[]{:S(2)}) collective-permute-start(bf16[2,2,4,16,384]{4,3,2,1,0:T(8,128)(2,1)S(1)} %get-tuple-element.56), channel_id=1, source_target_pairs={{0,0},{1,136},{8,144},{9,24},{16,1},{17,137},{24,145},{25,25},{128... | collective-permute-start | bytes 589832 | tf_op jit(solution)/shard_map/ppermute | solution.py:85
  16.2 17.5 %collective-permute-start.4 = (bf16[2,2,4,16,384]{4,3,2,1,0:T(8,128)(2,1)S(1)}, bf16[2,2,4,16,384]{4,3,2,1,0:T(8,128)(2,1)S(1)}, u32[]{:S(2)}, u32[]{:S(2)}) collective-permute-start(bf16[2,2,4,16,384]{4,3,2,1,0:T(8,128)(2,1)S(1)} %get-tuple-element.57), channel_id=1, source_target_pairs={{0,16},{1,152},{8,0},{9,136},{16,17},{17,25},{24,129},{25,9},{128,... | collective-permute-start | bytes 589832 | tf_op jit(solution)/shard_map/ppermute | solution.py:85
  22.5 17.2 %collective-permute-start.6 = (bf16[2,2,4,16,384]{4,3,2,1,0:T(8,128)(2,1)S(1)}, bf16[2,2,4,16,384]{4,3,2,1,0:T(8,128)(2,1)S(1)}, u32[]{:S(2)}, u32[]{:S(2)}) collective-permute-start(bf16[2,2,4,16,384]{4,3,2,1,0:T(8,128)(2,1)S(1)} %get-tuple-element.60), channel_id=1, source_target_pairs={{0,144},{1,24},{8,128},{9,8},{16,145},{17,153},{24,1},{25,137},{12... | collective-permute-start | bytes 589832 | tf_op jit(solution)/shard_map/ppermute | solution.py:85
  24.4 15.3 %collective-permute-start.7 = (bf16[2,2,4,16,384]{4,3,2,1,0:T(8,128)(2,1)S(1)}, bf16[2,2,4,16,384]{4,3,2,1,0:T(8,128)(2,1)S(1)}, u32[]{:S(2)}, u32[]{:S(2)}) collective-permute-start(bf16[2,2,4,16,384]{4,3,2,1,0:T(8,128)(2,1)S(1)} %get-tuple-element.61), channel_id=1, source_target_pairs={{0,0},{1,136},{8,144},{9,24},{16,1},{17,137},{24,145},{25,25},{128... | collective-permute-start | bytes 589832 | tf_op jit(solution)/shard_map/ppermute | solution.py:85
  27.8 15.9 %collective-permute-start.8 = (bf16[2,2,4,16,384]{4,3,2,1,0:T(8,128)(2,1)S(1)}, bf16[2,2,4,16,384]{4,3,2,1,0:T(8,128)(2,1)S(1)}, u32[]{:S(2)}, u32[]{:S(2)}) collective-permute-start(bf16[2,2,4,16,384]{4,3,2,1,0:T(8,128)(2,1)S(1)} %get-tuple-element.62), channel_id=1, source_target_pairs={{0,16},{1,152},{8,0},{9,136},{16,17},{17,25},{24,129},{25,9},{128,... | collective-permute-start | bytes 589832 | tf_op jit(solution)/shard_map/ppermute | solution.py:85
  34.2 9.5 %collective-permute-start.5 = (bf16[2,64,384]{2,1,0:T(8,128)(2,1)S(1)}, bf16[2,64,384]{2,1,0:T(8,128)(2,1)S(1)}, u32[]{:S(2)}, u32[]{:S(2)}) collective-permute-start(bf16[2,64,384]{2,1,0:T(8,128)(2,1)S(1)} %get-tuple-element.59), channel_id=1, source_target_pairs={{0,8},{1,9},{8,0},{9,1},{16,24},{17,25},{24,16},{25,17},{128,136},... | collective-permute-start | bytes 294920 | tf_op jit(solution)/shard_map/ppermute | solution.py:94
  37.3 6.4 %collective-permute-start.9 = (bf16[2,64,384]{2,1,0:T(8,128)(2,1)S(1)}, bf16[2,64,384]{2,1,0:T(8,128)(2,1)S(1)}, u32[]{:S(2)}, u32[]{:S(2)}) collective-permute-start(bf16[2,64,384]{2,1,0:T(8,128)(2,1)S(1)} %get-tuple-element.64), channel_id=1, source_target_pairs={{8,10},{9,11},{24,26},{25,27},{136,138},{137,139},{152,154},{153,1... | collective-permute-start | bytes 294920 | tf_op jit(solution)/shard_map/ppermute | solution.py:94
  43.7 4.0 %collective-permute-start.10 = (bf16[2,160,384]{2,1,0:T(8,128)(2,1)S(1)}, bf16[2,160,384]{2,1,0:T(8,128)(2,1)S(1)}, u32[]{:S(2)}, u32[]{:S(2)}) collective-permute-start(bf16[2,160,384]{2,1,0:T(8,128)(2,1)S(1)} %get-tuple-element.65), channel_id=1, source_target_pairs={{0,1},{1,0},{8,9},{9,8},{16,17},{17,16},{24,25},{25,24},{128,129},... | collective-permute-start | bytes 737288 | tf_op jit(solution)/shard_map/ppermute | solution.py:94
  44.6 7.5 %collective-permute-start.11 = (bf16[2,160,384]{2,1,0:T(8,128)(2,1)S(1)}, bf16[2,160,384]{2,1,0:T(8,128)(2,1)S(1)}, u32[]{:S(2)}, u32[]{:S(2)}) collective-permute-start(bf16[2,160,384]{2,1,0:T(8,128)(2,1)S(1)} %get-tuple-element.66), channel_id=1, source_target_pairs={{1,32},{9,40},{17,48},{25,56},{129,160},{137,168},{145,176},{153,1... | collective-permute-start | bytes 737288 | tf_op jit(solution)/shard_map/ppermute | solution.py:94
  57.5 11.2 %collective-permute-start.12 = (bf16[2,96,384]{2,1,0:T(8,128)(2,1)S(1)}, bf16[2,96,384]{2,1,0:T(8,128)(2,1)S(1)}, u32[]{:S(2)}, u32[]{:S(2)}) collective-permute-start(bf16[2,96,384]{2,1,0:T(8,128)(2,1)S(1)} %get-tuple-element.72), channel_id=1, source_target_pairs={{0,8},{1,9},{8,0},{9,1},{16,24},{17,25},{24,16},{25,17},{128,136},... | collective-permute-start | bytes 442376 | tf_op jit(solution)/shard_map/ppermute | solution.py:94
  59.8 8.9 %collective-permute-start.13 = (bf16[2,96,384]{2,1,0:T(8,128)(2,1)S(1)}, bf16[2,96,384]{2,1,0:T(8,128)(2,1)S(1)}, u32[]{:S(2)}, u32[]{:S(2)}) collective-permute-start(bf16[2,96,384]{2,1,0:T(8,128)(2,1)S(1)} %get-tuple-element.73), channel_id=1, source_target_pairs={{8,10},{9,11},{24,26},{25,27},{136,138},{137,139},{152,154},{153,1... | collective-permute-start | bytes 442376 | tf_op jit(solution)/shard_map/ppermute | solution.py:94
  62.8 15.3 %collective-permute-start.15 = (bf16[2,2,4,16,384]{4,3,2,1,0:T(8,128)(2,1)S(1)}, bf16[2,2,4,16,384]{4,3,2,1,0:T(8,128)(2,1)S(1)}, u32[]{:S(2)}, u32[]{:S(2)}) collective-permute-start(bf16[2,2,4,16,384]{4,3,2,1,0:T(8,128)(2,1)S(1)} %get-tuple-element.75), channel_id=1, source_target_pairs={{128,0},{8,1},{16,8},{152,9},{129,16},{9,17},{17,24},{153,25},{0,1... | collective-permute-start | bytes 589832 | tf_op jit(solution)/shard_map/ppermute | solution.py:85
  62.9 17.1 %collective-permute-start.16 = (bf16[2,2,4,16,384]{4,3,2,1,0:T(8,128)(2,1)S(1)}, bf16[2,2,4,16,384]{4,3,2,1,0:T(8,128)(2,1)S(1)}, u32[]{:S(2)}, u32[]{:S(2)}) collective-permute-start(bf16[2,2,4,16,384]{4,3,2,1,0:T(8,128)(2,1)S(1)} %get-tuple-element.76), channel_id=1, source_target_pairs={{144,0},{24,1},{128,8},{8,9},{145,16},{153,17},{1,24},{137,25},{16... | collective-permute-start | bytes 589832 | tf_op jit(solution)/shard_map/ppermute | solution.py:85
  69.0 11.0 %collective-permute-start.14 = (bf16[2,128,384]{2,1,0:T(8,128)(2,1)S(1)}, bf16[2,128,384]{2,1,0:T(8,128)(2,1)S(1)}, u32[]{:S(2)}, u32[]{:S(2)}) collective-permute-start(bf16[2,128,384]{2,1,0:T(8,128)(2,1)S(1)} %get-tuple-element.74), channel_id=1, source_target_pairs={{0,1},{1,0},{8,9},{9,8},{16,17},{17,16},{24,25},{25,24},{128,129},... | collective-permute-start | bytes 589832 | tf_op jit(solution)/shard_map/ppermute | solution.py:94
  69.1 10.9 %collective-permute-start.19 = (bf16[2,128,384]{2,1,0:T(8,128)(2,1)S(1)}, bf16[2,128,384]{2,1,0:T(8,128)(2,1)S(1)}, u32[]{:S(2)}, u32[]{:S(2)}) collective-permute-start(bf16[2,128,384]{2,1,0:T(8,128)(2,1)S(1)} %get-tuple-element.85), channel_id=1, source_target_pairs={{1,32},{9,40},{17,48},{25,56},{129,160},{137,168},{145,176},{153,1... | collective-permute-start | bytes 589832 | tf_op jit(solution)/shard_map/ppermute | solution.py:94
  72.6 20.5 %collective-permute-start.17 = (bf16[2,2,4,16,384]{4,3,2,1,0:T(8,128)(2,1)S(1)}, bf16[2,2,4,16,384]{4,3,2,1,0:T(8,128)(2,1)S(1)}, u32[]{:S(2)}, u32[]{:S(2)}) collective-permute-start(bf16[2,2,4,16,384]{4,3,2,1,0:T(8,128)(2,1)S(1)} %get-tuple-element.79), channel_id=1, source_target_pairs={{0,0},{136,1},{144,8},{24,9},{1,16},{137,17},{145,24},{25,25},{128... | collective-permute-start | bytes 589832 | tf_op jit(solution)/shard_map/ppermute | solution.py:85
  78.1 16.9 %collective-permute-start.18 = (bf16[2,2,4,16,384]{4,3,2,1,0:T(8,128)(2,1)S(1)}, bf16[2,2,4,16,384]{4,3,2,1,0:T(8,128)(2,1)S(1)}, u32[]{:S(2)}, u32[]{:S(2)}) collective-permute-start(bf16[2,2,4,16,384]{4,3,2,1,0:T(8,128)(2,1)S(1)} %get-tuple-element.80), channel_id=1, source_target_pairs={{16,0},{152,1},{0,8},{136,9},{17,16},{25,17},{129,24},{9,25},{144,... | collective-permute-start | bytes 589832 | tf_op jit(solution)/shard_map/ppermute | solution.py:85
  80.7 15.3 %collective-permute-start.21 = (bf16[2,2,4,16,384]{4,3,2,1,0:T(8,128)(2,1)S(1)}, bf16[2,2,4,16,384]{4,3,2,1,0:T(8,128)(2,1)S(1)}, u32[]{:S(2)}, u32[]{:S(2)}) collective-permute-start(bf16[2,2,4,16,384]{4,3,2,1,0:T(8,128)(2,1)S(1)} %get-tuple-element.87), channel_id=1, source_target_pairs={{128,0},{8,1},{16,8},{152,9},{129,16},{9,17},{17,24},{153,25},{0,1... | collective-permute-start | bytes 589832 | tf_op jit(solution)/shard_map/ppermute | solution.py:85
  80.8 15.2 %collective-permute-start.22 = (bf16[2,2,4,16,384]{4,3,2,1,0:T(8,128)(2,1)S(1)}, bf16[2,2,4,16,384]{4,3,2,1,0:T(8,128)(2,1)S(1)}, u32[]{:S(2)}, u32[]{:S(2)}) collective-permute-start(bf16[2,2,4,16,384]{4,3,2,1,0:T(8,128)(2,1)S(1)} %get-tuple-element.88), channel_id=1, source_target_pairs={{144,0},{24,1},{128,8},{8,9},{145,16},{153,17},{1,24},{137,25},{16... | collective-permute-start | bytes 589832 | tf_op jit(solution)/shard_map/ppermute | solution.py:85
  85.2 19.8 %collective-permute-start.23 = (bf16[2,2,4,16,384]{4,3,2,1,0:T(8,128)(2,1)S(1)}, bf16[2,2,4,16,384]{4,3,2,1,0:T(8,128)(2,1)S(1)}, u32[]{:S(2)}, u32[]{:S(2)}) collective-permute-start(bf16[2,2,4,16,384]{4,3,2,1,0:T(8,128)(2,1)S(1)} %get-tuple-element.89), channel_id=1, source_target_pairs={{0,0},{136,1},{144,8},{24,9},{1,16},{137,17},{145,24},{25,25},{128... | collective-permute-start | bytes 589832 | tf_op jit(solution)/shard_map/ppermute | solution.py:85
  93.1 14.8 %collective-permute-start.20 = (bf16[2,2,4,16,384]{4,3,2,1,0:T(8,128)(2,1)S(1)}, bf16[2,2,4,16,384]{4,3,2,1,0:T(8,128)(2,1)S(1)}, u32[]{:S(2)}, u32[]{:S(2)}) collective-permute-start(bf16[2,2,4,16,384]{4,3,2,1,0:T(8,128)(2,1)S(1)} %get-tuple-element.86), channel_id=1, source_target_pairs={{16,0},{152,1},{0,8},{136,9},{17,16},{25,17},{129,24},{9,25},{144,... | collective-permute-start | bytes 589832 | tf_op jit(solution)/shard_map/ppermute | solution.py:85
